TPU v7x, 32 devices: a whole 2x2x4 slice. The times are simulated.
32 devices in a mesh: groups: 2 (over x), gx: 16 (over z, y, core).
Axes of the slice: x: 2, y: 2, z: 4, core: 2. Of those that a mesh axis runs over, the one named last changes fastest.
Arguments:
- node_feat: bfloat16 [3200, 4096], P(None, ('groups', 'gx')), parts along dimension 1, may hold values from -6 to 6
- frames: bfloat16 [115, 16384], P(None, ('groups', 'gx')), parts along dimension 1, may hold values from -2.390625 to 2.390625
- neighbours: int32 [4, 4096], P(None, ('groups', 'gx')), parts along dimension 1, may hold values from 0 to 2047, as said below
- counts: int32 [4096], P(('groups', 'gx')), parts along dimension 0, may hold values from 2 to 4, as said below
- positions: float32 [3, 4096], P(None, ('groups', 'gx')), parts along dimension 1, may hold values from 0 to 331.776, as said below
- velocities: float32 [3, 4096], P(None, ('groups', 'gx')), parts along dimension 1
- masses: float32 [4096], P(('groups', 'gx')), parts along dimension 0, may hold values from 1 to 2
- thermal_noise: float32 [3, 4096], P(None, ('groups', 'gx')), parts along dimension 1, may hold values from -6 to 6
- box_lengths: float32 [6], P('groups'), parts along dimension 0, may hold values from 6.5 to 331.776
- control: float32 [6], P('groups'), parts along dimension 0, may hold values from 0.05 to 2
- conv_weight: bfloat16 [2, 5, 128, 128], replicated, may hold values from -0.5 to 0.5
- radial_weight: float32 [2, 16, 128], replicated, may hold values from -3 to 3
- readout: float32 [5, 128], replicated, may hold values from -0.5 to 0.5
Outputs:
- fractional: float32 [3, 4096], P(None, ('groups', 'gx')), parts along dimension 1
- new_velocities: float32 [3, 4096], P(None, ('groups', 'gx')), parts along dimension 1
- new_box: float32 [6], P('groups'), parts along dimension 0
There are 2 independent parts, one for each index of `groups`. A program takes and returns all parts, laid end to end along the dimension named above; an argument that names none is the same for every part. Nothing has to cross between parts.
Inputs may be any that keep to these rules, and one draw needn't show every extreme that they name: `neighbours`: the 4 slots of an atom name different atoms other than itself, each at most 32 places away from it in the cyclic order of atoms. `counts`: slots at or past an atom's count are padding. `positions`: every atom lies inside the box.
All inputs are finite; a program needn't handle non-finite values.
Results may differ from a plain program's by a relative error of at most 0.0055.
Values may be sent and summed in bfloat16 or wider, within the bound.
No kernel may reach another device: no remote copies, remote signals or barrier semaphores. Data moves between devices by JAX's collectives and lax.ppermute only.
A program may use at most 128 MiB of HBM per device.

v0:
```python
import jax
import jax.numpy as jnp
from jax import lax
from jax.sharding import PartitionSpec as P

LMAX = 4
MMAX = 2
NCOEF = 25
KNB = 4
GHOST = 32
NRBF = 16


EPSILON = 1e-06
SOFTENING = 0.25
STEP_TIME = 0.1
FRICTION = 0.9
RADIAL_SPREAD = 0.5


def extended(block, sides, width):
    for axis, dim in sides:
        count = lax.axis_size(axis)
        forward = [(i, i + 1) for i in range(count - 1)]
        forward.append((count - 1, 0))
        backward = [(target, source) for source, target in forward]
        low = lax.ppermute(
            lax.slice_in_dim(block, block.shape[dim] - width, None, axis=dim), axis, forward
        )
        high = lax.ppermute(lax.slice_in_dim(block, 0, width, axis=dim), axis, backward)
        block = jnp.concatenate([low, block, high], axis=dim)
    return block


def frame_layout():
    layout = []
    offset = 0
    for degree in range(LMAX + 1):
        row_count = min(2 * degree + 1, 2 * MMAX + 1)
        layout.append((degree, row_count, offset))
        offset = offset + row_count * (2 * degree + 1)
    return layout


def keep_round(values):
    rounded = lax.optimization_barrier(values.astype(jnp.bfloat16)).astype(jnp.float32)
    return values + lax.stop_gradient(rounded - values)


def contract(closed_expression, former, latter):
    return jnp.einsum(closed_expression, former, latter, preferred_element_type=jnp.float32)


def edge_messages(
    source, source_pos, target_pos, source_index, slot_mask, frames, conv_weights, radial_weights
):
    channels = source.shape[0] // NCOEF
    edge_total = source_index.shape[0]
    targets = target_pos.shape[1]
    squares = jnp.mean(source * source, axis=0, keepdims=True)
    normed = source * lax.rsqrt(squares + EPSILON)
    picked = (
        jnp.take(normed, source_index, axis=1)
        .astype(jnp.bfloat16)
        .reshape(NCOEF, channels, edge_total)
    )
    vectors = jnp.take(source_pos, source_index, axis=1) - jnp.repeat(target_pos, KNB, axis=1)
    distance = jnp.sqrt(jnp.sum(vectors * vectors, axis=0) + SOFTENING)
    centers = 0.5 + 5.5 * jnp.arange(NRBF, dtype=jnp.float32)[:, None] / (NRBF - 1)
    radial_basis = jnp.exp(-jnp.square((distance[None, :] - centers) / RADIAL_SPREAD))
    edge_gates = jnp.dot(radial_weights.T, radial_basis, precision=lax.Precision.HIGHEST)
    layout = frame_layout()
    in_frame = []
    frame_blocks = []
    for degree, row_count, offset in layout:
        degree_size = 2 * degree + 1
        frame_block = frames[offset : offset + row_count * degree_size].reshape(
            row_count, degree_size, edge_total
        )
        frame_blocks.append(frame_block)
        first_row = degree * degree
        rotated = contract("rke,kce->rce", frame_block, picked[first_row : first_row + degree_size])
        in_frame.append(rotated.astype(jnp.bfloat16))
    out_rows = [[None] * row_count for degree, row_count, offset in layout]
    zero_order = jnp.stack([rotated[0] for rotated in in_frame])
    zero_out = contract("rce,cd->rde", zero_order, conv_weights[0])
    for degree in range(LMAX + 1):
        out_rows[degree][0] = zero_out[degree]
    for azimuth in range(1, MMAX + 1):
        members = list(range(azimuth, LMAX + 1))
        plus_rows = jnp.stack([in_frame[degree][2 * azimuth - 1] for degree in members])
        minus_rows = jnp.stack([in_frame[degree][2 * azimuth] for degree in members])
        real_weight = conv_weights[2 * azimuth - 1]
        imag_weight = conv_weights[2 * azimuth]
        plus_out = contract("rce,cd->rde", plus_rows, real_weight) - contract(
            "rce,cd->rde", minus_rows, imag_weight
        )
        minus_out = contract("rce,cd->rde", minus_rows, real_weight) + contract(
            "rce,cd->rde", plus_rows, imag_weight
        )
        for member_index, degree in enumerate(members):
            out_rows[degree][2 * azimuth - 1] = plus_out[member_index]
            out_rows[degree][2 * azimuth] = minus_out[member_index]
    rotated_back = []
    for degree, row_count, offset in layout:
        gated_rows = (jnp.stack(out_rows[degree]) * edge_gates[None]).astype(jnp.bfloat16)
        rotated_back.append(contract("rke,rce->kce", frame_blocks[degree], gated_rows))
    message = jnp.concatenate(rotated_back, axis=0).reshape(NCOEF, channels, targets, KNB)
    return jnp.sum(message * slot_mask[None, None], axis=3).reshape(NCOEF * channels, targets)


def layer_block(
    window_feat, window_pos, source_index, slot_mask, frames, conv_weights, radial_weights
):
    message = edge_messages(
        window_feat,
        window_pos,
        window_pos[:, GHOST : 2 * GHOST],
        source_index,
        slot_mask,
        frames,
        conv_weights,
        radial_weights,
    )
    return window_feat[:, GHOST : 2 * GHOST] + message * KNB ** (-0.5)


def readout_energy(hidden, readout):
    channels = hidden.shape[0] // NCOEF
    shaped = hidden.reshape(NCOEF, channels, hidden.shape[1])
    energy = jnp.zeros((), jnp.float32)
    for degree in range(LMAX + 1):
        degree_rows = shaped[degree * degree : (degree + 1) * (degree + 1)]
        energy = energy + jnp.sum(
            readout[degree][:, None] * jnp.mean(degree_rows * degree_rows, axis=0)
        )
    return energy


def block_inputs(extended_index, live_slots, frames, block_index):
    start_col = block_index * GHOST
    local_index = lax.dynamic_slice_in_dim(extended_index, start_col, GHOST, 1) - start_col
    source_index = local_index.T.reshape(-1)
    slot_mask = lax.dynamic_slice_in_dim(live_slots, start_col, GHOST, 1).T
    frame_cols = lax.dynamic_slice_in_dim(frames, start_col * KNB, GHOST * KNB, 1)
    return (source_index, slot_mask, frame_cols)


def block_windows(feat_ext, pos_ext, block_index):
    start_col = block_index * GHOST
    window_feat = lax.dynamic_slice_in_dim(feat_ext, start_col, 3 * GHOST, 1)
    window_pos = lax.dynamic_slice_in_dim(pos_ext, start_col, 3 * GHOST, 1)
    return (window_feat, window_pos)


def first_pass(feat_ext, pos_ext, extended_index, live_slots, frames, conv_weights, radial_weights):
    block_total = extended_index.shape[1] // GHOST

    def first_one_block(block_index):
        source_index, slot_mask, frame_cols = block_inputs(
            extended_index, live_slots, frames, block_index
        )
        window_feat, window_pos = block_windows(feat_ext, pos_ext, block_index)
        return keep_round(
            layer_block(
                window_feat,
                window_pos,
                source_index,
                slot_mask,
                frame_cols,
                conv_weights,
                radial_weights,
            )
        )

    stacked = lax.map(first_one_block, jnp.arange(block_total, dtype=jnp.int32))
    return jnp.moveaxis(stacked, 0, 1).reshape(feat_ext.shape[0], block_total * GHOST)


def energy_pass(
    feat_ext, pos_ext, extended_index, live_slots, frames, conv_weights, radial_weights, readout
):
    block_total = extended_index.shape[1] // GHOST

    def energy_one_block(block_index):
        source_index, slot_mask, frame_cols = block_inputs(
            extended_index, live_slots, frames, block_index
        )
        window_feat, window_pos = block_windows(feat_ext, pos_ext, block_index)
        return readout_energy(
            layer_block(
                window_feat,
                window_pos,
                source_index,
                slot_mask,
                frame_cols,
                conv_weights,
                radial_weights,
            ),
            readout,
        )

    return jnp.sum(lax.map(energy_one_block, jnp.arange(block_total, dtype=jnp.int32)))


def unwrap_rims(extended_atoms, rim_width, length, place_index, devices):
    column = jnp.arange(extended_atoms.shape[1])
    left_fix = jnp.where((column < rim_width) & (place_index == 0), -length, 0.0)
    right_fix = jnp.where(
        (column >= extended_atoms.shape[1] - rim_width) & (place_index == devices - 1), length, 0.0
    )
    return extended_atoms + jnp.zeros_like(extended_atoms).at[0].set(left_fix + right_fix)


def ghost_rims(values, rim_width, own_atoms):
    return jnp.concatenate([values[:, :rim_width], values[:, rim_width + own_atoms :]], axis=1)


def settle_rims(values, returned, rim_width, own_atoms):
    central_slab_portion = values[:, rim_width : rim_width + own_atoms]
    central_slab_portion = central_slab_portion.at[:, :rim_width].add(returned[:, :rim_width])
    return central_slab_portion.at[:, own_atoms - rim_width :].add(returned[:, 3 * rim_width :])


def shards(
    node_feat,
    frames,
    neighbours,
    counts,
    positions,
    velocities,
    masses,
    thermal_noise,
    box_lengths,
    control,
    conv_weight,
    radial_weight,
    readout,
):
    own_atoms = positions.shape[1]
    devices = lax.axis_size("gx")
    place_index = lax.axis_index("gx")
    total_atoms = own_atoms * devices
    live_slots = (jnp.arange(KNB, dtype=jnp.int32)[:, None] < counts[None, :]).astype(jnp.float32)
    extended_index = jnp.mod(neighbours - place_index * own_atoms + GHOST, total_atoms)
    rim_width = GHOST
    ext_pos = unwrap_rims(
        extended(positions, (("gx", 1),), GHOST), GHOST, box_lengths[0], place_index, devices
    )

    def near_features(values):
        return extended(values, (("gx", 1),), GHOST)

    feat_ext = near_features(node_feat).astype(jnp.float32)

    def first_layer(pos_in):
        return first_pass(
            feat_ext, pos_in, extended_index, live_slots, frames, conv_weight[0], radial_weight[0]
        )

    hidden, pull_first = jax.vjp(first_layer, ext_pos)
    hidden_ext = near_features(hidden.astype(jnp.bfloat16)).astype(jnp.float32)

    def second_layer(feat_in, pos_in):
        return energy_pass(
            feat_in,
            pos_in,
            extended_index,
            live_slots,
            frames,
            conv_weight[1],
            radial_weight[1],
            readout,
        )

    energy, backward_latter_layer = jax.vjp(second_layer, hidden_ext, ext_pos)
    feat_grad, pos_grad_two = backward_latter_layer(jnp.ones((), jnp.float32))
    returned = extended(
        ghost_rims(feat_grad, GHOST, own_atoms).astype(jnp.bfloat16), (("gx", 1),), GHOST
    ).astype(jnp.float32)
    hidden_grad = settle_rims(feat_grad, returned, GHOST, own_atoms)
    (pos_grad_one,) = pull_first(hidden_grad)
    ext_grad = pos_grad_one + pos_grad_two
    returned_grad = extended(ghost_rims(ext_grad, GHOST, own_atoms), (("gx", 1),), GHOST)
    forces = -settle_rims(ext_grad, returned_grad, rim_width, own_atoms)
    virial_local = -jnp.sum((ext_pos - positions[:, :1]) * ext_grad)
    kicked = velocities + STEP_TIME * forces / masses[None, :]
    virial = lax.psum(virial_local, "gx")
    kinetic = lax.psum(0.5 * jnp.sum(masses * jnp.sum(kicked * kicked, axis=0)), "gx")
    volume = box_lengths[0] * box_lengths[1] * box_lengths[2]
    pressure = (2.0 * kinetic + virial) / (3.0 * volume)
    thermal = (
        FRICTION * kicked
        + jnp.sqrt((1.0 - FRICTION * FRICTION) * control[0] / masses)[None, :] * thermal_noise
    )
    rescale = jnp.exp(control[1] * (pressure - control[2]) / 3.0)
    fractional = (positions + STEP_TIME * thermal) / box_lengths[:, None]
    return (fractional, thermal / rescale, box_lengths * rescale)


def solution(mesh):
    return jax.shard_map(
        shards,
        mesh=mesh,
        in_specs=(
            P(None, ("groups", "gx")),
            P(None, ("groups", "gx")),
            P(None, ("groups", "gx")),
            P(("groups", "gx")),
            P(None, ("groups", "gx")),
            P(None, ("groups", "gx")),
            P(("groups", "gx")),
            P(None, ("groups", "gx")),
            P("groups"),
            P("groups"),
            P(),
            P(),
            P(),
        ),
        out_specs=(P(None, ("groups", "gx")), P(None, ("groups", "gx")), P("groups")),
        check_vma=False,
    )
```

profile of v0, /device:TPU:0, one launch (start us, length us, event | category | flops | bytes accessed | tf_op | source)
XLA Modules:
  0.0 1026.4 jit_solution(5047802753716088545)
XLA Ops:
  1.9 5.1 collective-permute-start.3
  8.7 4.4 collective-permute-start.1
  34.9 214.8 %while.158 = (s32[]{:T(128)}, bf16[4,3200,32]{1,2,0:T(8,128)(2,1)}, s32[4]{0:T(128)}, s32[4,128,1]{1,2,0:T(1,128)}, f32[4,3,128]{1,2,0:T(8,128)}, /*index=5*/f32...) while((s32[]{:T(128)}, bf16[4,3200,32]{1,2,0:T(8,128)(2,1)}, ...), condition=%wide.region_4.6_spmd.clone.clone, body=%wide.region_0.5_spmd.clone.clone.sunk | while | flops 155189904 | bytes 66846624 | solution.py:176
  68.8 6.6 concatenate.53
  122.5 6.6 concatenate.53
  176.2 6.6 concatenate.53
  229.9 6.6 concatenate.53
  250.9 4.7 collective-permute-start.5
  273.6 357.8 %while.159 = (s32[]{:T(128)}, s32[4]{0:T(128)}, f32[4,3200,96]{1,2,0:T(8,128)}, f32[4,1,96]{2,1,0:T(1,128)}, f32[4,1,96]{2,1,0:T(1,128)}, /*index=5*/s32[4,128,1...) while((s32[]{:T(128)}, s32[4]{0:T(128)}, ...), condition=%wide.region_9.11_spmd.clone.clone, body=%wide.region_5.10_spmd.clone.clone.sunk | while | flops 153925008 | bytes 54779616 | solution.py:203
  322.5 11.1 %concatenate.54 = f32[25,128,128]{1,0,2:T(8,128)} concatenate(f32[1,128,128]{1,0,2:T(1,128)} %bitcast.1359, f32[3,128,128]{1,0,2:T(4,128)} %convolution_bitcast_fusion.28, f32[5,128,128]{1,0,2:T(8,128)} %convolution_bitcast_fusion.29, f32[7,128,128]{1,0,2:T(8,128)} %convolution_bitcast_fusion.30, f32[9,128,128]{1,0,2:T(8,128)S(1)} %convolution_bitcast_fusion.31), dimensions={0} | concatenate | bytes 3276800 | tf_op jit(solution)/shard_map/jvp()/while/body/eval_jaxpr/concatenate | solution.py:108
  412.0 11.1 %concatenate.54 = f32[25,128,128]{1,0,2:T(8,128)} concatenate(f32[1,128,128]{1,0,2:T(1,128)} %bitcast.1359, f32[3,128,128]{1,0,2:T(4,128)} %convolution_bitcast_fusion.28, f32[5,128,128]{1,0,2:T(8,128)} %convolution_bitcast_fusion.29, f32[7,128,128]{1,0,2:T(8,128)} %convolution_bitcast_fusion.30, f32[9,128,128]{1,0,2:T(8,128)S(1)} %convolution_bitcast_fusion.31), dimensions={0} | concatenate | bytes 3276800 | tf_op jit(solution)/shard_map/jvp()/while/body/eval_jaxpr/concatenate | solution.py:108
  501.5 11.1 %concatenate.54 = f32[25,128,128]{1,0,2:T(8,128)} concatenate(f32[1,128,128]{1,0,2:T(1,128)} %bitcast.1359, f32[3,128,128]{1,0,2:T(4,128)} %convolution_bitcast_fusion.28, f32[5,128,128]{1,0,2:T(8,128)} %convolution_bitcast_fusion.29, f32[7,128,128]{1,0,2:T(8,128)} %convolution_bitcast_fusion.30, f32[9,128,128]{1,0,2:T(8,128)S(1)} %convolution_bitcast_fusion.31), dimensions={0} | concatenate | bytes 3276800 | tf_op jit(solution)/shard_map/jvp()/while/body/eval_jaxpr/concatenate | solution.py:108
  590.9 11.1 %concatenate.54 = f32[25,128,128]{1,0,2:T(8,128)} concatenate(f32[1,128,128]{1,0,2:T(1,128)} %bitcast.1359, f32[3,128,128]{1,0,2:T(4,128)} %convolution_bitcast_fusion.28, f32[5,128,128]{1,0,2:T(8,128)} %convolution_bitcast_fusion.29, f32[7,128,128]{1,0,2:T(8,128)} %convolution_bitcast_fusion.30, f32[9,128,128]{1,0,2:T(8,128)S(1)} %convolution_bitcast_fusion.31), dimensions={0} | concatenate | bytes 3276800 | tf_op jit(solution)/shard_map/jvp()/while/body/eval_jaxpr/concatenate | solution.py:108
  633.2 248.0 %while.156 = (s32[]{:T(128)}, f32[3200,192]{0,1:T(8,128)}, f32[3,192]{1,0:T(4,128)S(1)}, s32[4]{0:T(128)}, f32[4,9,128,32]{2,1,3,0:T(8,128)S(1)}, /*index=5*/f32...) while((s32[]{:T(128)}, f32[3200,192]{0,1:T(8,128)}, ...), condition=%wide.region_20.22_spmd, body=%wide.region_10.21_spmd.sunk | while | flops 159278464 | bytes 69106816 | solution.py:203
  678.6 2.5 fusion.575
  689.2 3.2 scatter_custom_fusion.14
  697.8 4.4 add_any.853
  737.5 2.5 fusion.575
  748.1 3.2 scatter_custom_fusion.14
  754.4 2.4 fusion.596
  756.8 5.0 add_any.853
  797.2 2.5 fusion.575
  807.8 3.2 scatter_custom_fusion.14
  814.0 2.4 fusion.596
  816.5 5.0 add_any.853
  856.7 2.5 fusion.575
  867.3 3.2 scatter_custom_fusion.14
  875.9 5.0 add_any.853
  883.3 4.7 collective-permute-start.7
  895.2 80.5 %while.157 = (s32[]{:T(128)}, f32[3,192]{1,0:T(4,128)S(1)}, s32[4]{0:T(128)}, f32[4,3,128]{1,2,0:T(8,128)S(1)}, f32[4,5,128,128]{2,3,1,0:T(8,128)}, /*index=5*/f...) while((s32[]{:T(128)}, f32[3,192]{1,0:T(4,128)S(1)}, ...), condition=%wide.region_30.32_spmd, body=%wide.region_22.31_spmd.sunk | while | flops 8356643 | bytes 13202993 | solution.py:176
  977.9 4.4 collective-permute-start.9
  986.7 34.2 %all-reduce.50 = (f32[]{:T(128)}, f32[]{:T(128)}) all-reduce(f32[]{:T(128)S(6)} %mul.959, f32[]{:T(128)S(6)} %neg.97), channel_id=1, replica_groups=mesh['groups'=2,'gx'=16] {'gx'}, use_global_device_ids=true, to_apply=%region_33.35 | all-reduce | flops 2 | bytes 16 | tf_op jit(solution)/shard_map/psum | solution.py:289
  (2556 shorter events, 810.8 us)
Async XLA Ops:
  0.6 12.5 %copy-start.123 = (f32[3]{0:T(128)S(1)}, f32[3]{0:T(128)}, u32[]{:S(2)}) copy-start(f32[3]{0:T(128)} %param.41) | copy-start | bytes 40
  0.6 13.8 %copy-start.87 = (bf16[2,5,128,128]{3,2,1,0:T(8,128)(2,1)S(1)}, bf16[2,5,128,128]{3,2,1,0:T(8,128)(2,1)}, u32[]{:S(2)}) copy-start(bf16[2,5,128,128]{3,2,1,0:T(8,128)(2,1)} %param.43) | copy-start | bytes 983044
  1.5 17.7 %collective-permute-start.2 = (f32[3,32]{1,0:T(4,128)S(1)}, f32[3,32]{1,0:T(4,128)S(1)}, u32[]{:S(2)}, u32[]{:S(2)}) collective-permute-start(f32[3,32]{1,0:T(4,128)S(1)} %get-tuple-element.3887), channel_id=1, source_target_pairs={{0,1},{1,2},{2,3},{3,4},{4,5},{5,6},{6,7},{7,8},{8,9},{9,10},{10,1... | collective-permute-start | bytes 1160 | tf_op jit(solution)/shard_map/ppermute | solution.py:27
  1.9 13.3 %copy-start.125 = (s32[4,128]{1,0:T(4,128)S(1)}, s32[4,128]{1,0:T(4,128)}, u32[]{:S(2)}) copy-start(s32[4,128]{1,0:T(4,128)} %param.35) | copy-start | bytes 6148
  1.9 14.0 %copy-start.118 = (f32[2,16,128]{2,1,0:T(8,128)S(1)}, f32[2,16,128]{2,1,0:T(8,128)}, u32[]{:S(2)}) copy-start(f32[2,16,128]{2,1,0:T(8,128)} %param.44) | copy-start | bytes 49156
  1.9 14.6 %copy-start.126 = (s32[128]{0:T(128)S(1)}, s32[128]{0:T(128)}, u32[]{:S(2)}) copy-start(s32[128]{0:T(128)} %param.36) | copy-start | bytes 1540
  1.9 17.2 %copy-start.106 = (f32[3,128]{1,0:T(4,128)S(1)}, f32[3,128]{1,0:T(4,128)}, u32[]{:S(2)}) copy-start(f32[3,128]{1,0:T(4,128)} %param.37) | copy-start | bytes 4612
  1.9 17.2 %collective-permute-start.3 = (f32[3,32]{1,0:T(4,128)S(1)}, f32[3,32]{1,0:T(4,128)S(1)}, u32[]{:S(2)}, u32[]{:S(2)}) collective-permute-start(f32[3,32]{1,0:T(4,128)S(1)} %get-tuple-element.3888), channel_id=1, source_target_pairs={{1,0},{2,1},{3,2},{4,3},{5,4},{6,5},{7,6},{8,7},{9,8},{10,9},{11,1... | collective-permute-start | bytes 1160 | tf_op jit(solution)/shard_map/ppermute | solution.py:30
  8.6 12.2 %collective-permute-start = (bf16[3200,32]{0,1:T(8,128)(2,1)S(1)}, bf16[3200,32]{0,1:T(8,128)(2,1)S(1)}, u32[]{:S(2)}, u32[]{:S(2)}) collective-permute-start(bf16[3200,32]{0,1:T(8,128)(2,1)S(1)} %get-tuple-element.3864), channel_id=1, source_target_pairs={{0,1},{1,2},{2,3},{3,4},{4,5},{5,6},{6,7},{7,8},{8,9},{9,10},{10,1... | collective-permute-start | bytes 614408 | tf_op jit(solution)/shard_map/ppermute | solution.py:27
  8.7 12.1 %collective-permute-start.1 = (bf16[3200,32]{0,1:T(8,128)(2,1)S(1)}, bf16[3200,32]{0,1:T(8,128)(2,1)}, u32[]{:S(2)}, u32[]{:S(2)}) collective-permute-start(bf16[3200,32]{0,1:T(8,128)(2,1)S(1)} %get-tuple-element.3865), channel_id=1, source_target_pairs={{1,0},{2,1},{3,2},{4,3},{5,4},{6,5},{7,6},{8,7},{9,8},{10,9},{11,1... | collective-permute-start | bytes 614408 | tf_op jit(solution)/shard_map/ppermute | solution.py:30
  39.5 22.9 %copy-start.119 = (s32[128]{0:T(128)}, s32[128]{0:T(128)S(1)}, u32[]{:S(2)}) copy-start(s32[128]{0:T(128)S(1)} %reshape.1508) | copy-start | bytes 1540 | tf_op jit(solution)/shard_map/jvp()/while
  93.3 22.9 %copy-start.119 = (s32[128]{0:T(128)}, s32[128]{0:T(128)S(1)}, u32[]{:S(2)}) copy-start(s32[128]{0:T(128)S(1)} %reshape.1508) | copy-start | bytes 1540 | tf_op jit(solution)/shard_map/jvp()/while
  147.0 22.9 %copy-start.119 = (s32[128]{0:T(128)}, s32[128]{0:T(128)S(1)}, u32[]{:S(2)}) copy-start(s32[128]{0:T(128)S(1)} %reshape.1508) | copy-start | bytes 1540 | tf_op jit(solution)/shard_map/jvp()/while
  200.6 23.0 %copy-start.119 = (s32[128]{0:T(128)}, s32[128]{0:T(128)S(1)}, u32[]{:S(2)}) copy-start(s32[128]{0:T(128)S(1)} %reshape.1508) | copy-start | bytes 1540 | tf_op jit(solution)/shard_map/jvp()/while
  250.9 7.9 collective-permute-start.4
  250.9 8.0 collective-permute-start.5
  336.7 12.0 %copy-start.16 = (f32[5,128,128]{1,2,0:T(8,128)S(1)}, f32[5,128,128]{1,2,0:T(8,128)}, u32[]{:S(2)}) copy-start(f32[5,128,128]{1,2,0:T(8,128)} %copy-done.15) | copy-start | bytes 983044 | tf_op jit(solution)/shard_map/jvp()/while
  426.2 12.0 %copy-start.16 = (f32[5,128,128]{1,2,0:T(8,128)S(1)}, f32[5,128,128]{1,2,0:T(8,128)}, u32[]{:S(2)}) copy-start(f32[5,128,128]{1,2,0:T(8,128)} %copy-done.15) | copy-start | bytes 983044 | tf_op jit(solution)/shard_map/jvp()/while
  515.7 12.0 %copy-start.16 = (f32[5,128,128]{1,2,0:T(8,128)S(1)}, f32[5,128,128]{1,2,0:T(8,128)}, u32[]{:S(2)}) copy-start(f32[5,128,128]{1,2,0:T(8,128)} %copy-done.15) | copy-start | bytes 983044 | tf_op jit(solution)/shard_map/jvp()/while
  605.1 12.0 %copy-start.16 = (f32[5,128,128]{1,2,0:T(8,128)S(1)}, f32[5,128,128]{1,2,0:T(8,128)}, u32[]{:S(2)}) copy-start(f32[5,128,128]{1,2,0:T(8,128)} %copy-done.15) | copy-start | bytes 983044 | tf_op jit(solution)/shard_map/jvp()/while
  664.7 13.6 %copy-start.18 = (f32[5,128,128]{1,0,2:T(8,128)S(1)}, f32[5,128,128]{1,0,2:T(8,128)}, u32[]{:S(2)}) copy-start(f32[5,128,128]{1,0,2:T(8,128)} %get-tuple-element.4786) | copy-start | bytes 983044 | tf_op jit(solution)/shard_map/transpose(jvp())/while
  667.6 13.5 %copy-start.19 = (f32[5,128,128]{1,0,2:T(8,128)S(1)}, f32[5,128,128]{1,0,2:T(8,128)}, u32[]{:S(2)}) copy-start(f32[5,128,128]{1,0,2:T(8,128)} %get-tuple-element.4791) | copy-start | bytes 983044 | tf_op jit(solution)/shard_map/transpose(jvp())/while
  723.6 13.6 %copy-start.18 = (f32[5,128,128]{1,0,2:T(8,128)S(1)}, f32[5,128,128]{1,0,2:T(8,128)}, u32[]{:S(2)}) copy-start(f32[5,128,128]{1,0,2:T(8,128)} %get-tuple-element.4786) | copy-start | bytes 983044 | tf_op jit(solution)/shard_map/transpose(jvp())/while
  726.5 13.5 %copy-start.19 = (f32[5,128,128]{1,0,2:T(8,128)S(1)}, f32[5,128,128]{1,0,2:T(8,128)}, u32[]{:S(2)}) copy-start(f32[5,128,128]{1,0,2:T(8,128)} %get-tuple-element.4791) | copy-start | bytes 983044 | tf_op jit(solution)/shard_map/transpose(jvp())/while
  783.2 13.7 %copy-start.18 = (f32[5,128,128]{1,0,2:T(8,128)S(1)}, f32[5,128,128]{1,0,2:T(8,128)}, u32[]{:S(2)}) copy-start(f32[5,128,128]{1,0,2:T(8,128)} %get-tuple-element.4786) | copy-start | bytes 983044 | tf_op jit(solution)/shard_map/transpose(jvp())/while
  786.2 13.5 %copy-start.19 = (f32[5,128,128]{1,0,2:T(8,128)S(1)}, f32[5,128,128]{1,0,2:T(8,128)}, u32[]{:S(2)}) copy-start(f32[5,128,128]{1,0,2:T(8,128)} %get-tuple-element.4791) | copy-start | bytes 983044 | tf_op jit(solution)/shard_map/transpose(jvp())/while
  842.9 13.5 %copy-start.18 = (f32[5,128,128]{1,0,2:T(8,128)S(1)}, f32[5,128,128]{1,0,2:T(8,128)}, u32[]{:S(2)}) copy-start(f32[5,128,128]{1,0,2:T(8,128)} %get-tuple-element.4786) | copy-start | bytes 983044 | tf_op jit(solution)/shard_map/transpose(jvp())/while
  845.8 13.4 %copy-start.19 = (f32[5,128,128]{1,0,2:T(8,128)S(1)}, f32[5,128,128]{1,0,2:T(8,128)}, u32[]{:S(2)}) copy-start(f32[5,128,128]{1,0,2:T(8,128)} %get-tuple-element.4791) | copy-start | bytes 983044 | tf_op jit(solution)/shard_map/transpose(jvp())/while
  883.3 8.7 collective-permute-start.6
  883.3 8.6 collective-permute-start.7
  977.2 5.8 collective-permute-start.8
  977.9 5.9 collective-permute-start.9
  (446 other events, 1492.8 us)
where the time goes:
time: 1050 us; the launch traced here: 1030 us
  local copies, waits for them, and re-layouts  591 us (56%)
  other arithmetic  177 us (17%)
  matrix products  158 us (15%)
  blocking collectives  34.2 us (3%)
  loops' own time  31.5 us (3%)
  starting transfers between devices  23.9 us (2%)
    dot_general x220, matrix products, contract(): jnp.einsum(closed_expression, former, latter, preferred_element_type=jnp....  139 us
    dynamic_update_slice x88, local copies, waits for them, and re-layouts, first_pass(): stacked = lax.map(first_one_block, jnp.arange(block_total, dtype=jnp.int32))  71.2 us
    concatenate x8, local copies, waits for them, and re-layouts, edge_messages(): jnp.concatenate(rotated_back, axis=0).reshape(NCOEF, channels, targets, KNB)  71 us
    dynamic_slice x108, local copies, waits for them, and re-layouts, energy_pass(): lax.map(energy_one_block, jnp.arange(block_total, dtype=jnp.int32))  69.2 us
    slice x96, local copies, waits for them, and re-layouts, edge_messages(): picked[first_row:first_row + degree_size]  51.4 us
    another operation x71, local copies, waits for them, and re-layouts  48.4 us
    while x944, local copies, waits for them, and re-layouts  36.7 us
    psum x1, blocking collectives, shards(): lax.psum(0.5 * jnp.sum(masses * jnp.sum(kicked * kicked, axis=0)), 'gx')  34.2 us
  transfers between devices with their start and end apart: 10, of which 2 were waited for; matrix products, arithmetic and copies ran while one was open for 1% of the time, Pallas kernels for 0%

commit v1 on v0

v1 whole, which is shorter than its diff:
```python
import functools

import jax
import jax.numpy as jnp
from jax import lax
from jax.experimental import pallas as pl
from jax.experimental.pallas import tpu as pltpu
from jax.sharding import PartitionSpec as P

LMAX = 4
MMAX = 2
NCOEF = 25
KNB = 4
GHOST = 32
NRBF = 16
C = 128
OWN = 128
ROWS = NCOEF * C
WROWS = 115
EDGES = KNB * OWN

EPSILON = 1e-06
SOFTENING = 0.25
STEP_TIME = 0.1
FRICTION = 0.9
RADIAL_SPREAD = 0.5

GROUPS = OWN // GHOST
PER_GROUP = -(-NCOEF // GROUPS)
PACKED = PER_GROUP * C
LAST = (NCOEF - (GROUPS - 1) * PER_GROUP) * C
GROUP_ROWS = (PACKED,) * (GROUPS - 1) + (LAST,)
VMEM_LIMIT = 56 * 1024 * 1024

F32 = jnp.float32
BF16 = jnp.bfloat16


def frame_layout():
    layout = []
    offset = 0
    for degree in range(LMAX + 1):
        row_count = min(2 * degree + 1, 2 * MMAX + 1)
        layout.append((degree, row_count, offset))
        offset = offset + row_count * (2 * degree + 1)
    return layout


LAYOUT = frame_layout()
ORDER_START = (0, 5, 13)
EDGE_ROWS = 19


def edge_row(degree, row):
    if row == 0:
        return degree
    order = (row + 1) // 2
    return ORDER_START[order] + 2 * (degree - order) + (row + 1) % 2


def iota(shape, dim):
    return lax.broadcasted_iota(jnp.int32, shape, dim)


def dot(former, latter):
    return jnp.dot(former, latter, preferred_element_type=F32)


def one_hot(hit):
    return jnp.where(hit, 1.0, 0.0).astype(BF16)


def split_three(values):
    high = values.astype(BF16).astype(F32)
    rest = values - high
    middle = rest.astype(BF16).astype(F32)
    return high, middle, rest - middle


def rim_select(group):
    atom = iota((OWN, 2 * OWN), 0)
    lane = iota((OWN, 2 * OWN), 1)
    low = (lane < OWN) & (lane - GHOST * group == atom) & (atom < GHOST)
    high = (lane >= OWN) & (lane - OWN - GHOST * group == atom - (OWN - GHOST))
    return one_hot(low | (high & (atom >= OWN - GHOST)))


def rim_place(group):
    lane = iota((2 * OWN, OWN), 0)
    atom = iota((2 * OWN, OWN), 1)
    low = (lane < OWN) & (lane - GHOST * group == atom) & (atom < GHOST)
    high = (lane >= OWN) & (lane - OWN - GHOST * group == atom - (OWN - GHOST))
    return one_hot(low | (high & (atom >= OWN - GHOST)))


def pack_rims(read_rows, low_ref, high_ref, extra=None):
    selects = [rim_select(group) for group in range(GROUPS)]
    for block in range(PER_GROUP):
        total = None
        for group in range(GROUPS):
            coef = PER_GROUP * group + block
            if coef < NCOEF:
                part = dot(read_rows(coef * C, C), selects[group])
                total = part if total is None else total + part
        low_ref[pl.ds(block * C, C), :] = total[:, :OWN].astype(BF16)
        high_ref[pl.ds(block * C, C), :] = total[:, OWN:].astype(BF16)
        if extra is not None and block * C == LAST:
            rows = extra.shape[0]
            total = total[:rows] + dot(extra, selects[GROUPS - 1])
            low_ref[pl.ds(block * C, rows), :] = total[:, :OWN].astype(BF16)
            high_ref[pl.ds(block * C, rows), :] = total[:, OWN:].astype(BF16)


def position_parts(pos_ref, parts_ref):
    parts_ref[...] = jnp.zeros_like(parts_ref)
    for at, part in enumerate(split_three(pos_ref[...])):
        parts_ref[pl.ds(8 * at, 3), :] = part
    return parts_ref[...].astype(BF16)


def pack_kernel(feat_ref, pos_ref, low_ref, high_ref, parts_ref):
    parts = position_parts(pos_ref, parts_ref)
    pack_rims(lambda start, size: feat_ref[pl.ds(start, size), :], low_ref, high_ref, parts)


def edge_sources(nb_ref):
    own_at = []
    low_at = []
    high_at = []
    for slot in range(KNB):
        place = jnp.bitwise_and(nb_ref[slot : slot + 1, :], OWN - 1)
        gap = place - iota((1, OWN), 1)
        low = gap > OWN // 2
        high = gap < -(OWN // 2)
        own_at.append(jnp.where(low | high, -1, place))
        low_at.append(jnp.where(low, place - (OWN - GHOST), -1))
        high_at.append(jnp.where(high, place + OWN, -1))
    merge = functools.partial(jnp.concatenate, axis=1)
    return merge(own_at), merge(low_at), merge(high_at)


def own_one_hot(own_at):
    return one_hot(iota((OWN, EDGES), 0) == own_at)


def ghost_one_hot(low_at, high_at, group):
    at = jnp.maximum(low_at, high_at)
    at = jnp.where(at >= 0, at + GHOST * group, -1)
    return one_hot(iota((2 * OWN, EDGES), 0) == at)


def build_gathers(nb_ref, own_ref, ghost_ref):
    own_at, low_at, high_at = edge_sources(nb_ref)
    own_ref[...] = own_one_hot(own_at)
    for group in range(GROUPS):
        ghost_ref[group] = ghost_one_hot(low_at, high_at, group)
    return own_at, low_at, high_at


def corner_mask(block):
    lane = jnp.bitwise_and(iota((C, 2 * OWN), 1), OWN - 1)
    return (lane < OWN - GHOST) | (block * C < LAST)


def read_ghosts(low_ref, high_ref, block):
    low = low_ref[pl.ds(block * C, C), :].astype(F32)
    high = high_ref[pl.ds(block * C, C), :].astype(F32)
    merged = jnp.concatenate([low, high], axis=1)
    if block * C >= LAST:
        merged = jnp.where(corner_mask(block), merged, 0.0)
    return merged


def fold_rows(values):
    return jnp.sum(values.reshape(-1, 8, values.shape[1]), axis=0)


def over_groups(values):
    column = jnp.broadcast_to(jnp.sum(values, axis=0, keepdims=True), values.shape)
    sides = []
    for side in range(2):
        part = column[:, side * OWN : (side + 1) * OWN]
        total = part
        for group in range(1, GROUPS):
            total = total + pltpu.roll(part, GHOST * group, 1)
        sides.append(total)
    return jnp.concatenate(sides, axis=1)[:1]


def normalise(feat_ref, low_ref, high_ref, own_ref, ghost_ref):
    squares = jnp.zeros((8, OWN), F32)
    for coef in range(NCOEF):
        block = feat_ref[pl.ds(coef * C, C), :].astype(F32)
        squares = squares + fold_rows(block * block)
    mean = jnp.sum(squares, axis=0, keepdims=True) * (1.0 / ROWS)
    own_scale = lax.rsqrt(mean + EPSILON)
    for coef in range(NCOEF):
        rows = pl.ds(coef * C, C)
        own_ref[rows, :] = (feat_ref[rows, :].astype(F32) * own_scale).astype(BF16)
    squares = jnp.zeros((8, 2 * OWN), F32)
    for block in range(PER_GROUP):
        values = read_ghosts(low_ref, high_ref, block)
        squares = squares + fold_rows(values * values)
    ghost_scale = lax.rsqrt(over_groups(squares) * (1.0 / ROWS) + EPSILON)
    for block in range(PER_GROUP):
        values = read_ghosts(low_ref, high_ref, block) * ghost_scale
        ghost_ref[pl.ds(block * C, C), :] = values.astype(BF16)
    return own_scale, ghost_scale


def gather(own_ref, ghost_ref, own_hot_ref, ghost_hot_ref, out_ref):
    for group, rows in enumerate(GROUP_ROWS):
        start = group * PACKED
        out_ref[pl.ds(start, rows), :] = dot(
            own_ref[pl.ds(start, rows), :], own_hot_ref[...]
        ) + dot(ghost_ref[pl.ds(0, rows), :], ghost_hot_ref[group])


def twice(values):
    return jnp.concatenate([values, values], axis=0)


def spread_frames(frame_ref, wide_ref):
    for entry in range(WROWS):
        wide_ref[entry] = jnp.broadcast_to(frame_ref[entry : entry + 1, :], (8, EDGES))


def slot_lanes(slot):
    return pl.ds(slot * OWN, OWN)


def to_frame(picked_ref, wide_ref, out_ref):
    @pl.loop(0, C // 16)
    def _(step):
        start = pl.multiple_of(step * 16, 16)
        for slot in range(KNB):
            lanes = slot_lanes(slot)
            for degree, row_count, offset in LAYOUT:
                size = 2 * degree + 1
                parts = [
                    picked_ref[pl.ds((degree * degree + k) * C + start, 16), lanes]
                    for k in range(size)
                ]
                for row in range(row_count):
                    total = None
                    for k in range(size):
                        term = twice(wide_ref[offset + row * size + k, :, lanes]) * parts[k]
                        total = term if total is None else total + term
                    at = edge_row(degree, row) * C
                    out_ref[pl.ds(at + start, 16), lanes] = total.astype(BF16)


def from_frame(frame_rows_ref, wide_ref, out_ref):
    @pl.loop(0, C // 16)
    def _(step):
        start = pl.multiple_of(step * 16, 16)
        for slot in range(KNB):
            lanes = slot_lanes(slot)
            for degree, row_count, offset in LAYOUT:
                size = 2 * degree + 1
                parts = [
                    frame_rows_ref[pl.ds(edge_row(degree, row) * C + start, 16), lanes]
                    for row in range(row_count)
                ]
                for k in range(size):
                    total = None
                    for row in range(row_count):
                        term = twice(wide_ref[offset + row * size + k, :, lanes]) * parts[row]
                        total = term if total is None else total + term
                    at = (degree * degree + k) * C
                    out_ref[pl.ds(at + start, 16), lanes] = total.astype(BF16)


def build_weights(weight_ref, zero_ref, pair_ref):
    turned = [
        jnp.transpose(weight_ref[part].astype(F32)).astype(BF16) for part in range(2 * MMAX + 1)
    ]
    zero_ref[...] = turned[0]
    for order in range(1, MMAX + 1):
        real, imag = turned[2 * order - 1], turned[2 * order]
        pair_ref[order - 1, :C, :C] = real
        pair_ref[order - 1, :C, C:] = -imag
        pair_ref[order - 1, C:, :C] = imag
        pair_ref[order - 1, C:, C:] = real


def build_back_weights(weight_ref, zero_ref, pair_ref):
    zero_ref[...] = weight_ref[0]
    for order in range(1, MMAX + 1):
        real, imag = weight_ref[2 * order - 1], weight_ref[2 * order]
        pair_ref[order - 1, :C, :C] = real
        pair_ref[order - 1, :C, C:] = imag
        pair_ref[order - 1, C:, :C] = -imag
        pair_ref[order - 1, C:, C:] = real


def convolve(rows_ref, zero_ref, pair_ref, out_ref):
    for degree in range(LMAX + 1):
        rows = pl.ds(degree * C, C)
        out_ref[rows, :] = dot(zero_ref[...], rows_ref[rows, :]).astype(out_ref.dtype)
    for order in range(1, MMAX + 1):
        for degree in range(order, LMAX + 1):
            rows = pl.ds((ORDER_START[order] + 2 * (degree - order)) * C, 2 * C)
            out_ref[rows, :] = dot(pair_ref[order - 1], rows_ref[rows, :]).astype(out_ref.dtype)


def radial(distance):
    centers = 0.5 + 5.5 * iota((NRBF, EDGES), 0).astype(F32) / (NRBF - 1)
    offset = (distance - centers) / RADIAL_SPREAD
    return jnp.exp(-(offset * offset)), offset


def edge_gate(radial_ref, basis):
    return lax.dot_general(
        radial_ref[...],
        basis,
        (((0,), (0,)), ((), ())),
        precision=lax.Precision.HIGHEST,
        preferred_element_type=F32,
    )


def distance_slope(radial_ref, gate_slope, distance):
    basis, offset = radial(distance)
    basis_slope = jnp.dot(
        radial_ref[...], gate_slope, precision=lax.Precision.HIGHEST, preferred_element_type=F32
    )
    terms = basis_slope * basis * offset * (-2.0 / RADIAL_SPREAD)
    return jnp.sum(terms, axis=0, keepdims=True)


def message_rows(degree, row_count, offset, start, turned_ref, gate_ref, wide_ref):
    size = 2 * degree + 1
    sums = [None] * size
    for slot in range(KNB):
        lanes = slot_lanes(slot)
        gate = gate_ref[pl.ds(start, 16), lanes]
        for row in range(row_count):
            gated = turned_ref[pl.ds(edge_row(degree, row) * C + start, 16), lanes] * gate
            for k in range(size):
                term = twice(wide_ref[offset + row * size + k, :, lanes]) * gated
                sums[k] = term if sums[k] is None else sums[k] + term
    return sums


def slope_rows(degree, row_count, offset, row, lanes, slopes, wide_ref):
    size = 2 * degree + 1
    total = None
    for k in range(size):
        term = twice(wide_ref[offset + row * size + k, :, lanes]) * slopes[k]
        total = term if total is None else total + term
    return total


def first_kernel(
    feat_ref, low_ref, high_ref, frames_ref, nb_ref, counts_ref, pos_ref, shift_ref,
    weight_ref, radial_ref,
    hidden_ref, turned_ref, frame_out_ref, edge_ref, send_low_ref, send_high_ref,
    parts_ref, own_hot_ref, ghost_hot_ref, own_ref, ghost_ref, picked_ref, wide_ref,
    rows_ref, turned_f32_ref, gate_ref, zero_ref, pair_ref,
):
    column = iota((EDGES, EDGES), 1)
    wanted = jnp.bitwise_and(column, OWN - 1) * KNB + column // OWN
    moved = dot(frames_ref[...], one_hot(iota((EDGES, EDGES), 0) == wanted))
    counts = counts_ref[...]
    live = jnp.concatenate(
        [jnp.where(slot < counts, 1.0, 0.0) for slot in range(KNB)], axis=1
    )
    frame_out_ref[...] = moved * live
    spread_frames(frame_out_ref, wide_ref)
    own_at, low_at, high_at = build_gathers(nb_ref, own_hot_ref, ghost_hot_ref)
    parts = position_parts(pos_ref, parts_ref)
    ghosts = jnp.concatenate(
        [low_ref[pl.ds(LAST, 32), :], high_ref[pl.ds(LAST, 32), :]], axis=1
    )
    found = dot(parts, own_hot_ref[...]) + dot(ghosts, ghost_hot_ref[GROUPS - 1])
    source = (found[0:8] + found[8:16]) + found[16:24]
    shift = jnp.where(low_at >= 0, shift_ref[0], jnp.where(high_at >= 0, shift_ref[1], 0.0))
    first = iota((8, EDGES), 0) == 0
    parts_ref[pl.ds(0, 3), :] = pos_ref[...]
    target = jnp.concatenate([parts_ref[0:8, :]] * KNB, axis=1)
    vector = source + jnp.where(first, shift, 0.0) - target
    distance = jnp.sqrt(jnp.sum(vector * vector, axis=0, keepdims=True) + SOFTENING)
    edge_ref[...] = jnp.where(iota((8, EDGES), 0) == 3, distance, vector)
    gate_ref[...] = edge_gate(radial_ref, radial(distance)[0])
    build_weights(weight_ref, zero_ref, pair_ref)
    normalise(feat_ref, low_ref, high_ref, own_ref, ghost_ref)
    gather(own_ref, ghost_ref, own_hot_ref, ghost_hot_ref, picked_ref)
    to_frame(picked_ref, wide_ref, rows_ref)
    convolve(rows_ref, zero_ref, pair_ref, turned_f32_ref)

    @pl.loop(0, C // 16)
    def _(step):
        start = pl.multiple_of(step * 16, 16)
        for degree, row_count, offset in LAYOUT:
            sums = message_rows(
                degree, row_count, offset, start, turned_f32_ref, gate_ref, wide_ref
            )
            for k, total in enumerate(sums):
                rows = pl.ds((degree * degree + k) * C + start, 16)
                hidden = feat_ref[rows, :].astype(F32) + total * KNB ** (-0.5)
                hidden_ref[rows, :] = hidden.astype(BF16)
        for row in range(EDGE_ROWS):
            rows = pl.ds(row * C + start, 16)
            turned_ref[rows, :] = turned_f32_ref[rows, :].astype(BF16)

    pack_rims(lambda start, size: hidden_ref[pl.ds(start, size), :], send_low_ref, send_high_ref)


def second_kernel(
    feat_ref, low_ref, high_ref, frame_ref, nb_ref, edge_ref, weight_ref, radial_ref,
    readout_ref,
    slope_ref, distance_slope_ref, send_low_ref, send_high_ref,
    own_hot_ref, ghost_hot_ref, own_ref, ghost_ref, picked_ref, wide_ref, rows_ref,
    turned_ref, gate_ref, zero_ref, pair_ref, upper_ref, gate_slope_ref, turned_slope_ref,
    readout_wide_ref, edge_slope_ref, ghost_slope_ref,
):
    spread_frames(frame_ref, wide_ref)
    build_gathers(nb_ref, own_hot_ref, ghost_hot_ref)
    distance = edge_ref[3:4, :]
    gate_ref[...] = edge_gate(radial_ref, radial(distance)[0])
    build_weights(weight_ref, zero_ref, pair_ref)
    own_scale, ghost_scale = normalise(feat_ref, low_ref, high_ref, own_ref, ghost_ref)
    gather(own_ref, ghost_ref, own_hot_ref, ghost_hot_ref, picked_ref)
    to_frame(picked_ref, wide_ref, rows_ref)
    convolve(rows_ref, zero_ref, pair_ref, turned_ref)
    for degree in range(LMAX + 1):
        row = jnp.broadcast_to(readout_ref[degree : degree + 1, :], (C, C))
        readout_wide_ref[degree] = jnp.transpose(row) * (1.0 / (2 * degree + 1))

    @pl.loop(0, C // 16)
    def _(step):
        start = pl.multiple_of(step * 16, 16)
        channels = pl.ds(start, 16)
        gate_slopes = [None] * KNB
        for degree, row_count, offset in LAYOUT:
            sums = message_rows(degree, row_count, offset, start, turned_ref, gate_ref, wide_ref)
            weight = readout_wide_ref[degree, channels, :]
            slopes = []
            for k, total in enumerate(sums):
                rows = pl.ds((degree * degree + k) * C + start, 16)
                upper = feat_ref[rows, :].astype(F32) + total * KNB ** (-0.5)
                slope = upper * weight
                upper_ref[rows, :] = slope * 2.0
                slopes.append(slope * (2.0 * KNB ** (-0.5)))
            for slot in range(KNB):
                lanes = slot_lanes(slot)
                gate = gate_ref[channels, lanes]
                for row in range(row_count):
                    slope = slope_rows(
                        degree, row_count, offset, row, lanes, slopes, wide_ref
                    )
                    rows = pl.ds(edge_row(degree, row) * C + start, 16)
                    term = turned_ref[rows, lanes] * slope
                    before = gate_slopes[slot]
                    gate_slopes[slot] = term if before is None else before + term
                    turned_slope_ref[rows, lanes] = (slope * gate).astype(BF16)
        for slot in range(KNB):
            gate_slope_ref[channels, slot_lanes(slot)] = gate_slopes[slot]

    distance_slope_ref[...] = jnp.broadcast_to(
        distance_slope(radial_ref, gate_slope_ref[...], distance), (8, EDGES)
    )
    build_back_weights(weight_ref, zero_ref, pair_ref)
    convolve(turned_slope_ref, zero_ref, pair_ref, turned_ref)
    from_frame(turned_ref, wide_ref, edge_slope_ref)
    spread_own = jnp.transpose(own_hot_ref[...].astype(F32)).astype(BF16)
    for group, rows in enumerate(GROUP_ROWS):
        block = pl.ds(group * PACKED, rows)
        slope_ref[block, :] = dot(edge_slope_ref[block, :], spread_own)
    for group, rows in enumerate(GROUP_ROWS):
        spread_ghost = jnp.transpose(ghost_hot_ref[group].astype(F32)).astype(BF16)
        part = dot(edge_slope_ref[pl.ds(group * PACKED, rows), :], spread_ghost)
        if group == 0:
            ghost_slope_ref[...] = part
        else:
            ghost_slope_ref[pl.ds(0, rows), :] += part
    along = jnp.zeros((8, OWN), F32)
    for coef in range(NCOEF):
        rows = pl.ds(coef * C, C)
        along = along + fold_rows(slope_ref[rows, :] * feat_ref[rows, :].astype(F32))
    along = jnp.sum(along, axis=0, keepdims=True) * (1.0 / ROWS)
    along = along * own_scale * own_scale * own_scale
    for coef in range(NCOEF):
        rows = pl.ds(coef * C, C)
        slope_ref[rows, :] = (
            upper_ref[rows, :]
            + slope_ref[rows, :] * own_scale
            - feat_ref[rows, :].astype(F32) * along
        )
    along = jnp.zeros((8, 2 * OWN), F32)
    for block in range(PER_GROUP):
        values = read_ghosts(low_ref, high_ref, block)
        along = along + fold_rows(ghost_slope_ref[pl.ds(block * C, C), :] * values)
    along = over_groups(along) * (1.0 / ROWS)
    along = along * ghost_scale * ghost_scale * ghost_scale
    for block in range(PER_GROUP):
        rows = pl.ds(block * C, C)
        values = read_ghosts(low_ref, high_ref, block)
        back = ghost_slope_ref[rows, :] * ghost_scale - values * along
        send_low_ref[rows, :] = back[:, :OWN].astype(BF16)
        send_high_ref[rows, :] = back[:, OWN:].astype(BF16)


def third_kernel(
    slope_ref, low_ref, high_ref, frame_ref, nb_ref, edge_ref, radial_ref, turned_ref,
    second_slope_ref,
    force_ref, ghost_low_ref, ghost_high_ref, virial_ref,
    wide_ref, gate_slope_ref, hidden_slope_ref,
):
    spread_frames(frame_ref, wide_ref)
    for group, rows in enumerate(GROUP_ROWS):
        block = pl.ds(group * PACKED, rows)
        back = jnp.concatenate([low_ref[pl.ds(0, rows), :], high_ref[pl.ds(0, rows), :]], axis=1)
        total = slope_ref[block, :] + dot(back, rim_place(group))
        hidden_slope_ref[block, :] = total * KNB ** (-0.5)

    @pl.loop(0, C // 16)
    def _(step):
        start = pl.multiple_of(step * 16, 16)
        gate_slopes = [None] * KNB
        for degree, row_count, offset in LAYOUT:
            slopes = [
                hidden_slope_ref[pl.ds((degree * degree + k) * C + start, 16), :]
                for k in range(2 * degree + 1)
            ]
            for slot in range(KNB):
                lanes = slot_lanes(slot)
                for row in range(row_count):
                    slope = slope_rows(
                        degree, row_count, offset, row, lanes, slopes, wide_ref
                    )
                    rows = pl.ds(edge_row(degree, row) * C + start, 16)
                    term = turned_ref[rows, lanes].astype(F32) * slope
                    before = gate_slopes[slot]
                    gate_slopes[slot] = term if before is None else before + term
        for slot in range(KNB):
            gate_slope_ref[pl.ds(start, 16), slot_lanes(slot)] = gate_slopes[slot]

    distance = edge_ref[3:4, :]
    slope = distance_slope(radial_ref, gate_slope_ref[...], distance) + second_slope_ref[0:1, :]
    vector = jnp.where(iota((8, EDGES), 0) < 3, edge_ref[...], 0.0)
    pull = vector * (slope / distance)
    virial = -jnp.sum(jnp.sum(pull * vector, axis=0, keepdims=True), axis=1, keepdims=True)
    virial_ref[...] = jnp.broadcast_to(virial, (8, OWN))
    high, middle, low = split_three(pull)
    parts = jnp.concatenate([high, middle, low, jnp.zeros((8, EDGES), F32)], axis=0).astype(BF16)
    own_at, low_at, high_at = edge_sources(nb_ref)
    spread_own = jnp.transpose(own_one_hot(own_at).astype(F32)).astype(BF16)
    spread_ghost = jnp.transpose(ghost_one_hot(low_at, high_at, 0).astype(F32)).astype(BF16)
    landed = dot(parts, spread_own)
    landed = landed[0:8] + landed[8:16] + landed[16:24]
    for slot in range(KNB):
        landed = landed - pull[:, slot * OWN : (slot + 1) * OWN]
    force_ref[...] = -landed
    landed = dot(parts, spread_ghost)
    landed = landed[0:8] + landed[8:16] + landed[16:24]
    ghost_low_ref[...] = -landed[:, :OWN]
    ghost_high_ref[...] = -landed[:, OWN:]


def kick_kernel(
    force_ref, low_ref, high_ref, virial_ref, velocities_ref, masses_ref,
    kicked_ref, strain_ref,
):
    lane = iota((8, OWN), 1)
    force = force_ref[...] + jnp.where(lane < GHOST, low_ref[...], 0.0)
    high = pltpu.roll(high_ref[...], OWN - GHOST, 1)
    force = force + jnp.where(lane >= OWN - GHOST, high, 0.0)
    masses = masses_ref[...]
    kicked = velocities_ref[...] + STEP_TIME * force[0:3] / masses
    kicked_ref[...] = kicked
    total = jnp.sum(masses * jnp.sum(kicked * kicked, axis=0, keepdims=True))
    strain_ref[...] = virial_ref[...] + total


def finish_kernel(
    strain_ref, kicked_ref, masses_ref, noise_ref, positions_ref, box_ref, control_ref,
    fractional_ref, velocities_ref, new_box_ref,
):
    row = iota((3, OWN), 0)
    box = jnp.where(row == 0, box_ref[0], jnp.where(row == 1, box_ref[1], box_ref[2]))
    volume = box_ref[0] * box_ref[1] * box_ref[2]
    pressure = strain_ref[0:1, :] / (3.0 * volume)
    rescale = jnp.exp(control_ref[1] * (pressure - control_ref[2]) / 3.0)
    kick = jnp.sqrt((1.0 - FRICTION * FRICTION) * control_ref[0] / masses_ref[...])
    thermal = FRICTION * kicked_ref[...] + kick * noise_ref[...]
    fractional_ref[...] = (positions_ref[...] + STEP_TIME * thermal) / box
    velocities_ref[...] = thermal / rescale
    new_box_ref[...] = box * rescale


def call(kernel, outs, scratch, args, flops=0, scalars=(), moved=4 << 20):
    specs = [
        pl.BlockSpec(memory_space=pltpu.SMEM if at in scalars else pltpu.VMEM)
        for at in range(len(args))
    ]
    return pl.pallas_call(
        kernel,
        out_shape=[jax.ShapeDtypeStruct(shape, kind) for shape, kind in outs],
        in_specs=specs,
        out_specs=[pl.BlockSpec(memory_space=pltpu.VMEM) for _ in outs],
        scratch_shapes=[pltpu.VMEM(shape, kind) for shape, kind in scratch],
        compiler_params=pltpu.CompilerParams(vmem_limit_bytes=VMEM_LIMIT),
        cost_estimate=pl.CostEstimate(flops=flops, bytes_accessed=moved, transcendentals=0),
    )(*args)


def shards(
    node_feat,
    frames,
    neighbours,
    counts,
    positions,
    velocities,
    masses,
    thermal_noise,
    box_lengths,
    control,
    conv_weight,
    radial_weight,
    readout,
):
    assert positions.shape[1] == OWN
    count = lax.axis_size("gx")
    place = lax.axis_index("gx")
    forward = [(i, (i + 1) % count) for i in range(count)]
    backward = [(target, source) for source, target in forward]

    def exchange(to_low, to_high):
        from_low = lax.ppermute(to_high, "gx", forward)
        from_high = lax.ppermute(to_low, "gx", backward)
        return from_low, from_high

    packed = ((PACKED, OWN), BF16)
    to_low, to_high = call(
        pack_kernel, [packed, packed], [((32, OWN), F32)], (node_feat, positions)
    )
    from_low, from_high = exchange(to_low, to_high)
    length = box_lengths[0]
    shift = jnp.stack(
        [
            jnp.where(place == 0, -length, 0.0),
            jnp.where(place == count - 1, length, 0.0),
        ]
    )
    gathers = [((OWN, EDGES), BF16), ((GROUPS, 2 * OWN, EDGES), BF16)]
    work = [
        ((ROWS, OWN), BF16),
        ((PACKED, 2 * OWN), BF16),
        ((ROWS, EDGES), F32),
        ((WROWS, 8, EDGES), F32),
        ((EDGE_ROWS * C, EDGES), BF16),
        ((EDGE_ROWS * C, EDGES), F32),
        ((C, EDGES), F32),
        ((C, C), BF16),
        ((MMAX, 2 * C, 2 * C), BF16),
    ]
    hidden, turned, frame, edge, to_low, to_high = call(
        first_kernel,
        [
            ((ROWS, OWN), BF16),
            ((EDGE_ROWS * C, EDGES), BF16),
            ((WROWS, EDGES), F32),
            ((8, EDGES), F32),
            packed,
            packed,
        ],
        [((32, OWN), F32)] + gathers + work,
        (
            node_feat, from_low, from_high, frames, neighbours, counts[None, :], positions,
            shift, conv_weight[0], radial_weight[0],
        ),
        scalars=(7,),
    )
    from_low, from_high = exchange(to_low, to_high)
    slope, second_slope, to_low, to_high = call(
        second_kernel,
        [((ROWS, OWN), F32), ((8, EDGES), F32), packed, packed],
        gathers
        + work
        + [
            ((ROWS, OWN), F32),
            ((C, EDGES), F32),
            ((EDGE_ROWS * C, EDGES), BF16),
            ((LMAX + 1, C, C), F32),
            ((ROWS, EDGES), BF16),
            ((PACKED, 2 * OWN), F32),
        ],
        (
            hidden, from_low, from_high, frame, neighbours, edge, conv_weight[1],
            radial_weight[1], readout,
        ),
    )
    from_low, from_high = exchange(to_low, to_high)
    small = ((8, OWN), F32)
    force, to_low, to_high, virial = call(
        third_kernel,
        [small] * 4,
        [((WROWS, 8, EDGES), F32), ((C, EDGES), F32), ((ROWS, OWN), F32)],
        (
            slope, from_low, from_high, frame, neighbours, edge, radial_weight[0], turned,
            second_slope,
        ),
    )
    from_low, from_high = exchange(to_low, to_high)
    kicked, strain = call(
        kick_kernel,
        [((3, OWN), F32), small],
        [],
        (force, from_low, from_high, virial, velocities, masses[None, :]),
    )
    if count & (count - 1) == 0:
        step = 1
        while step < count:
            strain = strain + lax.ppermute(strain, "gx", [(i, i ^ step) for i in range(count)])
            step = 2 * step
    else:
        strain = lax.psum(strain, "gx")
    fractional, new_velocities, new_box = call(
        finish_kernel,
        [((3, OWN), F32)] * 3,
        [],
        (strain, kicked, masses[None, :], thermal_noise, positions, box_lengths, control),
        scalars=(5, 6),
    )
    return fractional, new_velocities, new_box[:, 0]


def solution(mesh):
    return jax.shard_map(
        shards,
        mesh=mesh,
        in_specs=(
            P(None, ("groups", "gx")),
            P(None, ("groups", "gx")),
            P(None, ("groups", "gx")),
            P(("groups", "gx")),
            P(None, ("groups", "gx")),
            P(None, ("groups", "gx")),
            P(("groups", "gx")),
            P(None, ("groups", "gx")),
            P("groups"),
            P("groups"),
            P(),
            P(),
            P(),
        ),
        out_specs=(P(None, ("groups", "gx")), P(None, ("groups", "gx")), P("groups")),
        check_vma=False,
    )
```

time: 1050 us -> 99.3 us (0.09); the launches traced: 1030 us -> 98.9 us
  local copies, waits for them, and re-layouts: 591 us -> 7.31 us
  other arithmetic: 177 us -> 1.86 us
  matrix products: 158 us -> 0 us
  Pallas kernels: 0 us -> 46.3 us
  blocking collectives: 34.2 us -> 0 us
  loops' own time: 31.5 us -> 0 us
  waiting for transfers between devices: 1.83 us -> 21.1 us
    dot_general x236 -> x0, matrix products: 158 us -> none  [the longest x220 139 us: contract(): jnp.einsum(closed_expression, former, latter, preferred_element_type=jnp....]
    slice x194 -> x1, local copies, waits for them, and re-layouts: 104 us -> 1.29 us  [shards(): return (fractional, new_velocities, new_box[:, 0])]
    dynamic_update_slice x112 -> x0, local copies, waits for them, and re-layouts: 100 us -> none  [the longest x88 71.2 us: first_pass(): stacked = lax.map(first_one_block, jnp.arange(block_total, dtype=jnp.int32))]
    dynamic_slice x140 -> x0, local copies, waits for them, and re-layouts: 94.1 us -> none  [the longest x108 69.2 us: energy_pass(): lax.map(energy_one_block, jnp.arange(block_total, dtype=jnp.int32))]
    concatenate x8 -> x0, local copies, waits for them, and re-layouts: 71 us -> none  [edge_messages(): jnp.concatenate(rotated_back, axis=0).reshape(NCOEF, channels, targets, KNB)]
    another operation x120 -> x0, local copies, waits for them, and re-layouts: 65 us -> none
    pallas_call x0 -> x6, Pallas kernels: none -> 46.3 us  [call(): pl.pallas_call(kernel, out_shape=[jax.ShapeDtypeStruct(shape, kind) for s...]
    dynamic_update_slice x44 -> x0, other arithmetic: 38.6 us -> none  [the longest x36 26.8 us: first_pass(): stacked = lax.map(first_one_block, jnp.arange(block_total, dtype=jnp.int32))]
  transfers between devices with their start and end apart: 10 -> 12, of which waited for: 2 -> 7; matrix products, arithmetic and copies ran while one was open for 1% -> 4% of each run, Pallas kernels for 0% -> 0%
where the time goes in v1:
time: 99.3 us; the launch traced here: 98.9 us
  Pallas kernels  46.3 us (47%)
  waiting for transfers between devices  21.1 us (21%)
  starting transfers between devices  20.3 us (20%)
  local copies, waits for them, and re-layouts  7.31 us (7%)
  between operations  1.98 us (2%)
  other arithmetic  1.86 us (2%)
    pallas_call x6, Pallas kernels, call(): pl.pallas_call(kernel, out_shape=[jax.ShapeDtypeStruct(shape, kind) for s...  46.3 us
    ppermute x4, starting transfers between devices, exchange(): from_high = lax.ppermute(to_low, 'gx', backward)  17.1 us
    ppermute x4, waiting for transfers between devices, shards(): lax.ppermute(strain, 'gx', [(i, i ^ step) for i in range(count)])  11.6 us
    ppermute x4, waiting for transfers between devices, exchange(): from_low = lax.ppermute(to_high, 'gx', forward)  9.53 us
    unnamed x16, local copies, waits for them, and re-layouts  2.94 us
  transfers between devices with their start and end apart: 12, of which 7 were waited for; matrix products, arithmetic and copies ran while one was open for 4% of the time, Pallas kernels for 0%

profile of v1, /device:TPU:0, one launch (start us, length us, event | category | flops | bytes accessed | tf_op | source)
XLA Modules:
  0.0 98.9 jit_solution(9568193910183239637)
XLA Ops:
  0.6 2.5 %shard_map.148 = (bf16[896,128]{1,0:T(8,128)(2,1)}, bf16[896,128]{1,0:T(8,128)(2,1)}) custom-call(bf16[3200,128]{1,0:T(8,128)(2,1)} %feat_ref.3, f32[3,128]{1,0:T(4,128)} %positions_ref.1), custom_call_target="tpu_custom_call" | custom-call | bytes 4194304 | tf_op jit(solution)/shard_map/pallas_call | solution.py:598
  3.1 0.5 collective-permute-start
  3.6 5.0 %collective-permute-start.1 = (bf16[896,128]{1,0:T(8,128)(2,1)}, bf16[896,128]{1,0:T(8,128)(2,1)S(1)}, u32[]{:S(2)}, u32[]{:S(2)}) collective-permute-start(bf16[896,128]{1,0:T(8,128)(2,1)} %get-tuple-element.25), channel_id=1, source_target_pairs={{1,0},{2,1},{3,2},{4,3},{5,4},{6,5},{7,6},{8,7},{9,8},{10,9},{11,1... | collective-permute-start | bytes 688136 | tf_op jit(solution)/shard_map/ppermute | solution.py:632
  9.2 1.8 %slice_bitcast_fusion = (bf16[5,128,128]{2,1,0:T(8,128)(2,1)}, bf16[5,128,128]{2,1,0:T(8,128)(2,1)}) fusion(bf16[2,5,128,128]{3,2,1,0:T(8,128)(2,1)} %param.23), kind=kLoop, calls=%fused_computation | loop fusion | bytes 655360 | tf_op jit(solution)/shard_map/squeeze | solution.py:691
  11.6 0.6 pad_maximum_fusion.shift_ref
  12.2 1.3 %slice_bitcast_fusion.2 = (f32[16,128]{1,0:T(8,128)}, f32[16,128]{1,0:T(8,128)}) fusion(f32[2,16,128]{2,1,0:T(8,128)} %param.24), kind=kLoop, calls=%fused_computation.2 | loop fusion | bytes 32768 | tf_op jit(solution)/shard_map/squeeze | solution.py:692
  13.6 0.7 copy-done
  14.4 12.0 %shard_map.149 = (bf16[3200,128]{1,0:T(8,128)(2,1)}, bf16[2432,512]{1,0:T(8,128)(2,1)}, f32[115,512]{1,0:T(8,128)}, f32[8,512]{1,0:T(8,128)}, bf16[896,128]{1,0:T(8,128)(2,1)}, /*index=5*/bf16[896,128]{1,0:T(8,128)(2,1)}) custom-call(bf16[3200,128]{1,0:T(8,128)(2,1)} %feat_ref.3, bf16[896,128]{1,0:T(8,128)(2,1)} %copy-done, bf16[896,128]{1,0:T(8,128)(2,1)} %copy-done.1, ...), custom_call_target="tpu_custom_call" | custom-call | bytes 4194304 | tf_op jit(solution)/shard_map/pallas_call | solution.py:598
  26.4 0.7 collective-permute-start.2
  27.0 3.8 %collective-permute-start.3 = (bf16[896,128]{1,0:T(8,128)(2,1)}, bf16[896,128]{1,0:T(8,128)(2,1)S(1)}, u32[]{:S(2)}, u32[]{:S(2)}) collective-permute-start(bf16[896,128]{1,0:T(8,128)(2,1)} %get-tuple-element.28), channel_id=1, source_target_pairs={{1,0},{2,1},{3,2},{4,3},{5,4},{6,5},{7,6},{8,7},{9,8},{10,9},{11,1... | collective-permute-start | bytes 688136 | tf_op jit(solution)/shard_map/ppermute | solution.py:632
  30.8 4.0 %collective-permute-done.2.low_ref = bf16[896,128]{1,0:T(8,128)(2,1)S(1)} collective-permute-done((bf16[896,128]{1,0:T(8,128)(2,1)}, bf16[896,128]{1,0:T(8,128)(2,1)S(1)}, u32[]{:S(2)}, u32[]{:S(2)}) %collective-permute-start.2) | collective-permute-done | bytes 229408 | tf_op jit(solution)/shard_map/ppermute | solution.py:631
  34.8 0.7 copy-done.3
  35.5 0.1 copy-done.5
  35.6 20.6 %shard_map.150 = (f32[3200,128]{1,0:T(8,128)}, f32[8,512]{1,0:T(8,128)}, bf16[896,128]{1,0:T(8,128)(2,1)}, bf16[896,128]{1,0:T(8,128)(2,1)}) custom-call(bf16[3200,128]{1,0:T(8,128)(2,1)} %get-tuple-element.26.feat_ref, bf16[896,128]{1,0:T(8,128)(2,1)} %copy-done.3, bf16[896,128]{1,0:T(8,128)(2,1)} %copy-done.5, f32[115,512]{1,0:T(8,128)} %get-tuple-element.29.frame_ref, ...), custom_call_target="tpu_custom_call" | custom-call | bytes 4194304 | tf_op jit(solution)/shard_map/pallas_call | solution.py:598
  56.2 0.5 collective-permute-start.4
  56.7 4.0 %collective-permute-start.5 = (bf16[896,128]{1,0:T(8,128)(2,1)}, bf16[896,128]{1,0:T(8,128)(2,1)S(1)}, u32[]{:S(2)}, u32[]{:S(2)}) collective-permute-start(bf16[896,128]{1,0:T(8,128)(2,1)} %get-tuple-element.33), channel_id=1, source_target_pairs={{1,0},{2,1},{3,2},{4,3},{5,4},{6,5},{7,6},{8,7},{9,8},{10,9},{11,1... | collective-permute-start | bytes 688136 | tf_op jit(solution)/shard_map/ppermute | solution.py:632
  60.7 4.0 %collective-permute-done.4.low_ref = bf16[896,128]{1,0:T(8,128)(2,1)S(1)} collective-permute-done((bf16[896,128]{1,0:T(8,128)(2,1)}, bf16[896,128]{1,0:T(8,128)(2,1)S(1)}, u32[]{:S(2)}, u32[]{:S(2)}) %collective-permute-start.4) | collective-permute-done | bytes 229408 | tf_op jit(solution)/shard_map/ppermute | solution.py:631
  64.7 0.7 copy-done.2
  65.5 8.3 %shard_map.151 = (f32[8,128]{1,0:T(8,128)}, f32[8,128]{1,0:T(8,128)}, f32[8,128]{1,0:T(8,128)}, f32[8,128]{1,0:T(8,128)}) custom-call(f32[3200,128]{1,0:T(8,128)} %get-tuple-element.31.slope_ref, bf16[896,128]{1,0:T(8,128)(2,1)} %copy-done.2, bf16[896,128]{1,0:T(8,128)(2,1)} %copy-done.4, f32[115,512]{1,0:T(8,128)} %get-tuple-element.29.frame_ref, ...), custom_call_target="tpu_custom_call" | custom-call | bytes 4194304 | tf_op jit(solution)/shard_map/pallas_call | solution.py:598
  73.8 4.4 %collective-permute-start.7 = (f32[8,128]{1,0:T(8,128)}, f32[8,128]{1,0:T(8,128)S(1)}, u32[]{:S(2)}, u32[]{:S(2)}) collective-permute-start(f32[8,128]{1,0:T(8,128)} %get-tuple-element.38), channel_id=1, source_target_pairs={{1,0},{2,1},{3,2},{4,3},{5,4},{6,5},{7,6},{8,7},{9,8},{10,9},{11,1... | collective-permute-start | bytes 12296 | tf_op jit(solution)/shard_map/ppermute | solution.py:632
  78.2 1.5 %collective-permute-done.6.low_ref = f32[8,128]{1,0:T(8,128)S(1)} collective-permute-done((f32[8,128]{1,0:T(8,128)}, f32[8,128]{1,0:T(8,128)S(1)}, u32[]{:S(2)}, u32[]{:S(2)}) %collective-permute-start.6) | collective-permute-done | bytes 4128 | tf_op jit(solution)/shard_map/ppermute | solution.py:631
  79.7 0.5 copy-done.6
  80.3 1.5 %shard_map.152 = (f32[3,128]{1,0:T(4,128)}, f32[8,128]{1,0:T(8,128)}) custom-call(f32[8,128]{1,0:T(8,128)} %get-tuple-element.36.force_ref, f32[8,128]{1,0:T(8,128)} %copy-done.6, f32[8,128]{1,0:T(8,128)} %copy-done.7, f32[8,128]{1,0:T(8,128)} %get-tuple-element.39.virial_ref, f32[3,128]{1,0:T(4,128)} %velocities_ref.1, f32[1,128]{1,0:T(1,128)} %bitcast.14), custom_call_target="tpu_custom_call" | custom-call | bytes 4194304 | tf_op jit(solution)/shard_map/pallas_call | solution.py:598
  81.8 1.4 %collective-permute-done.8 = f32[8,128]{1,0:T(8,128)S(1)} collective-permute-done((f32[8,128]{1,0:T(8,128)}, f32[8,128]{1,0:T(8,128)S(1)}, u32[]{:S(2)}, u32[]{:S(2)}) %collective-permute-start.8) | collective-permute-done | bytes 4128 | tf_op jit(solution)/shard_map/ppermute | solution.py:716
  83.2 0.7 add.12
  83.9 3.6 %collective-permute-done.9 = f32[8,128]{1,0:T(8,128)S(1)} collective-permute-done((f32[8,128]{1,0:T(8,128)S(1)}, f32[8,128]{1,0:T(8,128)S(1)}, u32[]{:S(2)}, u32[]{:S(2)}) %collective-permute-start.9) | collective-permute-done | bytes 4128 | tf_op jit(solution)/shard_map/ppermute | solution.py:716
  87.5 3.6 %collective-permute-done.10 = f32[8,128]{1,0:T(8,128)S(1)} collective-permute-done((f32[8,128]{1,0:T(8,128)S(1)}, f32[8,128]{1,0:T(8,128)S(1)}, u32[]{:S(2)}, u32[]{:S(2)}) %collective-permute-start.10) | collective-permute-done | bytes 4128 | tf_op jit(solution)/shard_map/ppermute | solution.py:716
  91.1 1.5 %collective-permute-start.11 = (f32[8,128]{1,0:T(8,128)S(1)}, f32[8,128]{1,0:T(8,128)S(1)}, u32[]{:S(2)}, u32[]{:S(2)}) collective-permute-start(f32[8,128]{1,0:T(8,128)S(1)} %add.14), channel_id=1, source_target_pairs={{0,8},{1,9},{2,10},{3,11},{4,12},{5,13},{6,14},{7,15},{8,0},{9,1},... | collective-permute-start | bytes 12296 | tf_op jit(solution)/shard_map/ppermute | solution.py:716
  92.6 3.0 %collective-permute-done.11 = f32[8,128]{1,0:T(8,128)S(1)} collective-permute-done((f32[8,128]{1,0:T(8,128)S(1)}, f32[8,128]{1,0:T(8,128)S(1)}, u32[]{:S(2)}, u32[]{:S(2)}) %collective-permute-start.11) | collective-permute-done | bytes 4128 | tf_op jit(solution)/shard_map/ppermute | solution.py:716
  95.6 0.6 add.15.strain_ref
  96.2 1.4 %shard_map.153 = (f32[3,128]{1,0:T(4,128)}, f32[3,128]{1,0:T(4,128)}, f32[3,128]{1,0:T(4,128)}) custom-call(f32[8,128]{1,0:T(8,128)} %add.15.strain_ref, f32[3,128]{1,0:T(4,128)} %get-tuple-element.41.kicked_ref, f32[1,128]{1,0:T(1,128)} %bitcast.15, f32[3,128]{1,0:T(4,128)} %noise_ref.1, f32[3,128]{1,0:T(4,128)} %positions_ref.1, f32[3]{0:T(128)} %box_ref.1, ...), custom_call_target="tpu_custom_call" | custom-call | bytes 4194304 | tf_op jit(solution)/shard_map/pallas_call | solution.py:598
  97.6 1.3 %slice_reduce_fusion = f32[3]{0:T(128)} fusion(f32[3,128]{1,0:T(4,128)} %get-tuple-element.44), kind=kLoop, calls=%fused_computation.4 | loop fusion | bytes 24 | tf_op jit(solution)/shard_map/slice | solution.py:727
  (22 shorter events, 0.4 us)
Async XLA Ops:
  3.1 10.4 %collective-permute-start = (bf16[896,128]{1,0:T(8,128)(2,1)}, bf16[896,128]{1,0:T(8,128)(2,1)S(1)}, u32[]{:S(2)}, u32[]{:S(2)}) collective-permute-start(bf16[896,128]{1,0:T(8,128)(2,1)} %get-tuple-element.24), channel_id=1, source_target_pairs={{0,1},{1,2},{2,3},{3,4},{4,5},{5,6},{6,7},{7,8},{8,9},{9,10},{10,1... | collective-permute-start | bytes 688136 | tf_op jit(solution)/shard_map/ppermute | solution.py:631
  3.6 10.0 %collective-permute-start.1 = (bf16[896,128]{1,0:T(8,128)(2,1)}, bf16[896,128]{1,0:T(8,128)(2,1)S(1)}, u32[]{:S(2)}, u32[]{:S(2)}) collective-permute-start(bf16[896,128]{1,0:T(8,128)(2,1)} %get-tuple-element.25), channel_id=1, source_target_pairs={{1,0},{2,1},{3,2},{4,3},{5,4},{6,5},{7,6},{8,7},{9,8},{10,9},{11,1... | collective-permute-start | bytes 688136 | tf_op jit(solution)/shard_map/ppermute | solution.py:632
  13.6 0.7 copy-start
  13.6 0.8 copy-start.1
  26.4 8.5 %collective-permute-start.2 = (bf16[896,128]{1,0:T(8,128)(2,1)}, bf16[896,128]{1,0:T(8,128)(2,1)S(1)}, u32[]{:S(2)}, u32[]{:S(2)}) collective-permute-start(bf16[896,128]{1,0:T(8,128)(2,1)} %get-tuple-element.27), channel_id=1, source_target_pairs={{0,1},{1,2},{2,3},{3,4},{4,5},{5,6},{6,7},{7,8},{8,9},{9,10},{10,1... | collective-permute-start | bytes 688136 | tf_op jit(solution)/shard_map/ppermute | solution.py:631
  27.0 7.8 %collective-permute-start.3 = (bf16[896,128]{1,0:T(8,128)(2,1)}, bf16[896,128]{1,0:T(8,128)(2,1)S(1)}, u32[]{:S(2)}, u32[]{:S(2)}) collective-permute-start(bf16[896,128]{1,0:T(8,128)(2,1)} %get-tuple-element.28), channel_id=1, source_target_pairs={{1,0},{2,1},{3,2},{4,3},{5,4},{6,5},{7,6},{8,7},{9,8},{10,9},{11,1... | collective-permute-start | bytes 688136 | tf_op jit(solution)/shard_map/ppermute | solution.py:632
  34.8 0.7 copy-start.3
  34.8 0.8 copy-start.5
  56.2 8.5 %collective-permute-start.4 = (bf16[896,128]{1,0:T(8,128)(2,1)}, bf16[896,128]{1,0:T(8,128)(2,1)S(1)}, u32[]{:S(2)}, u32[]{:S(2)}) collective-permute-start(bf16[896,128]{1,0:T(8,128)(2,1)} %get-tuple-element.32), channel_id=1, source_target_pairs={{0,1},{1,2},{2,3},{3,4},{4,5},{5,6},{6,7},{7,8},{8,9},{9,10},{10,1... | collective-permute-start | bytes 688136 | tf_op jit(solution)/shard_map/ppermute | solution.py:631
  56.7 8.0 %collective-permute-start.5 = (bf16[896,128]{1,0:T(8,128)(2,1)}, bf16[896,128]{1,0:T(8,128)(2,1)S(1)}, u32[]{:S(2)}, u32[]{:S(2)}) collective-permute-start(bf16[896,128]{1,0:T(8,128)(2,1)} %get-tuple-element.33), channel_id=1, source_target_pairs={{1,0},{2,1},{3,2},{4,3},{5,4},{6,5},{7,6},{8,7},{9,8},{10,9},{11,1... | collective-permute-start | bytes 688136 | tf_op jit(solution)/shard_map/ppermute | solution.py:632
  64.7 0.7 copy-start.2
  64.7 0.8 copy-start.4
  73.7 5.9 %collective-permute-start.6 = (f32[8,128]{1,0:T(8,128)}, f32[8,128]{1,0:T(8,128)S(1)}, u32[]{:S(2)}, u32[]{:S(2)}) collective-permute-start(f32[8,128]{1,0:T(8,128)} %get-tuple-element.37), channel_id=1, source_target_pairs={{0,1},{1,2},{2,3},{3,4},{4,5},{5,6},{6,7},{7,8},{8,9},{9,10},{10,1... | collective-permute-start | bytes 12296 | tf_op jit(solution)/shard_map/ppermute | solution.py:631
  73.8 5.9 %collective-permute-start.7 = (f32[8,128]{1,0:T(8,128)}, f32[8,128]{1,0:T(8,128)S(1)}, u32[]{:S(2)}, u32[]{:S(2)}) collective-permute-start(f32[8,128]{1,0:T(8,128)} %get-tuple-element.38), channel_id=1, source_target_pairs={{1,0},{2,1},{3,2},{4,3},{5,4},{6,5},{7,6},{8,7},{9,8},{10,9},{11,1... | collective-permute-start | bytes 12296 | tf_op jit(solution)/shard_map/ppermute | solution.py:632
  79.7 0.6 copy-start.6
  79.7 0.6 copy-start.7
  81.8 1.4 %collective-permute-start.8 = (f32[8,128]{1,0:T(8,128)}, f32[8,128]{1,0:T(8,128)S(1)}, u32[]{:S(2)}, u32[]{:S(2)}) collective-permute-start(f32[8,128]{1,0:T(8,128)} %get-tuple-element.40), channel_id=1, source_target_pairs={{0,1},{1,0},{2,3},{3,2},{4,5},{5,4},{6,7},{7,6},{8,9},{9,8},{10,11... | collective-permute-start | bytes 12296 | tf_op jit(solution)/shard_map/ppermute | solution.py:716
  83.9 3.6 %collective-permute-start.9 = (f32[8,128]{1,0:T(8,128)S(1)}, f32[8,128]{1,0:T(8,128)S(1)}, u32[]{:S(2)}, u32[]{:S(2)}) collective-permute-start(f32[8,128]{1,0:T(8,128)S(1)} %add.12), channel_id=1, source_target_pairs={{0,2},{1,3},{2,0},{3,1},{4,6},{5,7},{6,4},{7,5},{8,10},{9,11},{10,... | collective-permute-start | bytes 12296 | tf_op jit(solution)/shard_map/ppermute | solution.py:716
  87.5 3.6 %collective-permute-start.10 = (f32[8,128]{1,0:T(8,128)S(1)}, f32[8,128]{1,0:T(8,128)S(1)}, u32[]{:S(2)}, u32[]{:S(2)}) collective-permute-start(f32[8,128]{1,0:T(8,128)S(1)} %add.13), channel_id=1, source_target_pairs={{0,4},{1,5},{2,6},{3,7},{4,0},{5,1},{6,2},{7,3},{8,12},{9,13},{10,... | collective-permute-start | bytes 12296 | tf_op jit(solution)/shard_map/ppermute | solution.py:716
  91.1 4.5 %collective-permute-start.11 = (f32[8,128]{1,0:T(8,128)S(1)}, f32[8,128]{1,0:T(8,128)S(1)}, u32[]{:S(2)}, u32[]{:S(2)}) collective-permute-start(f32[8,128]{1,0:T(8,128)S(1)} %add.14), channel_id=1, source_target_pairs={{0,8},{1,9},{2,10},{3,11},{4,12},{5,13},{6,14},{7,15},{8,0},{9,1},... | collective-permute-start | bytes 12296 | tf_op jit(solution)/shard_map/ppermute | solution.py:716

commit v2 on v1

--- a/solution.py
+++ b/solution.py
@@ -30,7 +30,7 @@
 PACKED = PER_GROUP * C
 LAST = (NCOEF - (GROUPS - 1) * PER_GROUP) * C
 GROUP_ROWS = (PACKED,) * (GROUPS - 1) + (LAST,)
-VMEM_LIMIT = 56 * 1024 * 1024
+GRANTS = (28, 36, 14)
 
 F32 = jnp.float32
 BF16 = jnp.bfloat16
@@ -353,7 +353,7 @@
 
 
 def first_kernel(
-    feat_ref, low_ref, high_ref, frames_ref, nb_ref, counts_ref, pos_ref, shift_ref,
+    feat_ref, low_ref, high_ref, frames_ref, nb_ref, counts_ref, pos_ref, box_ref,
     weight_ref, radial_ref,
     hidden_ref, turned_ref, frame_out_ref, edge_ref, send_low_ref, send_high_ref,
     parts_ref, own_hot_ref, ghost_hot_ref, own_ref, ghost_ref, picked_ref, wide_ref,
@@ -375,7 +375,10 @@
     )
     found = dot(parts, own_hot_ref[...]) + dot(ghosts, ghost_hot_ref[GROUPS - 1])
     source = (found[0:8] + found[8:16]) + found[16:24]
-    shift = jnp.where(low_at >= 0, shift_ref[0], jnp.where(high_at >= 0, shift_ref[1], 0.0))
+    place = lax.axis_index("gx")
+    low_shift = jnp.where(place == 0, -box_ref[0], 0.0)
+    high_shift = jnp.where(place == lax.axis_size("gx") - 1, box_ref[0], 0.0)
+    shift = jnp.where(low_at >= 0, low_shift, jnp.where(high_at >= 0, high_shift, 0.0))
     first = iota((8, EDGES), 0) == 0
     parts_ref[pl.ds(0, 3), :] = pos_ref[...]
     target = jnp.concatenate([parts_ref[0:8, :]] * KNB, axis=1)
@@ -504,8 +507,8 @@
 
 def third_kernel(
     slope_ref, low_ref, high_ref, frame_ref, nb_ref, edge_ref, radial_ref, turned_ref,
-    second_slope_ref,
-    force_ref, ghost_low_ref, ghost_high_ref, virial_ref,
+    second_slope_ref, velocities_ref, masses_ref,
+    tile_ref,
     wide_ref, gate_slope_ref, hidden_slope_ref,
 ):
     spread_frames(frame_ref, wide_ref)
@@ -541,69 +544,139 @@
     slope = distance_slope(radial_ref, gate_slope_ref[...], distance) + second_slope_ref[0:1, :]
     vector = jnp.where(iota((8, EDGES), 0) < 3, edge_ref[...], 0.0)
     pull = vector * (slope / distance)
-    virial = -jnp.sum(jnp.sum(pull * vector, axis=0, keepdims=True), axis=1, keepdims=True)
-    virial_ref[...] = jnp.broadcast_to(virial, (8, OWN))
+    virial = -jnp.sum(pull * vector)
     high, middle, low = split_three(pull)
     parts = jnp.concatenate([high, middle, low, jnp.zeros((8, EDGES), F32)], axis=0).astype(BF16)
     own_at, low_at, high_at = edge_sources(nb_ref)
     spread_own = jnp.transpose(own_one_hot(own_at).astype(F32)).astype(BF16)
-    spread_ghost = jnp.transpose(ghost_one_hot(low_at, high_at, 0).astype(F32)).astype(BF16)
+    rim_at = jnp.where(low_at >= 0, low_at + (OWN - GHOST), high_at - OWN)
+    rim_at = jnp.where((low_at >= 0) | (high_at >= 0), rim_at, -1)
+    spread_rim = jnp.transpose(own_one_hot(rim_at).astype(F32)).astype(BF16)
     landed = dot(parts, spread_own)
     landed = landed[0:8] + landed[8:16] + landed[16:24]
     for slot in range(KNB):
         landed = landed - pull[:, slot * OWN : (slot + 1) * OWN]
-    force_ref[...] = -landed
-    landed = dot(parts, spread_ghost)
-    landed = landed[0:8] + landed[8:16] + landed[16:24]
-    ghost_low_ref[...] = -landed[:, :OWN]
-    ghost_high_ref[...] = -landed[:, OWN:]
-
-
-def kick_kernel(
-    force_ref, low_ref, high_ref, virial_ref, velocities_ref, masses_ref,
-    kicked_ref, strain_ref,
-):
+    outward = dot(parts, spread_rim)
+    outward = -(outward[0:8] + outward[8:16] + outward[16:24])
+    masses = masses_ref[...]
+    speed = jnp.concatenate([velocities_ref[...], jnp.zeros((5, OWN), F32)], axis=0)
+    per_mass = STEP_TIME / masses
+    kicked = speed - landed * per_mass
     lane = iota((8, OWN), 1)
-    force = force_ref[...] + jnp.where(lane < GHOST, low_ref[...], 0.0)
-    high = pltpu.roll(high_ref[...], OWN - GHOST, 1)
-    force = force + jnp.where(lane >= OWN - GHOST, high, 0.0)
-    masses = masses_ref[...]
-    kicked = velocities_ref[...] + STEP_TIME * force[0:3] / masses
-    kicked_ref[...] = kicked
-    total = jnp.sum(masses * jnp.sum(kicked * kicked, axis=0, keepdims=True))
-    strain_ref[...] = virial_ref[...] + total
-
-
-def finish_kernel(
-    strain_ref, kicked_ref, masses_ref, noise_ref, positions_ref, box_ref, control_ref,
-    fractional_ref, velocities_ref, new_box_ref,
-):
+    row = iota((8, OWN), 0)
+    inner = (row < 3) & (lane >= GHOST) & (lane < OWN - GHOST)
+    strain = virial + jnp.sum(jnp.where(inner, masses * kicked * kicked, 0.0))
+    tile = jnp.where(row < 3, kicked, jnp.where(row == 3, per_mass, pltpu.roll(outward, 4, 0)))
+    tile_ref[...] = jnp.where(row == 7, strain, tile)
+
+
+def join_tiles(left, right):
+    lane = iota((8, OWN), 1)
+    row = iota((8, OWN), 0)
+    top = lane >= OWN - GHOST
+    rims = top | (lane < GHOST)
+    near = jnp.where(top, left, right)
+    pushed = pltpu.roll(jnp.where(top, right, left), 4, 0)
+    per_mass = near[3:4]
+    kicked = near + per_mass * pushed
+    terms = jnp.where(rims & (row < 3), kicked * kicked * (STEP_TIME / per_mass), 0.0)
+    return jnp.sum(terms)
+
+
+def merge_runs(width, ways, tiles, caught):
+    place = lax.axis_index("gx")
+    lane = iota((8, OWN), 1)
+    row = iota((8, OWN), 0)
+    top = lane >= OWN - GHOST
+    bottom = lane < GHOST
+    digit = lax.rem(place // width, ways)
+    at_start = lax.rem(place, width) == 0
+    at_end = lax.rem(place, width) == width - 1
+    ordered = []
+    for run in range(ways):
+        chosen = tiles[0]
+        step = lax.rem(run - digit + ways, ways)
+        for far in range(1, ways):
+            chosen = jnp.where(step == far, tiles[far], chosen)
+        ordered.append(chosen)
+    merged = ordered[0]
+    for run in range(1, ways):
+        right = ordered[run]
+        caught = jnp.where(top & (at_end & (digit == run - 1)), right, caught)
+        caught = jnp.where(bottom & (at_start & (digit == run)), merged, caught)
+        strain = merged + right + join_tiles(merged, right)
+        outer = jnp.where(top == (row < 4), right, merged)
+        merged = jnp.where(row == 7, strain, outer)
+    return merged, caught
+
+
+def merge_kernel(width, ways, *refs):
+    ins, (tile_ref, caught_ref) = refs[:-2], refs[-2:]
+    tiles = [ref[...] for ref in ins[:ways]]
+    caught = ins[ways][...] if len(ins) > ways else jnp.zeros((8, OWN), F32)
+    tile_ref[...], caught_ref[...] = merge_runs(width, ways, tiles, caught)
+
+
+def finish_kernel(width, ways, first_round, *refs):
+    (
+        masses_ref, noise_ref, positions_ref, box_ref, control_ref,
+        fractional_ref, velocities_ref, new_box_ref,
+    ) = refs[-8:]
+    tiles = [ref[...] for ref in refs[:ways]]
+    start = tiles[0] if first_round else refs[ways][...]
+    caught = jnp.zeros((8, OWN), F32) if first_round else refs[ways + 1][...]
+    merged, caught = merge_runs(width, ways, tiles, caught)
+    place = lax.axis_index("gx")
+    lane = iota((8, OWN), 1)
+    caught = jnp.where((lane >= OWN - GHOST) & (place == width * ways - 1), merged, caught)
+    caught = jnp.where((lane < GHOST) & (place == 0), merged, caught)
+    strain = merged[7:8] + join_tiles(merged, merged)
+    kicked = (start + start[3:4] * pltpu.roll(caught, 4, 0))[0:3]
     row = iota((3, OWN), 0)
     box = jnp.where(row == 0, box_ref[0], jnp.where(row == 1, box_ref[1], box_ref[2]))
     volume = box_ref[0] * box_ref[1] * box_ref[2]
-    pressure = strain_ref[0:1, :] / (3.0 * volume)
+    pressure = strain / (3.0 * volume)
     rescale = jnp.exp(control_ref[1] * (pressure - control_ref[2]) / 3.0)
     kick = jnp.sqrt((1.0 - FRICTION * FRICTION) * control_ref[0] / masses_ref[...])
-    thermal = FRICTION * kicked_ref[...] + kick * noise_ref[...]
+    thermal = FRICTION * kicked + kick * noise_ref[...]
     fractional_ref[...] = (positions_ref[...] + STEP_TIME * thermal) / box
     velocities_ref[...] = thermal / rescale
-    new_box_ref[...] = box * rescale
-
-
-def call(kernel, outs, scratch, args, flops=0, scalars=(), moved=4 << 20):
-    specs = [
-        pl.BlockSpec(memory_space=pltpu.SMEM if at in scalars else pltpu.VMEM)
-        for at in range(len(args))
+    scale = rescale[0, 0]
+    for side in range(3):
+        new_box_ref[side] = box_ref[side] * scale
+
+
+SMALL = ("box", "control")
+
+
+def call(kernel, outs, scratch, args, grant, layers=()):
+    names = list(args)
+
+    def body(*refs):
+        views = list(refs)
+        for name, layer in dict(layers).items():
+            views[names.index(name)] = refs[names.index(name)].at[layer]
+        kernel(*views)
+
+    specs = []
+    for name in names:
+        if name in SMALL:
+            specs.append(pl.BlockSpec(memory_space=pltpu.SMEM))
+        else:
+            specs.append(pl.BlockSpec(memory_space=pltpu.VMEM))
+    out_specs = [
+        pl.BlockSpec(memory_space=pltpu.SMEM if len(shape) == 1 else pltpu.VMEM)
+        for shape, kind in outs
     ]
     return pl.pallas_call(
-        kernel,
+        body,
         out_shape=[jax.ShapeDtypeStruct(shape, kind) for shape, kind in outs],
         in_specs=specs,
-        out_specs=[pl.BlockSpec(memory_space=pltpu.VMEM) for _ in outs],
+        out_specs=out_specs,
         scratch_shapes=[pltpu.VMEM(shape, kind) for shape, kind in scratch],
-        compiler_params=pltpu.CompilerParams(vmem_limit_bytes=VMEM_LIMIT),
-        cost_estimate=pl.CostEstimate(flops=flops, bytes_accessed=moved, transcendentals=0),
-    )(*args)
+        compiler_params=pltpu.CompilerParams(vmem_limit_bytes=grant << 20),
+        cost_estimate=pl.CostEstimate(flops=0, bytes_accessed=1 << 20, transcendentals=0),
+    )(*args.values())
 
 
 def shards(
@@ -623,7 +696,6 @@
 ):
     assert positions.shape[1] == OWN
     count = lax.axis_size("gx")
-    place = lax.axis_index("gx")
     forward = [(i, (i + 1) % count) for i in range(count)]
     backward = [(target, source) for source, target in forward]
 
@@ -633,17 +705,15 @@
         return from_low, from_high
 
     packed = ((PACKED, OWN), BF16)
+    mass_row = masses[None, :]
     to_low, to_high = call(
-        pack_kernel, [packed, packed], [((32, OWN), F32)], (node_feat, positions)
+        pack_kernel,
+        [packed, packed],
+        [((32, OWN), F32)],
+        dict(feat=node_feat, positions=positions),
+        8,
     )
     from_low, from_high = exchange(to_low, to_high)
-    length = box_lengths[0]
-    shift = jnp.stack(
-        [
-            jnp.where(place == 0, -length, 0.0),
-            jnp.where(place == count - 1, length, 0.0),
-        ]
-    )
     gathers = [((OWN, EDGES), BF16), ((GROUPS, 2 * OWN, EDGES), BF16)]
     work = [
         ((ROWS, OWN), BF16),
@@ -667,11 +737,13 @@
             packed,
         ],
         [((32, OWN), F32)] + gathers + work,
-        (
-            node_feat, from_low, from_high, frames, neighbours, counts[None, :], positions,
-            shift, conv_weight[0], radial_weight[0],
+        dict(
+            feat=node_feat, low=from_low, high=from_high, frames=frames,
+            neighbours=neighbours, counts=counts[None, :], positions=positions,
+            box=box_lengths, weight=conv_weight, radial=radial_weight,
         ),
-        scalars=(7,),
+        GRANTS[0],
+        dict(weight=0, radial=0),
     )
     from_low, from_high = exchange(to_low, to_high)
     slope, second_slope, to_low, to_high = call(
@@ -687,44 +759,62 @@
             ((ROWS, EDGES), BF16),
             ((PACKED, 2 * OWN), F32),
         ],
-        (
-            hidden, from_low, from_high, frame, neighbours, edge, conv_weight[1],
-            radial_weight[1], readout,
+        dict(
+            hidden=hidden, low=from_low, high=from_high, frame=frame, neighbours=neighbours,
+            edge=edge, weight=conv_weight, radial=radial_weight, readout=readout,
         ),
+        GRANTS[1],
+        dict(weight=1, radial=1),
     )
     from_low, from_high = exchange(to_low, to_high)
     small = ((8, OWN), F32)
-    force, to_low, to_high, virial = call(
+    (tile,) = call(
         third_kernel,
-        [small] * 4,
+        [small],
         [((WROWS, 8, EDGES), F32), ((C, EDGES), F32), ((ROWS, OWN), F32)],
-        (
-            slope, from_low, from_high, frame, neighbours, edge, radial_weight[0], turned,
-            second_slope,
+        dict(
+            slope=slope, low=from_low, high=from_high, frame=frame, neighbours=neighbours,
+            edge=edge, radial=radial_weight, turned=turned, second_slope=second_slope,
+            velocities=velocities, masses=mass_row,
         ),
-    )
-    from_low, from_high = exchange(to_low, to_high)
-    kicked, strain = call(
-        kick_kernel,
-        [((3, OWN), F32), small],
+        GRANTS[2],
+        dict(radial=0),
+    )
+    own = tile
+    caught = None
+    width = 1
+    while True:
+        left = count // width
+        ways = next(way for way in (4, 2, 3, left) if left % way == 0)
+        tiles = {"tile0": tile}
+        for far in range(1, ways):
+            pairs = []
+            for target in range(count):
+                digit = target // width % ways
+                source = target + ((digit + far) % ways - digit) * width
+                pairs.append((source, target))
+            tiles["tile%d" % far] = lax.ppermute(tile, "gx", pairs)
+        if caught is not None:
+            tiles["caught"] = caught
+        if width * ways == count:
+            break
+        tile, caught = call(
+            functools.partial(merge_kernel, width, ways), [small, small], [], tiles, 1
+        )
+        width = width * ways
+    if caught is not None:
+        del tiles["caught"]
+        tiles.update(own=own, caught=caught)
+    return call(
+        functools.partial(finish_kernel, width, ways, caught is None),
+        [((3, OWN), F32), ((3, OWN), F32), ((3,), F32)],
         [],
-        (force, from_low, from_high, virial, velocities, masses[None, :]),
-    )
-    if count & (count - 1) == 0:
-        step = 1
-        while step < count:
-            strain = strain + lax.ppermute(strain, "gx", [(i, i ^ step) for i in range(count)])
-            step = 2 * step
-    else:
-        strain = lax.psum(strain, "gx")
-    fractional, new_velocities, new_box = call(
-        finish_kernel,
-        [((3, OWN), F32)] * 3,
-        [],
-        (strain, kicked, masses[None, :], thermal_noise, positions, box_lengths, control),
-        scalars=(5, 6),
-    )
-    return fractional, new_velocities, new_box[:, 0]
+        dict(
+            tiles, masses=mass_row, noise=thermal_noise, positions=positions,
+            box=box_lengths, control=control,
+        ),
+        1,
+    )
 
 
 def solution(mesh):

time: 99.3 us -> 82.7 us (0.83)
  Pallas kernels: 46.3 us -> 35.9 us
  waiting for transfers between devices: 21.1 us -> 15.7 us
  other arithmetic: 1.86 us -> 0 us
  starting transfers between devices: 20.3 us -> 21.5 us
  between operations: 1.98 us -> 0.94 us
    pallas_call x6, Pallas kernels: 46.3 us -> 35.9 us  [call(): pl.pallas_call(body, out_shape=[jax.ShapeDtypeStruct(shape, kind) for sha...]
    ppermute x4 -> x6, waiting for transfers between devices: 11.6 us -> 4.61 us  [shards(): tiles['tile%d' % far] = lax.ppermute(tile, 'gx', pairs)]
    ppermute x4 -> x3, starting transfers between devices: 17.1 us -> 11 us  [exchange(): from_high = lax.ppermute(to_low, 'gx', backward)]
    unnamed x16 -> x38, local copies, waits for them, and re-layouts: 2.94 us -> 8.27 us
    ppermute x4 -> x6, starting transfers between devices: 1.54 us -> 6.59 us  [shards(): tiles['tile%d' % far] = lax.ppermute(tile, 'gx', pairs)]
    squeeze x2 -> x0, local copies, waits for them, and re-layouts: 3.07 us -> none  [the longest x1 1.75 us: shards(): conv_weight[1]]
    ppermute x4 -> x3, starting transfers between devices: 1.69 us -> 3.93 us  [exchange(): from_low = lax.ppermute(to_high, 'gx', forward)]
    ppermute x4 -> x3, waiting for transfers between devices: 9.53 us -> 11.1 us  [exchange(): from_low = lax.ppermute(to_high, 'gx', forward)]
  transfers between devices with their start and end apart: 12 -> 12, of which waited for: 7 -> 7; matrix products, arithmetic and copies ran while one was open for 4% -> 0% of each run, Pallas kernels for 0% -> 0%
where the time goes in v2:
time: 82.7 us; the launch traced here: 82.3 us
  Pallas kernels  35.9 us (43%)
  starting transfers between devices  21.5 us (26%)
  waiting for transfers between devices  15.7 us (19%)
  local copies, waits for them, and re-layouts  8.27 us (10%)
  between operations  0.94 us (1%)
    pallas_call x6, Pallas kernels, call(): pl.pallas_call(body, out_shape=[jax.ShapeDtypeStruct(shape, kind) for sha...  35.9 us
    ppermute x3, waiting for transfers between devices, exchange(): from_low = lax.ppermute(to_high, 'gx', forward)  11.1 us
    ppermute x3, starting transfers between devices, exchange(): from_high = lax.ppermute(to_low, 'gx', backward)  11 us
    unnamed x38, local copies, waits for them, and re-layouts  8.27 us
    ppermute x6, starting transfers between devices, shards(): tiles['tile%d' % far] = lax.ppermute(tile, 'gx', pairs)  6.59 us
    ppermute x6, waiting for transfers between devices, shards(): tiles['tile%d' % far] = lax.ppermute(tile, 'gx', pairs)  4.61 us
    ppermute x3, starting transfers between devices, exchange(): from_low = lax.ppermute(to_high, 'gx', forward)  3.93 us
  transfers between devices with their start and end apart: 12, of which 7 were waited for; matrix products, arithmetic and copies ran while one was open for 0% of the time, Pallas kernels for 0%

profile of v2, /device:TPU:0, one launch (start us, length us, event | category | flops | bytes accessed | tf_op | source)
XLA Modules:
  0.0 82.3 jit_solution(1309506577321703950)
XLA Ops:
  0.6 1.1 %copy-done = bf16[3200,128]{1,0:T(8,128)(2,1)S(1)} copy-done((bf16[3200,128]{1,0:T(8,128)(2,1)S(1)}, bf16[3200,128]{1,0:T(8,128)(2,1)}, u32[]{:S(2)}) %copy-start) | copy-done | bytes 819224
  1.8 0.7 copy-done.8
  2.5 0.6 shard_map.148
  3.1 0.5 collective-permute-start
  3.6 5.1 %collective-permute-start.1 = (bf16[896,128]{1,0:T(8,128)(2,1)S(1)}, bf16[896,128]{1,0:T(8,128)(2,1)S(1)}, u32[]{:S(2)}, u32[]{:S(2)}) collective-permute-start(bf16[896,128]{1,0:T(8,128)(2,1)S(1)} %get-tuple-element.18), channel_id=1, source_target_pairs={{1,0},{2,1},{3,2},{4,3},{5,4},{6,5},{7,6},{8,7},{9,8},{10,9},{11,1... | collective-permute-start | bytes 688136 | tf_op jit(solution)/shard_map/ppermute | solution.py:704
  8.6 3.7 %collective-permute-done.refs_1_ = bf16[896,128]{1,0:T(8,128)(2,1)S(1)} collective-permute-done((bf16[896,128]{1,0:T(8,128)(2,1)S(1)}, bf16[896,128]{1,0:T(8,128)(2,1)S(1)}, u32[]{:S(2)}, u32[]{:S(2)}) %collective-permute-start) | collective-permute-done | bytes 229408 | tf_op jit(solution)/shard_map/ppermute | solution.py:703
  12.4 1.1 %copy-done.1 = bf16[3200,128]{1,0:T(8,128)(2,1)S(1)} copy-done((bf16[3200,128]{1,0:T(8,128)(2,1)S(1)}, bf16[3200,128]{1,0:T(8,128)(2,1)}, u32[]{:S(2)}) %copy-start.1) | copy-done | bytes 819224
  13.5 1.0 %copy-done.2 = bf16[2,5,128,128]{3,2,1,0:T(8,128)(2,1)S(1)} copy-done((bf16[2,5,128,128]{3,2,1,0:T(8,128)(2,1)S(1)}, bf16[2,5,128,128]{3,2,1,0:T(8,128)(2,1)}, u32[]{:S(2)}) %copy-start.2) | copy-done | bytes 327704
  14.5 0.7 copy-done.4
  15.2 0.9 %copy-done.5 = bf16[115,512]{1,0:T(8,128)(2,1)S(1)} copy-done((bf16[115,512]{1,0:T(8,128)(2,1)S(1)}, bf16[115,512]{1,0:T(8,128)(2,1)}, u32[]{:S(2)}) %copy-start.5) | copy-done | bytes 117784
  16.1 0.7 copy-done.6
  16.8 0.7 copy-done.9
  17.5 0.7 copy-done.13
  18.2 0.7 copy-done.17
  18.8 9.7 %shard_map.149 = (bf16[3200,128]{1,0:T(8,128)(2,1)S(1)}, bf16[2432,512]{1,0:T(8,128)(2,1)S(1)}, f32[115,512]{1,0:T(8,128)S(1)}, f32[8,512]{1,0:T(8,128)S(1)}, bf...) custom-call(bf16[3200,128]{1,0:T(8,128)(2,1)S(1)} %copy-done.1, ...), custom_call_target="tpu_custom_call" | custom-call | bytes 1048576 | tf_op jit(solution)/shard_map/pallas_call | solution.py:671
  28.5 1.8 %collective-permute-start.2 = (bf16[896,128]{1,0:T(8,128)(2,1)S(1)}, bf16[896,128]{1,0:T(8,128)(2,1)S(1)}, u32[]{:S(2)}, u32[]{:S(2)}) collective-permute-start(bf16[896,128]{1,0:T(8,128)(2,1)S(1)} %get-tuple-element.20), channel_id=1, source_target_pairs={{0,1},{1,2},{2,3},{3,4},{4,5},{5,6},{6,7},{7,8},{8,9},{9,10},{10,1... | collective-permute-start | bytes 688136 | tf_op jit(solution)/shard_map/ppermute | solution.py:703
  30.3 2.9 %collective-permute-start.3 = (bf16[896,128]{1,0:T(8,128)(2,1)S(1)}, bf16[896,128]{1,0:T(8,128)(2,1)S(1)}, u32[]{:S(2)}, u32[]{:S(2)}) collective-permute-start(bf16[896,128]{1,0:T(8,128)(2,1)S(1)} %get-tuple-element.21), channel_id=1, source_target_pairs={{1,0},{2,1},{3,2},{4,3},{5,4},{6,5},{7,6},{8,7},{9,8},{10,9},{11,1... | collective-permute-start | bytes 688136 | tf_op jit(solution)/shard_map/ppermute | solution.py:704
  33.2 3.6 %collective-permute-done.2.refs_1_ = bf16[896,128]{1,0:T(8,128)(2,1)S(1)} collective-permute-done((bf16[896,128]{1,0:T(8,128)(2,1)S(1)}, bf16[896,128]{1,0:T(8,128)(2,1)S(1)}, u32[]{:S(2)}, u32[]{:S(2)}) %collective-permute-start.2) | collective-permute-done | bytes 229408 | tf_op jit(solution)/shard_map/ppermute | solution.py:703
  36.9 18.2 %shard_map.150 = (f32[3200,128]{1,0:T(8,128)S(1)}, f32[8,512]{1,0:T(8,128)S(1)}, bf16[896,128]{1,0:T(8,128)(2,1)S(1)}, bf16[896,128]{1,0:T(8,128)(2,1)S(1)}) custom-call(bf16[3200,128]{1,0:T(8,128)(2,1)S(1)} %get-tuple-element.19.refs_0_, bf16[896,128]{1,0:T(8,128)(2,1)S(1)} %collective-permute-done.2.refs_1_, ...), custom_call_target="tpu_custom_call" | custom-call | bytes 1048576 | tf_op jit(solution)/shard_map/pallas_call | solution.py:671
  55.1 1.7 %collective-permute-start.4 = (bf16[896,128]{1,0:T(8,128)(2,1)S(1)}, bf16[896,128]{1,0:T(8,128)(2,1)S(1)}, u32[]{:S(2)}, u32[]{:S(2)}) collective-permute-start(bf16[896,128]{1,0:T(8,128)(2,1)S(1)} %get-tuple-element.25), channel_id=1, source_target_pairs={{0,1},{1,2},{2,3},{3,4},{4,5},{5,6},{6,7},{7,8},{8,9},{9,10},{10,1... | collective-permute-start | bytes 688136 | tf_op jit(solution)/shard_map/ppermute | solution.py:703
  56.8 3.0 %collective-permute-start.5 = (bf16[896,128]{1,0:T(8,128)(2,1)S(1)}, bf16[896,128]{1,0:T(8,128)(2,1)S(1)}, u32[]{:S(2)}, u32[]{:S(2)}) collective-permute-start(bf16[896,128]{1,0:T(8,128)(2,1)S(1)} %get-tuple-element.26), channel_id=1, source_target_pairs={{1,0},{2,1},{3,2},{4,3},{5,4},{6,5},{7,6},{8,7},{9,8},{10,9},{11,1... | collective-permute-start | bytes 688136 | tf_op jit(solution)/shard_map/ppermute | solution.py:704
  59.8 3.7 %collective-permute-done.4.refs_1_ = bf16[896,128]{1,0:T(8,128)(2,1)S(1)} collective-permute-done((bf16[896,128]{1,0:T(8,128)(2,1)S(1)}, bf16[896,128]{1,0:T(8,128)(2,1)S(1)}, u32[]{:S(2)}, u32[]{:S(2)}) %collective-permute-start.4) | collective-permute-done | bytes 229408 | tf_op jit(solution)/shard_map/ppermute | solution.py:703
  63.5 5.3 %shard_map.151.refs_0_.refs_4_ = f32[8,128]{1,0:T(8,128)S(1)} custom-call(f32[3200,128]{1,0:T(8,128)S(1)} %get-tuple-element.24.refs_0_, bf16[896,128]{1,0:T(8,128)(2,1)S(1)} %collective-permute-done.4.refs_1_, bf16[896,128]{1,0:T(8,128)(2,1)S(1)} %collective-permute-done.5.refs_2_, f32[115,512]{1,0:T(8,128)S(1)} %get-tuple-element.22.refs_3_, ...), custom_call_target="tpu_custom_call" | custom-call | bytes 1048576 | tf_op jit(solution)/shard_map/pallas_call | solution.py:671
  68.9 1.3 %collective-permute-start.8 = (f32[8,128]{1,0:T(8,128)S(1)}, f32[8,128]{1,0:T(8,128)S(1)}, u32[]{:S(2)}, u32[]{:S(2)}) collective-permute-start(f32[8,128]{1,0:T(8,128)S(1)} %shard_map.151.refs_0_.refs_4_), channel_id=1, source_target_pairs={{3,0},{0,1},{1,2},{2,3},{7,4},{4,5},{5,6},{6,7},{11,8},{8,9},{9,10... | collective-permute-start | bytes 12296 | tf_op jit(solution)/shard_map/ppermute | solution.py:796
  70.1 1.4 %collective-permute-start.6 = (f32[8,128]{1,0:T(8,128)S(1)}, f32[8,128]{1,0:T(8,128)S(1)}, u32[]{:S(2)}, u32[]{:S(2)}) collective-permute-start(f32[8,128]{1,0:T(8,128)S(1)} %shard_map.151.refs_0_.refs_4_), channel_id=1, source_target_pairs={{1,0},{2,1},{3,2},{0,3},{5,4},{6,5},{7,6},{4,7},{9,8},{10,9},{11,1... | collective-permute-start | bytes 12296 | tf_op jit(solution)/shard_map/ppermute | solution.py:796
  71.9 1.8 %collective-permute-done.7.refs_2_ = f32[8,128]{1,0:T(8,128)S(1)} collective-permute-done((f32[8,128]{1,0:T(8,128)S(1)}, f32[8,128]{1,0:T(8,128)S(1)}, u32[]{:S(2)}, u32[]{:S(2)}) %collective-permute-start.7) | collective-permute-done | bytes 4128 | tf_op jit(solution)/shard_map/ppermute | solution.py:796
  73.8 0.4 shard_map.152
  74.2 2.6 %collective-permute-start.10 = (f32[8,128]{1,0:T(8,128)S(1)}, f32[8,128]{1,0:T(8,128)S(1)}, u32[]{:S(2)}, u32[]{:S(2)}) collective-permute-start(f32[8,128]{1,0:T(8,128)S(1)} %get-tuple-element.29.refs_0_), channel_id=1, source_target_pairs={{8,0},{9,1},{10,2},{11,3},{12,4},{13,5},{14,6},{15,7},{0,8},{1,9},... | collective-permute-start | bytes 12296 | tf_op jit(solution)/shard_map/ppermute | solution.py:796
  76.9 1.2 %collective-permute-start.9 = (f32[8,128]{1,0:T(8,128)S(1)}, f32[8,128]{1,0:T(8,128)S(1)}, u32[]{:S(2)}, u32[]{:S(2)}) collective-permute-start(f32[8,128]{1,0:T(8,128)S(1)} %get-tuple-element.29.refs_0_), channel_id=1, source_target_pairs={{4,0},{5,1},{6,2},{7,3},{8,4},{9,5},{10,6},{11,7},{12,8},{13,9},{1... | collective-permute-start | bytes 12296 | tf_op jit(solution)/shard_map/ppermute | solution.py:796
  78.0 1.6 %collective-permute-done.11.refs_3_ = f32[8,128]{1,0:T(8,128)S(1)} collective-permute-done((f32[8,128]{1,0:T(8,128)S(1)}, f32[8,128]{1,0:T(8,128)S(1)}, u32[]{:S(2)}, u32[]{:S(2)}) %collective-permute-start.11) | collective-permute-done | bytes 4128 | tf_op jit(solution)/shard_map/ppermute | solution.py:796
  79.6 0.8 %collective-permute-done.9.refs_1_ = f32[8,128]{1,0:T(8,128)S(1)} collective-permute-done((f32[8,128]{1,0:T(8,128)S(1)}, f32[8,128]{1,0:T(8,128)S(1)}, u32[]{:S(2)}, u32[]{:S(2)}) %collective-permute-start.9) | collective-permute-done | bytes 4128 | tf_op jit(solution)/shard_map/ppermute | solution.py:796
  80.5 1.7 %shard_map.153 = (f32[3,128]{1,0:T(4,128)}, f32[3,128]{1,0:T(4,128)}, f32[3]{0:T(128)}) custom-call(f32[8,128]{1,0:T(8,128)S(1)} %get-tuple-element.29.refs_0_, f32[8,128]{1,0:T(8,128)S(1)} %collective-permute-done.9.refs_1_, f32[8,128]{1,0:T(8,128)S(1)} %collective-permute-done.10.refs_2_, f32[8,128]{1,0:T(8,128)S(1)} %collective-permute-done.11.refs_3_, ...), custom_call_target="tpu_custom_call" | custom-call | bytes 1048576 | tf_op jit(solution)/shard_map/pallas_call | solution.py:671
  (36 shorter events, 0.5 us)
Async XLA Ops:
  0.6 1.1 %copy-start = (bf16[3200,128]{1,0:T(8,128)(2,1)S(1)}, bf16[3200,128]{1,0:T(8,128)(2,1)}, u32[]{:S(2)}) copy-start(bf16[3200,128]{1,0:T(8,128)(2,1)} %refs_0_.3) | copy-start | bytes 2457604
  1.8 0.7 copy-start.8
  2.5 34.4 %copy-start.3 = (bf16[2,5,128,128]{3,2,1,0:T(8,128)(2,1)S(1)}, bf16[2,5,128,128]{3,2,1,0:T(8,128)(2,1)}, u32[]{:S(2)}) copy-start(bf16[2,5,128,128]{3,2,1,0:T(8,128)(2,1)} %refs_6_.4) | copy-start | bytes 983044
  2.5 34.4 %copy-start.7 = (s32[4,128]{1,0:T(4,128)S(1)}, s32[4,128]{1,0:T(4,128)}, u32[]{:S(2)}) copy-start(s32[4,128]{1,0:T(4,128)} %refs_4_.5) | copy-start | bytes 6148
  2.5 34.4 %copy-start.11 = (f32[5,128]{1,0:T(8,128)S(1)}, f32[5,128]{1,0:T(8,128)}, u32[]{:S(2)}) copy-start(f32[5,128]{1,0:T(8,128)} %refs_8_.4) | copy-start | bytes 7684
  2.5 61.0 %copy-start.12 = (f32[3,128]{1,0:T(4,128)S(1)}, f32[3,128]{1,0:T(4,128)}, u32[]{:S(2)}) copy-start(f32[3,128]{1,0:T(4,128)} %refs_9_.4) | copy-start | bytes 4612
  2.5 61.0 %copy-start.15 = (f32[128]{0:T(128)S(1)}, f32[128]{0:T(128)}, u32[]{:S(2)}) copy-start(f32[128]{0:T(128)} %param.19) | copy-start | bytes 1540
  3.1 9.3 %collective-permute-start = (bf16[896,128]{1,0:T(8,128)(2,1)S(1)}, bf16[896,128]{1,0:T(8,128)(2,1)S(1)}, u32[]{:S(2)}, u32[]{:S(2)}) collective-permute-start(bf16[896,128]{1,0:T(8,128)(2,1)S(1)} %get-tuple-element.17), channel_id=1, source_target_pairs={{0,1},{1,2},{2,3},{3,4},{4,5},{5,6},{6,7},{7,8},{8,9},{9,10},{10,1... | collective-permute-start | bytes 688136 | tf_op jit(solution)/shard_map/ppermute | solution.py:703
  3.6 8.8 %collective-permute-start.1 = (bf16[896,128]{1,0:T(8,128)(2,1)S(1)}, bf16[896,128]{1,0:T(8,128)(2,1)S(1)}, u32[]{:S(2)}, u32[]{:S(2)}) collective-permute-start(bf16[896,128]{1,0:T(8,128)(2,1)S(1)} %get-tuple-element.18), channel_id=1, source_target_pairs={{1,0},{2,1},{3,2},{4,3},{5,4},{6,5},{7,6},{8,7},{9,8},{10,9},{11,1... | collective-permute-start | bytes 688136 | tf_op jit(solution)/shard_map/ppermute | solution.py:704
  12.4 1.1 %copy-start.1 = (bf16[3200,128]{1,0:T(8,128)(2,1)S(1)}, bf16[3200,128]{1,0:T(8,128)(2,1)}, u32[]{:S(2)}) copy-start(bf16[3200,128]{1,0:T(8,128)(2,1)} %refs_0_.3) | copy-start | bytes 2457604
  13.5 1.0 %copy-start.2 = (bf16[2,5,128,128]{3,2,1,0:T(8,128)(2,1)S(1)}, bf16[2,5,128,128]{3,2,1,0:T(8,128)(2,1)}, u32[]{:S(2)}) copy-start(bf16[2,5,128,128]{3,2,1,0:T(8,128)(2,1)} %refs_6_.4) | copy-start | bytes 983044
  14.5 0.7 copy-start.4
  15.2 0.9 %copy-start.5 = (bf16[115,512]{1,0:T(8,128)(2,1)S(1)}, bf16[115,512]{1,0:T(8,128)(2,1)}, u32[]{:S(2)}) copy-start(bf16[115,512]{1,0:T(8,128)(2,1)} %refs_3_.1) | copy-start | bytes 353284
  16.1 0.7 copy-start.6
  16.8 0.7 copy-start.9
  17.5 0.7 copy-start.13
  18.1 0.7 copy-start.17
  28.5 8.3 %collective-permute-start.2 = (bf16[896,128]{1,0:T(8,128)(2,1)S(1)}, bf16[896,128]{1,0:T(8,128)(2,1)S(1)}, u32[]{:S(2)}, u32[]{:S(2)}) collective-permute-start(bf16[896,128]{1,0:T(8,128)(2,1)S(1)} %get-tuple-element.20), channel_id=1, source_target_pairs={{0,1},{1,2},{2,3},{3,4},{4,5},{5,6},{6,7},{7,8},{8,9},{9,10},{10,1... | collective-permute-start | bytes 688136 | tf_op jit(solution)/shard_map/ppermute | solution.py:703
  30.3 6.5 %collective-permute-start.3 = (bf16[896,128]{1,0:T(8,128)(2,1)S(1)}, bf16[896,128]{1,0:T(8,128)(2,1)S(1)}, u32[]{:S(2)}, u32[]{:S(2)}) collective-permute-start(bf16[896,128]{1,0:T(8,128)(2,1)S(1)} %get-tuple-element.21), channel_id=1, source_target_pairs={{1,0},{2,1},{3,2},{4,3},{5,4},{6,5},{7,6},{8,7},{9,8},{10,9},{11,1... | collective-permute-start | bytes 688136 | tf_op jit(solution)/shard_map/ppermute | solution.py:704
  55.1 25.4 %copy-start.10 = (f32[3,128]{1,0:T(4,128)S(1)}, f32[3,128]{1,0:T(4,128)}, u32[]{:S(2)}) copy-start(f32[3,128]{1,0:T(4,128)} %refs_8_.5) | copy-start | bytes 4612
  55.1 25.4 %copy-start.14 = (f32[3]{0:T(128)S(1)}, f32[3]{0:T(128)}, u32[]{:S(2)}) copy-start(f32[3]{0:T(128)} %refs_9_.5) | copy-start | bytes 40
  55.1 25.4 %copy-start.16 = (f32[3,128]{1,0:T(4,128)S(1)}, f32[3,128]{1,0:T(4,128)}, u32[]{:S(2)}) copy-start(f32[3,128]{1,0:T(4,128)} %refs_7_.5) | copy-start | bytes 4612
  55.1 25.4 %copy-start.18 = (f32[3]{0:T(128)S(1)}, f32[3]{0:T(128)}, u32[]{:S(2)}) copy-start(f32[3]{0:T(128)} %refs_10_.1) | copy-start | bytes 40
  55.1 8.4 %collective-permute-start.4 = (bf16[896,128]{1,0:T(8,128)(2,1)S(1)}, bf16[896,128]{1,0:T(8,128)(2,1)S(1)}, u32[]{:S(2)}, u32[]{:S(2)}) collective-permute-start(bf16[896,128]{1,0:T(8,128)(2,1)S(1)} %get-tuple-element.25), channel_id=1, source_target_pairs={{0,1},{1,2},{2,3},{3,4},{4,5},{5,6},{6,7},{7,8},{8,9},{9,10},{10,1... | collective-permute-start | bytes 688136 | tf_op jit(solution)/shard_map/ppermute | solution.py:703
  56.8 6.7 %collective-permute-start.5 = (bf16[896,128]{1,0:T(8,128)(2,1)S(1)}, bf16[896,128]{1,0:T(8,128)(2,1)S(1)}, u32[]{:S(2)}, u32[]{:S(2)}) collective-permute-start(bf16[896,128]{1,0:T(8,128)(2,1)S(1)} %get-tuple-element.26), channel_id=1, source_target_pairs={{1,0},{2,1},{3,2},{4,3},{5,4},{6,5},{7,6},{8,7},{9,8},{10,9},{11,1... | collective-permute-start | bytes 688136 | tf_op jit(solution)/shard_map/ppermute | solution.py:704
  68.9 3.1 %collective-permute-start.8 = (f32[8,128]{1,0:T(8,128)S(1)}, f32[8,128]{1,0:T(8,128)S(1)}, u32[]{:S(2)}, u32[]{:S(2)}) collective-permute-start(f32[8,128]{1,0:T(8,128)S(1)} %shard_map.151.refs_0_.refs_4_), channel_id=1, source_target_pairs={{3,0},{0,1},{1,2},{2,3},{7,4},{4,5},{5,6},{6,7},{11,8},{8,9},{9,10... | collective-permute-start | bytes 12296 | tf_op jit(solution)/shard_map/ppermute | solution.py:796
  70.1 3.6 %collective-permute-start.7 = (f32[8,128]{1,0:T(8,128)S(1)}, f32[8,128]{1,0:T(8,128)S(1)}, u32[]{:S(2)}, u32[]{:S(2)}) collective-permute-start(f32[8,128]{1,0:T(8,128)S(1)} %shard_map.151.refs_0_.refs_4_), channel_id=1, source_target_pairs={{2,0},{3,1},{0,2},{1,3},{6,4},{7,5},{4,6},{5,7},{10,8},{11,9},{8,1... | collective-permute-start | bytes 12296 | tf_op jit(solution)/shard_map/ppermute | solution.py:796
  70.1 3.6 %collective-permute-start.6 = (f32[8,128]{1,0:T(8,128)S(1)}, f32[8,128]{1,0:T(8,128)S(1)}, u32[]{:S(2)}, u32[]{:S(2)}) collective-permute-start(f32[8,128]{1,0:T(8,128)S(1)} %shard_map.151.refs_0_.refs_4_), channel_id=1, source_target_pairs={{1,0},{2,1},{3,2},{0,3},{5,4},{6,5},{7,6},{4,7},{9,8},{10,9},{11,1... | collective-permute-start | bytes 12296 | tf_op jit(solution)/shard_map/ppermute | solution.py:796
  74.2 5.5 %collective-permute-start.11 = (f32[8,128]{1,0:T(8,128)S(1)}, f32[8,128]{1,0:T(8,128)S(1)}, u32[]{:S(2)}, u32[]{:S(2)}) collective-permute-start(f32[8,128]{1,0:T(8,128)S(1)} %get-tuple-element.29.refs_0_), channel_id=1, source_target_pairs={{12,0},{13,1},{14,2},{15,3},{0,4},{1,5},{2,6},{3,7},{4,8},{5,9},{6... | collective-permute-start | bytes 12296 | tf_op jit(solution)/shard_map/ppermute | solution.py:796
  74.2 5.4 %collective-permute-start.10 = (f32[8,128]{1,0:T(8,128)S(1)}, f32[8,128]{1,0:T(8,128)S(1)}, u32[]{:S(2)}, u32[]{:S(2)}) collective-permute-start(f32[8,128]{1,0:T(8,128)S(1)} %get-tuple-element.29.refs_0_), channel_id=1, source_target_pairs={{8,0},{9,1},{10,2},{11,3},{12,4},{13,5},{14,6},{15,7},{0,8},{1,9},... | collective-permute-start | bytes 12296 | tf_op jit(solution)/shard_map/ppermute | solution.py:796
  76.9 3.6 %collective-permute-start.9 = (f32[8,128]{1,0:T(8,128)S(1)}, f32[8,128]{1,0:T(8,128)S(1)}, u32[]{:S(2)}, u32[]{:S(2)}) collective-permute-start(f32[8,128]{1,0:T(8,128)S(1)} %get-tuple-element.29.refs_0_), channel_id=1, source_target_pairs={{4,0},{5,1},{6,2},{7,3},{8,4},{9,5},{10,6},{11,7},{12,8},{13,9},{1... | collective-permute-start | bytes 12296 | tf_op jit(solution)/shard_map/ppermute | solution.py:796

commit v3 on v2

--- a/solution.py
+++ b/solution.py
@@ -17,7 +17,8 @@
 OWN = 128
 ROWS = NCOEF * C
 WROWS = 115
-EDGES = KNB * OWN
+TILES = KNB // 2
+EDGES = TILES * OWN
 
 EPSILON = 1e-06
 SOFTENING = 0.25
@@ -30,7 +31,7 @@
 PACKED = PER_GROUP * C
 LAST = (NCOEF - (GROUPS - 1) * PER_GROUP) * C
 GROUP_ROWS = (PACKED,) * (GROUPS - 1) + (LAST,)
-GRANTS = (28, 36, 14)
+GRANT = 18
 
 F32 = jnp.float32
 BF16 = jnp.bfloat16
@@ -118,18 +119,65 @@
     return parts_ref[...].astype(BF16)
 
 
-def pack_kernel(feat_ref, pos_ref, low_ref, high_ref, parts_ref):
+def fetch(pairs, sems):
+    copies = [
+        pltpu.make_async_copy(source, target, sems.at[at])
+        for at, (source, target) in enumerate(pairs)
+    ]
+    for copy in copies:
+        copy.start()
+    for copy in copies:
+        copy.wait()
+
+
+def pack_kernel(feat_hbm, pos_hbm, low_ref, high_ref, feat_ref, pos_ref, parts_ref, sems):
+    fetch([(feat_hbm, feat_ref), (pos_hbm, pos_ref)], sems)
     parts = position_parts(pos_ref, parts_ref)
     pack_rims(lambda start, size: feat_ref[pl.ds(start, size), :], low_ref, high_ref, parts)
 
 
-def edge_sources(nb_ref):
+INNER = 0
+RIM = 1
+
+
+def inside(shape, half):
+    lane = iota(shape, 1)
+    middle = (lane >= GHOST) & (lane < OWN - GHOST)
+    return middle if half == INNER else jnp.logical_not(middle)
+
+
+def pick(even, odd, half):
+    return jnp.where(inside(even.shape, half), even, pltpu.roll(odd, OWN // 2, 1))
+
+
+def both_lanes(values, half):
+    return pick(values, values, half)
+
+
+def fold_slots(values):
+    return values + pltpu.roll(values, OWN // 2, 1)
+
+
+def slot_rows(ref, half):
+    tiles = []
+    for tile in range(TILES):
+        even = jnp.broadcast_to(ref[2 * tile : 2 * tile + 1, :], (8, OWN))
+        odd = jnp.broadcast_to(ref[2 * tile + 1 : 2 * tile + 2, :], (8, OWN))
+        tiles.append(pick(even, odd, half)[:1])
+    return tiles
+
+
+def edge_atoms(half):
+    return both_lanes(iota((8, OWN), 1), half)[:1]
+
+
+def edge_sources(nb_ref, half):
     own_at = []
     low_at = []
     high_at = []
-    for slot in range(KNB):
-        place = jnp.bitwise_and(nb_ref[slot : slot + 1, :], OWN - 1)
-        gap = place - iota((1, OWN), 1)
+    for rows in slot_rows(nb_ref, half):
+        place = jnp.bitwise_and(rows, OWN - 1)
+        gap = place - edge_atoms(half)
         low = gap > OWN // 2
         high = gap < -(OWN // 2)
         own_at.append(jnp.where(low | high, -1, place))
@@ -149,12 +197,23 @@
     return one_hot(iota((2 * OWN, EDGES), 0) == at)
 
 
-def build_gathers(nb_ref, own_ref, ghost_ref):
-    own_at, low_at, high_at = edge_sources(nb_ref)
-    own_ref[...] = own_one_hot(own_at)
-    for group in range(GROUPS):
-        ghost_ref[group] = ghost_one_hot(low_at, high_at, group)
-    return own_at, low_at, high_at
+def half_frames(frames_ref, counts, half, wide_ref):
+    total = KNB * OWN
+    column = iota((total, EDGES), 1)
+    lane = jnp.bitwise_and(column, OWN - 1)
+    middle = (lane >= GHOST) & (lane < OWN - GHOST)
+    held = middle if half == INNER else jnp.logical_not(middle)
+    atom = jnp.where(held, lane, jnp.bitwise_and(lane + OWN // 2, OWN - 1))
+    slot = 2 * (column // OWN) + jnp.where(held, 0, 1)
+    moved = dot(frames_ref[...], one_hot(iota((total, EDGES), 0) == atom * KNB + slot))
+    counts = both_lanes(jnp.broadcast_to(counts, (8, OWN)), half)[:1]
+    odd = jnp.where(inside((1, OWN), half), 0, 1)
+    live = jnp.concatenate(
+        [jnp.where(2 * tile + odd < counts, 1.0, 0.0) for tile in range(TILES)], axis=1
+    )
+    moved = moved * live
+    for entry in range(WROWS):
+        wide_ref[entry] = jnp.broadcast_to(moved[entry : entry + 1, :], (8, EDGES))
 
 
 def corner_mask(block):
@@ -187,42 +246,42 @@
     return jnp.concatenate(sides, axis=1)[:1]
 
 
-def normalise(feat_ref, low_ref, high_ref, own_ref, ghost_ref):
+def normalise_own(feat_ref, own_ref):
     squares = jnp.zeros((8, OWN), F32)
     for coef in range(NCOEF):
         block = feat_ref[pl.ds(coef * C, C), :].astype(F32)
         squares = squares + fold_rows(block * block)
     mean = jnp.sum(squares, axis=0, keepdims=True) * (1.0 / ROWS)
-    own_scale = lax.rsqrt(mean + EPSILON)
+    scale = lax.rsqrt(mean + EPSILON)
     for coef in range(NCOEF):
         rows = pl.ds(coef * C, C)
-        own_ref[rows, :] = (feat_ref[rows, :].astype(F32) * own_scale).astype(BF16)
+        own_ref[rows, :] = (feat_ref[rows, :].astype(F32) * scale).astype(BF16)
+    return scale
+
+
+def normalise_ghosts(low_ref, high_ref, ghost_ref):
     squares = jnp.zeros((8, 2 * OWN), F32)
     for block in range(PER_GROUP):
         values = read_ghosts(low_ref, high_ref, block)
         squares = squares + fold_rows(values * values)
-    ghost_scale = lax.rsqrt(over_groups(squares) * (1.0 / ROWS) + EPSILON)
+    scale = lax.rsqrt(over_groups(squares) * (1.0 / ROWS) + EPSILON)
     for block in range(PER_GROUP):
-        values = read_ghosts(low_ref, high_ref, block) * ghost_scale
+        values = read_ghosts(low_ref, high_ref, block) * scale
         ghost_ref[pl.ds(block * C, C), :] = values.astype(BF16)
-    return own_scale, ghost_scale
-
-
-def gather(own_ref, ghost_ref, own_hot_ref, ghost_hot_ref, out_ref):
+    return scale
+
+
+def gather(own_ref, own_hot_ref, out_ref, ghost_ref=None, ghost_hot_ref=None):
     for group, rows in enumerate(GROUP_ROWS):
         start = group * PACKED
-        out_ref[pl.ds(start, rows), :] = dot(
-            own_ref[pl.ds(start, rows), :], own_hot_ref[...]
-        ) + dot(ghost_ref[pl.ds(0, rows), :], ghost_hot_ref[group])
+        found = dot(own_ref[pl.ds(start, rows), :], own_hot_ref[...])
+        if ghost_ref is not None:
+            found = found + dot(ghost_ref[pl.ds(0, rows), :], ghost_hot_ref[group])
+        out_ref[pl.ds(start, rows), :] = found
 
 
 def twice(values):
     return jnp.concatenate([values, values], axis=0)
-
-
-def spread_frames(frame_ref, wide_ref):
-    for entry in range(WROWS):
-        wide_ref[entry] = jnp.broadcast_to(frame_ref[entry : entry + 1, :], (8, EDGES))
 
 
 def slot_lanes(slot):
@@ -233,7 +292,7 @@
     @pl.loop(0, C // 16)
     def _(step):
         start = pl.multiple_of(step * 16, 16)
-        for slot in range(KNB):
+        for slot in range(TILES):
             lanes = slot_lanes(slot)
             for degree, row_count, offset in LAYOUT:
                 size = 2 * degree + 1
@@ -254,7 +313,7 @@
     @pl.loop(0, C // 16)
     def _(step):
         start = pl.multiple_of(step * 16, 16)
-        for slot in range(KNB):
+        for slot in range(TILES):
             lanes = slot_lanes(slot)
             for degree, row_count, offset in LAYOUT:
                 size = 2 * degree + 1
@@ -271,9 +330,9 @@
                     out_ref[pl.ds(at + start, 16), lanes] = total.astype(BF16)
 
 
-def build_weights(weight_ref, zero_ref, pair_ref):
+def build_weights(weight_ref, layer, zero_ref, pair_ref):
     turned = [
-        jnp.transpose(weight_ref[part].astype(F32)).astype(BF16) for part in range(2 * MMAX + 1)
+        jnp.transpose(weight_ref[layer, part].astype(F32)).astype(BF16) for part in range(2 * MMAX + 1)
     ]
     zero_ref[...] = turned[0]
     for order in range(1, MMAX + 1):
@@ -284,10 +343,10 @@
         pair_ref[order - 1, C:, C:] = real
 
 
-def build_back_weights(weight_ref, zero_ref, pair_ref):
-    zero_ref[...] = weight_ref[0]
+def build_back_weights(weight_ref, layer, zero_ref, pair_ref):
+    zero_ref[...] = weight_ref[layer, 0]
     for order in range(1, MMAX + 1):
-        real, imag = weight_ref[2 * order - 1], weight_ref[2 * order]
+        real, imag = weight_ref[layer, 2 * order - 1], weight_ref[layer, 2 * order]
         pair_ref[order - 1, :C, :C] = real
         pair_ref[order - 1, :C, C:] = imag
         pair_ref[order - 1, C:, :C] = -imag
@@ -332,7 +391,7 @@
 def message_rows(degree, row_count, offset, start, turned_ref, gate_ref, wide_ref):
     size = 2 * degree + 1
     sums = [None] * size
-    for slot in range(KNB):
+    for slot in range(TILES):
         lanes = slot_lanes(slot)
         gate = gate_ref[pl.ds(start, 16), lanes]
         for row in range(row_count):
@@ -340,7 +399,7 @@
             for k in range(size):
                 term = twice(wide_ref[offset + row * size + k, :, lanes]) * gated
                 sums[k] = term if sums[k] is None else sums[k] + term
-    return sums
+    return [fold_slots(total) for total in sums]
 
 
 def slope_rows(degree, row_count, offset, row, lanes, slopes, wide_ref):
@@ -352,101 +411,139 @@
     return total
 
 
-def first_kernel(
-    feat_ref, low_ref, high_ref, frames_ref, nb_ref, counts_ref, pos_ref, box_ref,
-    weight_ref, radial_ref,
-    hidden_ref, turned_ref, frame_out_ref, edge_ref, send_low_ref, send_high_ref,
-    parts_ref, own_hot_ref, ghost_hot_ref, own_ref, ghost_ref, picked_ref, wide_ref,
-    rows_ref, turned_f32_ref, gate_ref, zero_ref, pair_ref,
+def layer_forward(picked_ref, wide_ref, rows_ref, zero_ref, pair_ref, turned_ref):
+    to_frame(picked_ref, wide_ref, rows_ref)
+    convolve(rows_ref, zero_ref, pair_ref, turned_ref)
+
+
+def add_messages(base_ref, half, turned_ref, gate_ref, wide_ref, hidden_ref, keep_ref):
+    @pl.loop(0, C // 16)
+    def _(step):
+        start = pl.multiple_of(step * 16, 16)
+        held = inside((16, OWN), half)
+        for degree, row_count, offset in LAYOUT:
+            sums = message_rows(degree, row_count, offset, start, turned_ref, gate_ref, wide_ref)
+            for k, total in enumerate(sums):
+                rows = pl.ds((degree * degree + k) * C + start, 16)
+                added = jnp.where(held, total * KNB ** (-0.5), 0.0)
+                hidden_ref[rows, :] = (base_ref[rows, :].astype(F32) + added).astype(BF16)
+        for row in range(EDGE_ROWS):
+            rows = pl.ds(row * C + start, 16)
+            keep_ref[rows, :] = turned_ref[rows, :].astype(BF16)
+
+
+def edge_geometry(source, shift, target, edge_ref):
+    first = iota((8, EDGES), 0) == 0
+    if shift is not None:
+        source = source + jnp.where(first, shift, 0.0)
+    vector = source - target
+    distance = jnp.sqrt(jnp.sum(vector * vector, axis=0, keepdims=True) + SOFTENING)
+    edge_ref[...] = jnp.where(iota((8, EDGES), 0) == 3, distance, vector)
+    return distance
+
+
+def join_parts(found):
+    return (found[0:8] + found[8:16]) + found[16:24]
+
+
+def first_inner_kernel(
+    feat_hbm, frames_hbm, nb_hbm, counts_hbm, pos_hbm, box_hbm, weight_hbm, radial_hbm,
+    readout_hbm,
+    hidden_ref, keep_ref, edge_ref, own_ref, inner_wide_ref, rim_wide_ref, inner_hot_ref,
+    rim_hot_ref, ghost_hot_ref, index_ref, target_ref, parts_out_ref, zero_ref, pair_ref,
+    radial_ref, readout_wide_ref,
+    feat_ref, frames_ref, nb_ref, counts_ref, pos_ref, box_ref, weight_ref, readout_ref,
+    parts_ref, picked_ref, rows_ref, turned_ref, gate_ref, sems,
 ):
-    column = iota((EDGES, EDGES), 1)
-    wanted = jnp.bitwise_and(column, OWN - 1) * KNB + column // OWN
-    moved = dot(frames_ref[...], one_hot(iota((EDGES, EDGES), 0) == wanted))
+    fetch(
+        [
+            (nb_hbm, nb_ref), (counts_hbm, counts_ref), (pos_hbm, pos_ref),
+            (box_hbm, box_ref), (frames_hbm, frames_ref), (radial_hbm, radial_ref),
+            (feat_hbm, feat_ref), (weight_hbm, weight_ref), (readout_hbm, readout_ref),
+        ],
+        sems,
+    )
     counts = counts_ref[...]
-    live = jnp.concatenate(
-        [jnp.where(slot < counts, 1.0, 0.0) for slot in range(KNB)], axis=1
-    )
-    frame_out_ref[...] = moved * live
-    spread_frames(frame_out_ref, wide_ref)
-    own_at, low_at, high_at = build_gathers(nb_ref, own_hot_ref, ghost_hot_ref)
+    half_frames(frames_ref, counts, INNER, inner_wide_ref)
+    own_at, low_at, high_at = edge_sources(nb_ref, INNER)
+    index_ref[...] = jnp.full((8, 2 * EDGES), -1, jnp.int32)
+    index_ref[0:1, :EDGES] = own_at
+    inner_hot_ref[...] = own_one_hot(own_at)
     parts = position_parts(pos_ref, parts_ref)
-    ghosts = jnp.concatenate(
-        [low_ref[pl.ds(LAST, 32), :], high_ref[pl.ds(LAST, 32), :]], axis=1
-    )
-    found = dot(parts, own_hot_ref[...]) + dot(ghosts, ghost_hot_ref[GROUPS - 1])
-    source = (found[0:8] + found[8:16]) + found[16:24]
+    parts_out_ref[...] = parts
+    parts_ref[pl.ds(0, 3), :] = pos_ref[...]
+    positions = parts_ref[0:8, :]
+    target = jnp.concatenate([both_lanes(positions, INNER)] * TILES, axis=1)
+    distance = edge_geometry(join_parts(dot(parts, inner_hot_ref[...])), None, target, edge_ref)
+    gate_ref[...] = edge_gate(radial_ref.at[0], radial(distance)[0])
+    build_weights(weight_ref, 0, zero_ref.at[0], pair_ref.at[0])
+    normalise_own(feat_ref, own_ref)
+    gather(own_ref, inner_hot_ref, picked_ref)
+    layer_forward(
+        picked_ref, inner_wide_ref, rows_ref, zero_ref.at[0], pair_ref.at[0], turned_ref
+    )
+    add_messages(feat_ref, INNER, turned_ref, gate_ref, inner_wide_ref, hidden_ref, keep_ref)
+    half_frames(frames_ref, counts, RIM, rim_wide_ref)
+    own_at, low_at, high_at = edge_sources(nb_ref, RIM)
+    index_ref[0:1, EDGES:] = own_at
+    index_ref[1:2, EDGES:] = low_at
+    index_ref[2:3, EDGES:] = high_at
+    rim_hot_ref[...] = own_one_hot(own_at)
+    for group in range(GROUPS):
+        ghost_hot_ref[group] = ghost_one_hot(low_at, high_at, group)
     place = lax.axis_index("gx")
     low_shift = jnp.where(place == 0, -box_ref[0], 0.0)
     high_shift = jnp.where(place == lax.axis_size("gx") - 1, box_ref[0], 0.0)
     shift = jnp.where(low_at >= 0, low_shift, jnp.where(high_at >= 0, high_shift, 0.0))
-    first = iota((8, EDGES), 0) == 0
-    parts_ref[pl.ds(0, 3), :] = pos_ref[...]
-    target = jnp.concatenate([parts_ref[0:8, :]] * KNB, axis=1)
-    vector = source + jnp.where(first, shift, 0.0) - target
-    distance = jnp.sqrt(jnp.sum(vector * vector, axis=0, keepdims=True) + SOFTENING)
-    edge_ref[...] = jnp.where(iota((8, EDGES), 0) == 3, distance, vector)
-    gate_ref[...] = edge_gate(radial_ref, radial(distance)[0])
-    build_weights(weight_ref, zero_ref, pair_ref)
-    normalise(feat_ref, low_ref, high_ref, own_ref, ghost_ref)
-    gather(own_ref, ghost_ref, own_hot_ref, ghost_hot_ref, picked_ref)
-    to_frame(picked_ref, wide_ref, rows_ref)
-    convolve(rows_ref, zero_ref, pair_ref, turned_f32_ref)
-
-    @pl.loop(0, C // 16)
-    def _(step):
-        start = pl.multiple_of(step * 16, 16)
-        for degree, row_count, offset in LAYOUT:
-            sums = message_rows(
-                degree, row_count, offset, start, turned_f32_ref, gate_ref, wide_ref
-            )
-            for k, total in enumerate(sums):
-                rows = pl.ds((degree * degree + k) * C + start, 16)
-                hidden = feat_ref[rows, :].astype(F32) + total * KNB ** (-0.5)
-                hidden_ref[rows, :] = hidden.astype(BF16)
-        for row in range(EDGE_ROWS):
-            rows = pl.ds(row * C + start, 16)
-            turned_ref[rows, :] = turned_f32_ref[rows, :].astype(BF16)
-
-    pack_rims(lambda start, size: hidden_ref[pl.ds(start, size), :], send_low_ref, send_high_ref)
-
-
-def second_kernel(
-    feat_ref, low_ref, high_ref, frame_ref, nb_ref, edge_ref, weight_ref, radial_ref,
-    readout_ref,
-    slope_ref, distance_slope_ref, send_low_ref, send_high_ref,
-    own_hot_ref, ghost_hot_ref, own_ref, ghost_ref, picked_ref, wide_ref, rows_ref,
-    turned_ref, gate_ref, zero_ref, pair_ref, upper_ref, gate_slope_ref, turned_slope_ref,
-    readout_wide_ref, edge_slope_ref, ghost_slope_ref,
-):
-    spread_frames(frame_ref, wide_ref)
-    build_gathers(nb_ref, own_hot_ref, ghost_hot_ref)
-    distance = edge_ref[3:4, :]
-    gate_ref[...] = edge_gate(radial_ref, radial(distance)[0])
-    build_weights(weight_ref, zero_ref, pair_ref)
-    own_scale, ghost_scale = normalise(feat_ref, low_ref, high_ref, own_ref, ghost_ref)
-    gather(own_ref, ghost_ref, own_hot_ref, ghost_hot_ref, picked_ref)
-    to_frame(picked_ref, wide_ref, rows_ref)
-    convolve(rows_ref, zero_ref, pair_ref, turned_ref)
+    target = jnp.concatenate([both_lanes(positions, RIM)] * TILES, axis=1)
+    target_ref[...] = jnp.where(iota((8, EDGES), 0) == 3, shift, target)
+    build_weights(weight_ref, 1, zero_ref.at[1], pair_ref.at[1])
+    build_back_weights(weight_ref, 1, zero_ref.at[2], pair_ref.at[2])
     for degree in range(LMAX + 1):
         row = jnp.broadcast_to(readout_ref[degree : degree + 1, :], (C, C))
         readout_wide_ref[degree] = jnp.transpose(row) * (1.0 / (2 * degree + 1))
 
+
+def first_rim_kernel(
+    base_ref, low_ref, high_ref, own_ref, wide_ref, own_hot_ref, ghost_hot_ref, target_ref,
+    parts_ref, zero_ref, pair_ref, radial_ref,
+    hidden_ref, keep_ref, edge_ref, send_low_ref, send_high_ref,
+    ghost_ref, picked_ref, rows_ref, turned_ref, gate_ref,
+):
+    ghosts = jnp.concatenate(
+        [low_ref[pl.ds(LAST, 32), :], high_ref[pl.ds(LAST, 32), :]], axis=1
+    )
+    found = dot(parts_ref[...], own_hot_ref[...]) + dot(ghosts, ghost_hot_ref[GROUPS - 1])
+    target = jnp.where(iota((8, EDGES), 0) == 3, 0.0, target_ref[...])
+    distance = edge_geometry(join_parts(found), target_ref[3:4, :], target, edge_ref)
+    gate_ref[...] = edge_gate(radial_ref.at[0], radial(distance)[0])
+    normalise_ghosts(low_ref, high_ref, ghost_ref)
+    gather(own_ref, own_hot_ref, picked_ref, ghost_ref, ghost_hot_ref)
+    layer_forward(picked_ref, wide_ref, rows_ref, zero_ref.at[0], pair_ref.at[0], turned_ref)
+    add_messages(base_ref, RIM, turned_ref, gate_ref, wide_ref, hidden_ref, keep_ref)
+    pack_rims(lambda start, size: hidden_ref[pl.ds(start, size), :], send_low_ref, send_high_ref)
+
+
+def turn_slopes(
+    hidden_ref, half, turned_ref, gate_ref, wide_ref, readout_wide_ref, upper_ref,
+    turned_slope_ref, gate_slope_ref,
+):
     @pl.loop(0, C // 16)
     def _(step):
         start = pl.multiple_of(step * 16, 16)
         channels = pl.ds(start, 16)
-        gate_slopes = [None] * KNB
+        gate_slopes = [None] * TILES
         for degree, row_count, offset in LAYOUT:
             sums = message_rows(degree, row_count, offset, start, turned_ref, gate_ref, wide_ref)
             weight = readout_wide_ref[degree, channels, :]
             slopes = []
             for k, total in enumerate(sums):
                 rows = pl.ds((degree * degree + k) * C + start, 16)
-                upper = feat_ref[rows, :].astype(F32) + total * KNB ** (-0.5)
-                slope = upper * weight
+                below = both_lanes(hidden_ref[rows, :].astype(F32), half)
+                slope = (below + total * KNB ** (-0.5)) * weight
                 upper_ref[rows, :] = slope * 2.0
                 slopes.append(slope * (2.0 * KNB ** (-0.5)))
-            for slot in range(KNB):
+            for slot in range(TILES):
                 lanes = slot_lanes(slot)
                 gate = gate_ref[channels, lanes]
                 for row in range(row_count):
@@ -458,19 +555,59 @@
                     before = gate_slopes[slot]
                     gate_slopes[slot] = term if before is None else before + term
                     turned_slope_ref[rows, lanes] = (slope * gate).astype(BF16)
-        for slot in range(KNB):
+        for slot in range(TILES):
             gate_slope_ref[channels, slot_lanes(slot)] = gate_slopes[slot]
 
-    distance_slope_ref[...] = jnp.broadcast_to(
-        distance_slope(radial_ref, gate_slope_ref[...], distance), (8, EDGES)
-    )
-    build_back_weights(weight_ref, zero_ref, pair_ref)
-    convolve(turned_slope_ref, zero_ref, pair_ref, turned_ref)
-    from_frame(turned_ref, wide_ref, edge_slope_ref)
-    spread_own = jnp.transpose(own_hot_ref[...].astype(F32)).astype(BF16)
+
+def write_distance_slope(radial_ref, gate_slope_ref, distance, out_ref):
+    slope = distance_slope(radial_ref, gate_slope_ref[...], distance)
+    out_ref[...] = jnp.broadcast_to(slope, (8, EDGES))
+
+
+def second_inner_kernel(
+    hidden_ref, wide_ref, own_hot_ref, edge_ref, zero_ref, pair_ref, radial_ref,
+    readout_wide_ref,
+    own_ref, scale_ref, upper_ref, turned_slope_ref, slope_ref,
+    picked_ref, rows_ref, turned_ref, gate_ref, gate_slope_ref,
+):
+    distance = edge_ref[3:4, :]
+    gate_ref[...] = edge_gate(radial_ref.at[1], radial(distance)[0])
+    scale_ref[...] = jnp.broadcast_to(normalise_own(hidden_ref, own_ref), (8, OWN))
+    gather(own_ref, own_hot_ref, picked_ref)
+    layer_forward(picked_ref, wide_ref, rows_ref, zero_ref.at[1], pair_ref.at[1], turned_ref)
+    turn_slopes(
+        hidden_ref, INNER, turned_ref, gate_ref, wide_ref, readout_wide_ref, upper_ref,
+        turned_slope_ref, gate_slope_ref,
+    )
+    write_distance_slope(radial_ref.at[1], gate_slope_ref, distance, slope_ref)
+
+
+def scatter_own(edge_slope_ref, own_hot_ref, out_ref, add_ref=None):
+    spread = jnp.transpose(own_hot_ref[...].astype(F32)).astype(BF16)
     for group, rows in enumerate(GROUP_ROWS):
         block = pl.ds(group * PACKED, rows)
-        slope_ref[block, :] = dot(edge_slope_ref[block, :], spread_own)
+        part = dot(edge_slope_ref[block, :], spread)
+        out_ref[block, :] = part if add_ref is None else part + add_ref[block, :]
+
+
+def second_rim_kernel(
+    hidden_ref, low_ref, high_ref, own_ref, wide_ref, own_hot_ref, ghost_hot_ref, edge_ref,
+    zero_ref, pair_ref, radial_ref, readout_wide_ref,
+    upper_ref, slope_ref, own_slope_ref, send_low_ref, send_high_ref,
+    ghost_ref, picked_ref, rows_ref, turned_ref, gate_ref, gate_slope_ref, turned_slope_ref,
+    edge_slope_ref, ghost_slope_ref,
+):
+    distance = edge_ref[3:4, :]
+    gate_ref[...] = edge_gate(radial_ref.at[1], radial(distance)[0])
+    ghost_scale = normalise_ghosts(low_ref, high_ref, ghost_ref)
+    gather(own_ref, own_hot_ref, picked_ref, ghost_ref, ghost_hot_ref)
+    layer_forward(picked_ref, wide_ref, rows_ref, zero_ref.at[1], pair_ref.at[1], turned_ref)
+    turn_slopes(
+        hidden_ref, RIM, turned_ref, gate_ref, wide_ref, readout_wide_ref, upper_ref,
+        turned_slope_ref, gate_slope_ref,
+    )
+    convolve(turned_slope_ref, zero_ref.at[2], pair_ref.at[2], turned_ref)
+    from_frame(turned_ref, wide_ref, edge_slope_ref)
     for group, rows in enumerate(GROUP_ROWS):
         spread_ghost = jnp.transpose(ghost_hot_ref[group].astype(F32)).astype(BF16)
         part = dot(edge_slope_ref[pl.ds(group * PACKED, rows), :], spread_ghost)
@@ -478,19 +615,6 @@
             ghost_slope_ref[...] = part
         else:
             ghost_slope_ref[pl.ds(0, rows), :] += part
-    along = jnp.zeros((8, OWN), F32)
-    for coef in range(NCOEF):
-        rows = pl.ds(coef * C, C)
-        along = along + fold_rows(slope_ref[rows, :] * feat_ref[rows, :].astype(F32))
-    along = jnp.sum(along, axis=0, keepdims=True) * (1.0 / ROWS)
-    along = along * own_scale * own_scale * own_scale
-    for coef in range(NCOEF):
-        rows = pl.ds(coef * C, C)
-        slope_ref[rows, :] = (
-            upper_ref[rows, :]
-            + slope_ref[rows, :] * own_scale
-            - feat_ref[rows, :].astype(F32) * along
-        )
     along = jnp.zeros((8, 2 * OWN), F32)
     for block in range(PER_GROUP):
         values = read_ghosts(low_ref, high_ref, block)
@@ -503,43 +627,37 @@
         back = ghost_slope_ref[rows, :] * ghost_scale - values * along
         send_low_ref[rows, :] = back[:, :OWN].astype(BF16)
         send_high_ref[rows, :] = back[:, OWN:].astype(BF16)
-
-
-def third_kernel(
-    slope_ref, low_ref, high_ref, frame_ref, nb_ref, edge_ref, radial_ref, turned_ref,
-    second_slope_ref, velocities_ref, masses_ref,
-    tile_ref,
-    wide_ref, gate_slope_ref, hidden_slope_ref,
-):
-    spread_frames(frame_ref, wide_ref)
-    for group, rows in enumerate(GROUP_ROWS):
-        block = pl.ds(group * PACKED, rows)
-        back = jnp.concatenate([low_ref[pl.ds(0, rows), :], high_ref[pl.ds(0, rows), :]], axis=1)
-        total = slope_ref[block, :] + dot(back, rim_place(group))
-        hidden_slope_ref[block, :] = total * KNB ** (-0.5)
-
+    scatter_own(edge_slope_ref, own_hot_ref, own_slope_ref)
+    write_distance_slope(radial_ref.at[1], gate_slope_ref, distance, slope_ref)
+
+
+def gate_slopes_back(hidden_slope_ref, half, wide_ref, keep_ref, gate_slope_ref):
     @pl.loop(0, C // 16)
     def _(step):
         start = pl.multiple_of(step * 16, 16)
-        gate_slopes = [None] * KNB
+        gate_slopes = [None] * TILES
         for degree, row_count, offset in LAYOUT:
             slopes = [
-                hidden_slope_ref[pl.ds((degree * degree + k) * C + start, 16), :]
+                both_lanes(
+                    hidden_slope_ref[pl.ds((degree * degree + k) * C + start, 16), :], half
+                )
                 for k in range(2 * degree + 1)
             ]
-            for slot in range(KNB):
+            for slot in range(TILES):
                 lanes = slot_lanes(slot)
                 for row in range(row_count):
                     slope = slope_rows(
                         degree, row_count, offset, row, lanes, slopes, wide_ref
                     )
                     rows = pl.ds(edge_row(degree, row) * C + start, 16)
-                    term = turned_ref[rows, lanes].astype(F32) * slope
+                    term = keep_ref[rows, lanes].astype(F32) * slope
                     before = gate_slopes[slot]
                     gate_slopes[slot] = term if before is None else before + term
-        for slot in range(KNB):
+        for slot in range(TILES):
             gate_slope_ref[pl.ds(start, 16), slot_lanes(slot)] = gate_slopes[slot]
 
+
+def edge_pulls(radial_ref, gate_slope_ref, edge_ref, second_slope_ref, half):
     distance = edge_ref[3:4, :]
     slope = distance_slope(radial_ref, gate_slope_ref[...], distance) + second_slope_ref[0:1, :]
     vector = jnp.where(iota((8, EDGES), 0) < 3, edge_ref[...], 0.0)
@@ -547,17 +665,69 @@
     virial = -jnp.sum(pull * vector)
     high, middle, low = split_three(pull)
     parts = jnp.concatenate([high, middle, low, jnp.zeros((8, EDGES), F32)], axis=0).astype(BF16)
-    own_at, low_at, high_at = edge_sources(nb_ref)
-    spread_own = jnp.transpose(own_one_hot(own_at).astype(F32)).astype(BF16)
+    on_target = pull[:, :OWN]
+    for tile in range(1, TILES):
+        on_target = on_target + pull[:, tile * OWN : (tile + 1) * OWN]
+    on_target = jnp.where(inside((8, OWN), half), fold_slots(on_target), 0.0)
+    return parts, on_target, virial
+
+
+def spread(hot):
+    return jnp.transpose(hot.astype(F32)).astype(BF16)
+
+
+def middle_kernel(
+    hidden_ref, scale_ref, inner_upper_ref, rim_upper_ref, own_slope_ref, turned_slope_ref,
+    wide_ref, own_hot_ref, zero_ref, pair_ref, radial_ref, keep_ref, edge_ref,
+    second_slope_ref,
+    slope_ref, part_ref,
+    turned_ref, edge_slope_ref, gate_slope_ref,
+):
+    convolve(turned_slope_ref, zero_ref.at[2], pair_ref.at[2], turned_ref)
+    from_frame(turned_ref, wide_ref, edge_slope_ref)
+    scatter_own(edge_slope_ref, own_hot_ref, slope_ref, own_slope_ref)
+    scale = scale_ref[0:1, :]
+    along = jnp.zeros((8, OWN), F32)
+    for coef in range(NCOEF):
+        rows = pl.ds(coef * C, C)
+        along = along + fold_rows(slope_ref[rows, :] * hidden_ref[rows, :].astype(F32))
+    along = jnp.sum(along, axis=0, keepdims=True) * (1.0 / ROWS)
+    along = along * scale * scale * scale
+    held = inside((C, OWN), INNER)
+    for coef in range(NCOEF):
+        rows = pl.ds(coef * C, C)
+        upper = jnp.where(held, inner_upper_ref[rows, :], rim_upper_ref[rows, :])
+        total = upper + slope_ref[rows, :] * scale - hidden_ref[rows, :].astype(F32) * along
+        slope_ref[rows, :] = total * KNB ** (-0.5)
+    gate_slopes_back(slope_ref, INNER, wide_ref, keep_ref, gate_slope_ref)
+    parts, on_target, virial = edge_pulls(
+        radial_ref.at[0], gate_slope_ref, edge_ref, second_slope_ref, INNER
+    )
+    landed = join_parts(dot(parts, spread(own_hot_ref[...]))) - on_target
+    part_ref[...] = jnp.where(iota((8, OWN), 0) == 7, virial, landed)
+
+
+def last_kernel(
+    slope_ref, low_ref, high_ref, wide_ref, own_hot_ref, index_ref, radial_ref, keep_ref,
+    edge_ref, second_slope_ref, part_ref, velocities_ref, masses_ref,
+    tile_ref,
+    gate_slope_ref, hidden_slope_ref,
+):
+    for group, rows in enumerate(GROUP_ROWS):
+        block = pl.ds(group * PACKED, rows)
+        back = jnp.concatenate([low_ref[pl.ds(0, rows), :], high_ref[pl.ds(0, rows), :]], axis=1)
+        added = dot(back, rim_place(group)) * KNB ** (-0.5)
+        hidden_slope_ref[block, :] = slope_ref[block, :] + added
+    gate_slopes_back(hidden_slope_ref, RIM, wide_ref, keep_ref, gate_slope_ref)
+    parts, on_target, virial = edge_pulls(
+        radial_ref.at[0], gate_slope_ref, edge_ref, second_slope_ref, RIM
+    )
+    landed = join_parts(dot(parts, spread(own_hot_ref[...]))) - on_target + part_ref[...]
+    low_at, high_at = index_ref[1:2, EDGES:], index_ref[2:3, EDGES:]
     rim_at = jnp.where(low_at >= 0, low_at + (OWN - GHOST), high_at - OWN)
     rim_at = jnp.where((low_at >= 0) | (high_at >= 0), rim_at, -1)
-    spread_rim = jnp.transpose(own_one_hot(rim_at).astype(F32)).astype(BF16)
-    landed = dot(parts, spread_own)
-    landed = landed[0:8] + landed[8:16] + landed[16:24]
-    for slot in range(KNB):
-        landed = landed - pull[:, slot * OWN : (slot + 1) * OWN]
-    outward = dot(parts, spread_rim)
-    outward = -(outward[0:8] + outward[8:16] + outward[16:24])
+    outward = -join_parts(dot(parts, spread(own_one_hot(rim_at))))
+    virial = virial + part_ref[7:8, :]
     masses = masses_ref[...]
     speed = jnp.concatenate([velocities_ref[...], jnp.zeros((5, OWN), F32)], axis=0)
     per_mass = STEP_TIME / masses
@@ -649,33 +819,35 @@
 SMALL = ("box", "control")
 
 
-def call(kernel, outs, scratch, args, grant, layers=()):
-    names = list(args)
-
-    def body(*refs):
-        views = list(refs)
-        for name, layer in dict(layers).items():
-            views[names.index(name)] = refs[names.index(name)].at[layer]
-        kernel(*views)
-
-    specs = []
-    for name in names:
-        if name in SMALL:
-            specs.append(pl.BlockSpec(memory_space=pltpu.SMEM))
+def call(kernel, outs, scratch, args, grant=GRANT, hbm=False, cost=1):
+    def space(name):
+        if hbm:
+            return pltpu.HBM
+        return pltpu.SMEM if name in SMALL else pltpu.VMEM
+
+    def buffer(entry):
+        return entry if len(entry) == 3 else entry + (pltpu.VMEM,)
+
+    buffers = []
+    for entry in scratch:
+        if isinstance(entry, int):
+            buffers.append(pltpu.SemaphoreType.DMA((entry,)))
         else:
-            specs.append(pl.BlockSpec(memory_space=pltpu.VMEM))
-    out_specs = [
-        pl.BlockSpec(memory_space=pltpu.SMEM if len(shape) == 1 else pltpu.VMEM)
-        for shape, kind in outs
-    ]
+            shape, kind, where = buffer(entry)
+            buffers.append(where(shape, kind))
     return pl.pallas_call(
-        body,
+        kernel,
         out_shape=[jax.ShapeDtypeStruct(shape, kind) for shape, kind in outs],
-        in_specs=specs,
-        out_specs=out_specs,
-        scratch_shapes=[pltpu.VMEM(shape, kind) for shape, kind in scratch],
+        in_specs=[pl.BlockSpec(memory_space=space(name)) for name in args],
+        out_specs=[
+            pl.BlockSpec(memory_space=pltpu.SMEM if len(shape) == 1 else pltpu.VMEM)
+            for shape, kind in outs
+        ],
+        scratch_shapes=buffers,
         compiler_params=pltpu.CompilerParams(vmem_limit_bytes=grant << 20),
-        cost_estimate=pl.CostEstimate(flops=0, bytes_accessed=1 << 20, transcendentals=0),
+        cost_estimate=pl.CostEstimate(
+            flops=cost << 30, bytes_accessed=1 << 20, transcendentals=0
+        ),
     )(*args.values())
 
 
@@ -705,80 +877,109 @@
         return from_low, from_high
 
     packed = ((PACKED, OWN), BF16)
+    own_rows = ((ROWS, OWN), BF16)
+    own_sums = ((ROWS, OWN), F32)
+    kept = ((EDGE_ROWS * C, EDGES), BF16)
+    turned = ((EDGE_ROWS * C, EDGES), F32)
+    picked = ((ROWS, EDGES), F32)
+    edge = ((8, EDGES), F32)
+    wide = ((WROWS, 8, EDGES), F32)
+    gate = ((C, EDGES), F32)
+    hot = ((OWN, EDGES), BF16)
+    ghost = ((PACKED, 2 * OWN), BF16)
+    small = ((8, OWN), F32)
+    place = ((3, OWN), F32)
+    parts = ((32, OWN), F32)
     mass_row = masses[None, :]
     to_low, to_high = call(
         pack_kernel,
         [packed, packed],
-        [((32, OWN), F32)],
+        [own_rows, place, parts, 2],
         dict(feat=node_feat, positions=positions),
-        8,
+        grant=8,
+        hbm=True,
     )
     from_low, from_high = exchange(to_low, to_high)
-    gathers = [((OWN, EDGES), BF16), ((GROUPS, 2 * OWN, EDGES), BF16)]
-    work = [
-        ((ROWS, OWN), BF16),
-        ((PACKED, 2 * OWN), BF16),
-        ((ROWS, EDGES), F32),
-        ((WROWS, 8, EDGES), F32),
-        ((EDGE_ROWS * C, EDGES), BF16),
-        ((EDGE_ROWS * C, EDGES), F32),
-        ((C, EDGES), F32),
-        ((C, C), BF16),
-        ((MMAX, 2 * C, 2 * C), BF16),
-    ]
-    hidden, turned, frame, edge, to_low, to_high = call(
-        first_kernel,
+    (
+        hidden, keep_inner, edge_inner, own, wide_inner, wide_rim, hot_inner, hot_rim,
+        hot_ghost, index, target, own_parts, zero, pair, radial_rows, readout_wide,
+    ) = call(
+        first_inner_kernel,
         [
-            ((ROWS, OWN), BF16),
-            ((EDGE_ROWS * C, EDGES), BF16),
-            ((WROWS, EDGES), F32),
-            ((8, EDGES), F32),
-            packed,
-            packed,
+            own_rows, kept, edge, own_rows, wide, wide, hot, hot,
+            ((GROUPS, 2 * OWN, EDGES), BF16), ((8, 2 * EDGES), jnp.int32), edge,
+            ((32, OWN), BF16), ((3, C, C), BF16), ((3, MMAX, 2 * C, 2 * C), BF16),
+            (radial_weight.shape, F32), ((LMAX + 1, C, C), F32),
         ],
-        [((32, OWN), F32)] + gathers + work,
+        [
+            own_rows, (frames.shape, BF16), ((KNB, OWN), jnp.int32), ((1, OWN), jnp.int32),
+            place, ((3,), F32, pltpu.SMEM), (conv_weight.shape, BF16), (readout.shape, F32),
+            parts, picked, kept, turned, gate, 9,
+        ],
         dict(
-            feat=node_feat, low=from_low, high=from_high, frames=frames,
-            neighbours=neighbours, counts=counts[None, :], positions=positions,
-            box=box_lengths, weight=conv_weight, radial=radial_weight,
+            feat=node_feat, frames=frames, neighbours=neighbours, counts=counts[None, :],
+            positions=positions, box=box_lengths, weight=conv_weight, radial=radial_weight,
+            readout=readout,
         ),
-        GRANTS[0],
-        dict(weight=0, radial=0),
+        hbm=True,
+        cost=5,
+    )
+    hidden, keep_rim, edge_rim, to_low, to_high = call(
+        first_rim_kernel,
+        [own_rows, kept, edge, packed, packed],
+        [ghost, picked, kept, turned, gate],
+        dict(
+            base=hidden, low=from_low, high=from_high, own=own, wide=wide_rim, hot=hot_rim,
+            ghost_hot=hot_ghost, target=target, parts=own_parts, zero=zero, pair=pair,
+            radial=radial_rows,
+        ),
     )
     from_low, from_high = exchange(to_low, to_high)
-    slope, second_slope, to_low, to_high = call(
-        second_kernel,
-        [((ROWS, OWN), F32), ((8, EDGES), F32), packed, packed],
-        gathers
-        + work
-        + [
-            ((ROWS, OWN), F32),
-            ((C, EDGES), F32),
-            ((EDGE_ROWS * C, EDGES), BF16),
-            ((LMAX + 1, C, C), F32),
-            ((ROWS, EDGES), BF16),
+    own, scale, upper_inner, turned_slope, slope_inner = call(
+        second_inner_kernel,
+        [own_rows, small, own_sums, kept, edge],
+        [picked, kept, turned, gate, gate],
+        dict(
+            hidden=hidden, wide=wide_inner, hot=hot_inner, edge=edge_inner, zero=zero,
+            pair=pair, radial=radial_rows, readout=readout_wide,
+        ),
+        cost=5,
+    )
+    upper_rim, slope_rim, own_slope, to_low, to_high = call(
+        second_rim_kernel,
+        [own_sums, edge, own_sums, packed, packed],
+        [
+            ghost, picked, kept, turned, gate, gate, kept, ((ROWS, EDGES), BF16),
             ((PACKED, 2 * OWN), F32),
         ],
         dict(
-            hidden=hidden, low=from_low, high=from_high, frame=frame, neighbours=neighbours,
-            edge=edge, weight=conv_weight, radial=radial_weight, readout=readout,
+            hidden=hidden, low=from_low, high=from_high, own=own, wide=wide_rim, hot=hot_rim,
+            ghost_hot=hot_ghost, edge=edge_rim, zero=zero, pair=pair, radial=radial_rows,
+            readout=readout_wide,
         ),
-        GRANTS[1],
-        dict(weight=1, radial=1),
     )
     from_low, from_high = exchange(to_low, to_high)
-    small = ((8, OWN), F32)
+    slope, part = call(
+        middle_kernel,
+        [own_sums, small],
+        [turned, ((ROWS, EDGES), BF16), gate],
+        dict(
+            hidden=hidden, scale=scale, upper_inner=upper_inner, upper_rim=upper_rim,
+            own_slope=own_slope, turned_slope=turned_slope, wide=wide_inner, hot=hot_inner,
+            zero=zero, pair=pair, radial=radial_rows, keep=keep_inner, edge=edge_inner,
+            second_slope=slope_inner,
+        ),
+        cost=5,
+    )
     (tile,) = call(
-        third_kernel,
+        last_kernel,
         [small],
-        [((WROWS, 8, EDGES), F32), ((C, EDGES), F32), ((ROWS, OWN), F32)],
+        [gate, own_sums],
         dict(
-            slope=slope, low=from_low, high=from_high, frame=frame, neighbours=neighbours,
-            edge=edge, radial=radial_weight, turned=turned, second_slope=second_slope,
-            velocities=velocities, masses=mass_row,
+            slope=slope, low=from_low, high=from_high, wide=wide_rim, hot=hot_rim, index=index,
+            radial=radial_rows, keep=keep_rim, edge=edge_rim, second_slope=slope_rim,
+            part=part, velocities=velocities, masses=mass_row,
         ),
-        GRANTS[2],
-        dict(radial=0),
     )
     own = tile
     caught = None
@@ -799,7 +1000,7 @@
         if width * ways == count:
             break
         tile, caught = call(
-            functools.partial(merge_kernel, width, ways), [small, small], [], tiles, 1
+            functools.partial(merge_kernel, width, ways), [small, small], [], tiles, grant=1
         )
         width = width * ways
     if caught is not None:
@@ -813,7 +1014,7 @@
             tiles, masses=mass_row, noise=thermal_noise, positions=positions,
             box=box_lengths, control=control,
         ),
-        1,
+        grant=1,
     )
 
 

time: 82.7 us -> 64 us (0.77)
  waiting for transfers between devices: 15.7 us -> 4.07 us
  local copies, waits for them, and re-layouts: 8.27 us -> 1.87 us
  starting transfers between devices: 21.5 us -> 20.2 us
    ppermute x3, waiting for transfers between devices: 11.1 us -> 0.01 us  [exchange(): from_low = lax.ppermute(to_high, 'gx', forward)]
    unnamed x38 -> x30, local copies, waits for them, and re-layouts: 8.27 us -> 1.87 us
    ppermute x3, starting transfers between devices: 3.93 us -> 0.62 us  [exchange(): from_low = lax.ppermute(to_high, 'gx', forward)]
    ppermute x3, starting transfers between devices: 11 us -> 13.9 us  [exchange(): from_high = lax.ppermute(to_low, 'gx', backward)]
    ppermute x6, starting transfers between devices: 6.59 us -> 5.69 us  [shards(): tiles['tile%d' % far] = lax.ppermute(tile, 'gx', pairs)]
    pallas_call x6 -> x9, Pallas kernels: 35.9 us -> 36.6 us  [call(): pl.pallas_call(kernel, out_shape=[jax.ShapeDtypeStruct(shape, kind) for s...]
  transfers between devices with their start and end apart: 12 -> 12, of which waited for: 7 -> 4; matrix products, arithmetic and copies ran while one was open for 0% -> 0% of each run, Pallas kernels for 0% -> 26%
where the time goes in v3:
time: 64 us; the launch traced here: 63.9 us
  Pallas kernels  36.6 us (57%)
  starting transfers between devices  20.2 us (32%)
  waiting for transfers between devices  4.07 us (6%)
  local copies, waits for them, and re-layouts  1.87 us (3%)
  between operations  1.08 us (2%)
    pallas_call x9, Pallas kernels, call(): pl.pallas_call(kernel, out_shape=[jax.ShapeDtypeStruct(shape, kind) for s...  36.6 us
    ppermute x3, starting transfers between devices, exchange(): from_high = lax.ppermute(to_low, 'gx', backward)  13.9 us
    ppermute x6, starting transfers between devices, shards(): tiles['tile%d' % far] = lax.ppermute(tile, 'gx', pairs)  5.69 us
    ppermute x6, waiting for transfers between devices, shards(): tiles['tile%d' % far] = lax.ppermute(tile, 'gx', pairs)  4.05 us
    unnamed x30, local copies, waits for them, and re-layouts  1.87 us
  transfers between devices with their start and end apart: 12, of which 4 were waited for; matrix products, arithmetic and copies ran while one was open for 0% of the time, Pallas kernels for 26%

profile of v3, /device:TPU:0, one launch (start us, length us, event | category | flops | bytes accessed | tf_op | source)
XLA Modules:
  0.0 63.9 jit_solution(1097580963851542197)
XLA Ops:
  0.6 1.1 %copy-done.2 = bf16[3200,128]{1,0:T(8,128)(2,1)S(1)} copy-done((bf16[3200,128]{1,0:T(8,128)(2,1)S(1)}, bf16[3200,128]{1,0:T(8,128)(2,1)}, u32[]{:S(2)}) %copy-start.2) | copy-done | bytes 819224
  1.8 0.7 %copy-done.9 = f32[3,128]{1,0:T(4,128)S(1)} copy-done((f32[3,128]{1,0:T(4,128)S(1)}, f32[3,128]{1,0:T(4,128)}, u32[]{:S(2)}) %copy-start.9) | copy-done | bytes 1560
  2.5 0.7 %shard_map.149 = (bf16[896,128]{1,0:T(8,128)(2,1)S(1)}, bf16[896,128]{1,0:T(8,128)(2,1)S(1)}) custom-call(bf16[3200,128]{1,0:T(8,128)(2,1)S(1)} %copy-done.2, f32[3,128]{1,0:T(4,128)S(1)} %copy-done.9), custom_call_target="tpu_custom_call" | custom-call | flops 1073741824 | bytes 1048576 | tf_op jit(solution)/shard_map/pallas_call | solution.py:838
  3.2 0.5 collective-permute-start
  3.7 5.1 %collective-permute-start.1 = (bf16[896,128]{1,0:T(8,128)(2,1)S(1)}, bf16[896,128]{1,0:T(8,128)(2,1)S(1)}, u32[]{:S(2)}, u32[]{:S(2)}) collective-permute-start(bf16[896,128]{1,0:T(8,128)(2,1)S(1)} %get-tuple-element.42), channel_id=1, source_target_pairs={{1,0},{2,1},{3,2},{4,3},{5,4},{6,5},{7,6},{8,7},{9,8},{10,9},{11,1... | collective-permute-start | bytes 688136 | tf_op jit(solution)/shard_map/ppermute | solution.py:876
  8.9 5.7 %shard_map.148 = (bf16[3200,128]{1,0:T(8,128)(2,1)S(1)}, bf16[2432,256]{1,0:T(8,128)(2,1)S(1)}, f32[8,256]{1,0:T(8,128)S(1)}, bf16[3200,128]{1,0:T(8,128)(2,1)S(...) custom-call(bf16[3200,128]{1,0:T(8,128)(2,1)S(1)} %copy-done.3, ...), custom_call_target="tpu_custom_call" | custom-call | flops 5368709120 | bytes 1048576 | tf_op jit(solution)/shard_map/pallas_call | solution.py:838
  14.6 0.0 collective-permute-done.1.high_ref
  14.6 5.3 %shard_map.150 = (bf16[3200,128]{1,0:T(8,128)(2,1)S(1)}, bf16[2432,256]{1,0:T(8,128)(2,1)S(1)}, f32[8,256]{1,0:T(8,128)S(1)}, bf16[896,128]{1,0:T(8,128)(2,1)S(1)}, bf16[896,128]{1,0:T(8,128)(2,1)S(1)}) custom-call(bf16[3200,128]{1,0:T(8,128)(2,1)S(1)} %get-tuple-element.40.base_ref, bf16[896,128]{1,0:T(8,128)(2,1)S(1)} %collective-permute-done.low_ref, ...), custom_call_target="tpu_custom_call" | custom-call | flops 1073741824 | bytes 1048576 | tf_op jit(solution)/shard_map/pallas_call | solution.py:838
  19.9 0.1 collective-permute-start.2
  20.0 4.4 %collective-permute-start.3 = (bf16[896,128]{1,0:T(8,128)(2,1)S(1)}, bf16[896,128]{1,0:T(8,128)(2,1)S(1)}, u32[]{:S(2)}, u32[]{:S(2)}) collective-permute-start(bf16[896,128]{1,0:T(8,128)(2,1)S(1)} %get-tuple-element.60), channel_id=1, source_target_pairs={{1,0},{2,1},{3,2},{4,3},{5,4},{6,5},{7,6},{8,7},{9,8},{10,9},{11,1... | collective-permute-start | bytes 688136 | tf_op jit(solution)/shard_map/ppermute | solution.py:876
  24.4 6.0 %shard_map.151 = (bf16[3200,128]{1,0:T(8,128)(2,1)S(1)}, f32[8,128]{1,0:T(8,128)S(1)}, f32[3200,128]{1,0:T(8,128)S(1)}, bf16[2432,256]{1,0:T(8,128)(2,1)S(1)}, f32[8,256]{1,0:T(8,128)S(1)}) custom-call(bf16[3200,128]{1,0:T(8,128)(2,1)S(1)} %get-tuple-element.52.hidden_ref, f32[115,8,256]{2,1,0:T(8,128)S(1)} %get-tuple-element.53.wide_ref, ...), custom_call_target="tpu_custom_call" | custom-call | flops 5368709120 | bytes 1048576 | tf_op jit(solution)/shard_map/pallas_call | solution.py:838
  30.4 0.0 collective-permute-done.2.low_ref
  30.4 8.7 %shard_map.152 = (f32[3200,128]{1,0:T(8,128)S(1)}, f32[8,256]{1,0:T(8,128)S(1)}, f32[3200,128]{1,0:T(8,128)S(1)}, bf16[896,128]{1,0:T(8,128)(2,1)S(1)}, bf16[896,128]{1,0:T(8,128)(2,1)S(1)}) custom-call(bf16[3200,128]{1,0:T(8,128)(2,1)S(1)} %get-tuple-element.52.hidden_ref, bf16[896,128]{1,0:T(8,128)(2,1)S(1)} %collective-permute-done.2.low_ref, ...), custom_call_target="tpu_custom_call" | custom-call | flops 1073741824 | bytes 1048576 | tf_op jit(solution)/shard_map/pallas_call | solution.py:838
  39.1 0.1 collective-permute-start.4
  39.2 4.4 %collective-permute-start.5 = (bf16[896,128]{1,0:T(8,128)(2,1)S(1)}, bf16[896,128]{1,0:T(8,128)(2,1)S(1)}, u32[]{:S(2)}, u32[]{:S(2)}) collective-permute-start(bf16[896,128]{1,0:T(8,128)(2,1)S(1)} %get-tuple-element.70), channel_id=1, source_target_pairs={{1,0},{2,1},{3,2},{4,3},{5,4},{6,5},{7,6},{8,7},{9,8},{10,9},{11,1... | collective-permute-start | bytes 688136 | tf_op jit(solution)/shard_map/ppermute | solution.py:876
  43.6 5.2 %shard_map.153 = (f32[3200,128]{1,0:T(8,128)S(1)}, f32[8,128]{1,0:T(8,128)S(1)}) custom-call(bf16[3200,128]{1,0:T(8,128)(2,1)S(1)} %get-tuple-element.52.hidden_ref, f32[8,128]{1,0:T(8,128)S(1)} %get-tuple-element.57.scale_ref, f32[3200,128]{1,0:T(8,128)S(1)} %get-tuple-element.58.inner_upper_ref, f32[3200,128]{1,0:T(8,128)S(1)} %get-tuple-element.63.rim_upper_ref, ...), custom_call_target="tpu_custom_call" | custom-call | flops 5368709120 | bytes 1048576 | tf_op jit(solution)/shard_map/pallas_call | solution.py:838
  48.8 0.0 collective-permute-done.5.high_ref
  48.9 3.0 %shard_map.154.refs_0_.refs_4_ = f32[8,128]{1,0:T(8,128)S(1)} custom-call(f32[3200,128]{1,0:T(8,128)S(1)} %get-tuple-element.68.slope_ref, bf16[896,128]{1,0:T(8,128)(2,1)S(1)} %collective-permute-done.4.low_ref, bf16[896,128]{1,0:T(8,128)(2,1)S(1)} %collective-permute-done.5.high_ref, f32[115,8,256]{2,1,0:T(8,128)S(1)} %get-tuple-element.44.wide_ref, ...), custom_call_target="tpu_custom_call" | custom-call | flops 1073741824 | bytes 1048576 | tf_op jit(solution)/shard_map/pallas_call | solution.py:838
  51.8 0.0 copy-start.11
  51.8 0.0 copy-start.14
  51.8 0.1 collective-permute-start.8
  51.9 0.1 collective-permute-start.7
  52.0 1.7 %collective-permute-start.6 = (f32[8,128]{1,0:T(8,128)S(1)}, f32[8,128]{1,0:T(8,128)S(1)}, u32[]{:S(2)}, u32[]{:S(2)}) collective-permute-start(f32[8,128]{1,0:T(8,128)S(1)} %shard_map.154.refs_0_.refs_4_), channel_id=1, source_target_pairs={{1,0},{2,1},{3,2},{0,3},{5,4},{6,5},{7,6},{4,7},{9,8},{10,9},{11,1... | collective-permute-start | bytes 12296 | tf_op jit(solution)/shard_map/ppermute | solution.py:997
  53.7 1.3 %collective-permute-done.8.refs_3_ = f32[8,128]{1,0:T(8,128)S(1)} collective-permute-done((f32[8,128]{1,0:T(8,128)S(1)}, f32[8,128]{1,0:T(8,128)S(1)}, u32[]{:S(2)}, u32[]{:S(2)}) %collective-permute-start.8) | collective-permute-done | bytes 4128 | tf_op jit(solution)/shard_map/ppermute | solution.py:997
  54.9 0.7 %collective-permute-done.7.refs_2_ = f32[8,128]{1,0:T(8,128)S(1)} collective-permute-done((f32[8,128]{1,0:T(8,128)S(1)}, f32[8,128]{1,0:T(8,128)S(1)}, u32[]{:S(2)}, u32[]{:S(2)}) %collective-permute-start.7) | collective-permute-done | bytes 4128 | tf_op jit(solution)/shard_map/ppermute | solution.py:997
  55.6 0.4 shard_map.155
  56.0 0.1 collective-permute-start.11
  56.0 2.3 %collective-permute-start.10 = (f32[8,128]{1,0:T(8,128)S(1)}, f32[8,128]{1,0:T(8,128)S(1)}, u32[]{:S(2)}, u32[]{:S(2)}) collective-permute-start(f32[8,128]{1,0:T(8,128)S(1)} %get-tuple-element.75.refs_0_), channel_id=1, source_target_pairs={{8,0},{9,1},{10,2},{11,3},{12,4},{13,5},{14,6},{15,7},{0,8},{1,9},... | collective-permute-start | bytes 12296 | tf_op jit(solution)/shard_map/ppermute | solution.py:997
  58.4 1.5 %collective-permute-start.9 = (f32[8,128]{1,0:T(8,128)S(1)}, f32[8,128]{1,0:T(8,128)S(1)}, u32[]{:S(2)}, u32[]{:S(2)}) collective-permute-start(f32[8,128]{1,0:T(8,128)S(1)} %get-tuple-element.75.refs_0_), channel_id=1, source_target_pairs={{4,0},{5,1},{6,2},{7,3},{8,4},{9,5},{10,6},{11,7},{12,8},{13,9},{1... | collective-permute-start | bytes 12296 | tf_op jit(solution)/shard_map/ppermute | solution.py:997
  59.9 1.6 %collective-permute-done.11.refs_3_ = f32[8,128]{1,0:T(8,128)S(1)} collective-permute-done((f32[8,128]{1,0:T(8,128)S(1)}, f32[8,128]{1,0:T(8,128)S(1)}, u32[]{:S(2)}, u32[]{:S(2)}) %collective-permute-start.11) | collective-permute-done | bytes 4128 | tf_op jit(solution)/shard_map/ppermute | solution.py:997
  61.4 0.6 collective-permute-done.9.refs_1_
  62.0 1.7 %shard_map.156 = (f32[3,128]{1,0:T(4,128)}, f32[3,128]{1,0:T(4,128)}, f32[3]{0:T(128)}) custom-call(f32[8,128]{1,0:T(8,128)S(1)} %get-tuple-element.75.refs_0_, f32[8,128]{1,0:T(8,128)S(1)} %collective-permute-done.9.refs_1_, f32[8,128]{1,0:T(8,128)S(1)} %collective-permute-done.10.refs_2_, f32[8,128]{1,0:T(8,128)S(1)} %collective-permute-done.11.refs_3_, ...), custom_call_target="tpu_custom_call" | custom-call | flops 1073741824 | bytes 1048576 | tf_op jit(solution)/shard_map/pallas_call | solution.py:838
  (31 shorter events, 0.1 us)
Async XLA Ops:
  0.6 1.1 %copy-start.2 = (bf16[3200,128]{1,0:T(8,128)(2,1)S(1)}, bf16[3200,128]{1,0:T(8,128)(2,1)}, u32[]{:S(2)}) copy-start(bf16[3200,128]{1,0:T(8,128)(2,1)} %feat_hbm.3) | copy-start | bytes 2457604
  1.8 0.7 %copy-start.9 = (f32[3,128]{1,0:T(4,128)S(1)}, f32[3,128]{1,0:T(4,128)}, u32[]{:S(2)}) copy-start(f32[3,128]{1,0:T(4,128)} %refs_8_.1) | copy-start | bytes 4612
  2.5 6.3 %copy-start.3 = (bf16[3200,128]{1,0:T(8,128)(2,1)S(1)}, bf16[3200,128]{1,0:T(8,128)(2,1)}, u32[]{:S(2)}) copy-start(bf16[3200,128]{1,0:T(8,128)(2,1)} %feat_hbm.3) | copy-start | bytes 2457604
  2.5 6.3 %copy-start.4 = (bf16[2,5,128,128]{3,2,1,0:T(8,128)(2,1)S(1)}, bf16[2,5,128,128]{3,2,1,0:T(8,128)(2,1)}, u32[]{:S(2)}) copy-start(bf16[2,5,128,128]{3,2,1,0:T(8,128)(2,1)} %weight_hbm.1) | copy-start | bytes 983044
  2.5 6.3 %copy-start.5 = (bf16[115,512]{1,0:T(8,128)(2,1)S(1)}, bf16[115,512]{1,0:T(8,128)(2,1)}, u32[]{:S(2)}) copy-start(bf16[115,512]{1,0:T(8,128)(2,1)} %frames_hbm.1) | copy-start | bytes 353284
  2.5 6.3 %copy-start.6 = (f32[2,16,128]{2,1,0:T(8,128)S(1)}, f32[2,16,128]{2,1,0:T(8,128)}, u32[]{:S(2)}) copy-start(f32[2,16,128]{2,1,0:T(8,128)} %radial_hbm.1) | copy-start | bytes 49156
  2.5 6.3 %copy-start.7 = (f32[5,128]{1,0:T(8,128)S(1)}, f32[5,128]{1,0:T(8,128)}, u32[]{:S(2)}) copy-start(f32[5,128]{1,0:T(8,128)} %readout_hbm.1) | copy-start | bytes 7684
  2.5 6.3 %copy-start.8 = (s32[4,128]{1,0:T(4,128)S(1)}, s32[4,128]{1,0:T(4,128)}, u32[]{:S(2)}) copy-start(s32[4,128]{1,0:T(4,128)} %nb_hbm.1) | copy-start | bytes 6148
  2.5 6.3 %copy-start.10 = (f32[3,128]{1,0:T(4,128)S(1)}, f32[3,128]{1,0:T(4,128)}, u32[]{:S(2)}) copy-start(f32[3,128]{1,0:T(4,128)} %refs_8_.1) | copy-start | bytes 4612
  2.5 6.3 %copy-start.12 = (s32[128]{0:T(128)S(1)}, s32[128]{0:T(128)}, u32[]{:S(2)}) copy-start(s32[128]{0:T(128)} %param.16) | copy-start | bytes 1540
  2.5 6.3 %copy-start.13 = (f32[3]{0:T(128)S(1)}, f32[3]{0:T(128)}, u32[]{:S(2)}) copy-start(f32[3]{0:T(128)} %refs_9_.1) | copy-start | bytes 40
  3.2 11.3 %collective-permute-start = (bf16[896,128]{1,0:T(8,128)(2,1)S(1)}, bf16[896,128]{1,0:T(8,128)(2,1)S(1)}, u32[]{:S(2)}, u32[]{:S(2)}) collective-permute-start(bf16[896,128]{1,0:T(8,128)(2,1)S(1)} %get-tuple-element.41), channel_id=1, source_target_pairs={{0,1},{1,2},{2,3},{3,4},{4,5},{5,6},{6,7},{7,8},{8,9},{9,10},{10,1... | collective-permute-start | bytes 688136 | tf_op jit(solution)/shard_map/ppermute | solution.py:875
  3.7 10.8 %collective-permute-start.1 = (bf16[896,128]{1,0:T(8,128)(2,1)S(1)}, bf16[896,128]{1,0:T(8,128)(2,1)S(1)}, u32[]{:S(2)}, u32[]{:S(2)}) collective-permute-start(bf16[896,128]{1,0:T(8,128)(2,1)S(1)} %get-tuple-element.42), channel_id=1, source_target_pairs={{1,0},{2,1},{3,2},{4,3},{5,4},{6,5},{7,6},{8,7},{9,8},{10,9},{11,1... | collective-permute-start | bytes 688136 | tf_op jit(solution)/shard_map/ppermute | solution.py:876
  19.9 10.5 %collective-permute-start.2 = (bf16[896,128]{1,0:T(8,128)(2,1)S(1)}, bf16[896,128]{1,0:T(8,128)(2,1)S(1)}, u32[]{:S(2)}, u32[]{:S(2)}) collective-permute-start(bf16[896,128]{1,0:T(8,128)(2,1)S(1)} %get-tuple-element.59), channel_id=1, source_target_pairs={{0,1},{1,2},{2,3},{3,4},{4,5},{5,6},{6,7},{7,8},{8,9},{9,10},{10,1... | collective-permute-start | bytes 688136 | tf_op jit(solution)/shard_map/ppermute | solution.py:875
  20.0 10.5 %collective-permute-start.3 = (bf16[896,128]{1,0:T(8,128)(2,1)S(1)}, bf16[896,128]{1,0:T(8,128)(2,1)S(1)}, u32[]{:S(2)}, u32[]{:S(2)}) collective-permute-start(bf16[896,128]{1,0:T(8,128)(2,1)S(1)} %get-tuple-element.60), channel_id=1, source_target_pairs={{1,0},{2,1},{3,2},{4,3},{5,4},{6,5},{7,6},{8,7},{9,8},{10,9},{11,1... | collective-permute-start | bytes 688136 | tf_op jit(solution)/shard_map/ppermute | solution.py:876
  39.1 9.7 %collective-permute-start.4 = (bf16[896,128]{1,0:T(8,128)(2,1)S(1)}, bf16[896,128]{1,0:T(8,128)(2,1)S(1)}, u32[]{:S(2)}, u32[]{:S(2)}) collective-permute-start(bf16[896,128]{1,0:T(8,128)(2,1)S(1)} %get-tuple-element.69), channel_id=1, source_target_pairs={{0,1},{1,2},{2,3},{3,4},{4,5},{5,6},{6,7},{7,8},{8,9},{9,10},{10,1... | collective-permute-start | bytes 688136 | tf_op jit(solution)/shard_map/ppermute | solution.py:875
  39.2 9.6 %collective-permute-start.5 = (bf16[896,128]{1,0:T(8,128)(2,1)S(1)}, bf16[896,128]{1,0:T(8,128)(2,1)S(1)}, u32[]{:S(2)}, u32[]{:S(2)}) collective-permute-start(bf16[896,128]{1,0:T(8,128)(2,1)S(1)} %get-tuple-element.70), channel_id=1, source_target_pairs={{1,0},{2,1},{3,2},{4,3},{5,4},{6,5},{7,6},{8,7},{9,8},{10,9},{11,1... | collective-permute-start | bytes 688136 | tf_op jit(solution)/shard_map/ppermute | solution.py:876
  43.6 5.2 %copy-start = (f32[3,128]{1,0:T(4,128)S(1)}, f32[3,128]{1,0:T(4,128)}, u32[]{:S(2)}) copy-start(f32[3,128]{1,0:T(4,128)} %velocities_ref.1) | copy-start | bytes 4612
  43.6 5.2 %copy-start.1 = (f32[128]{0:T(128)S(1)}, f32[128]{0:T(128)}, u32[]{:S(2)}) copy-start(f32[128]{0:T(128)} %param.19) | copy-start | bytes 1540
  51.8 10.2 %copy-start.11 = (f32[3,128]{1,0:T(4,128)S(1)}, f32[3,128]{1,0:T(4,128)}, u32[]{:S(2)}) copy-start(f32[3,128]{1,0:T(4,128)} %refs_7_.1) | copy-start | bytes 4612
  51.8 10.2 %copy-start.14 = (f32[3]{0:T(128)S(1)}, f32[3]{0:T(128)}, u32[]{:S(2)}) copy-start(f32[3]{0:T(128)} %refs_10_.1) | copy-start | bytes 40
  51.8 3.1 %collective-permute-start.8 = (f32[8,128]{1,0:T(8,128)S(1)}, f32[8,128]{1,0:T(8,128)S(1)}, u32[]{:S(2)}, u32[]{:S(2)}) collective-permute-start(f32[8,128]{1,0:T(8,128)S(1)} %shard_map.154.refs_0_.refs_4_), channel_id=1, source_target_pairs={{3,0},{0,1},{1,2},{2,3},{7,4},{4,5},{5,6},{6,7},{11,8},{8,9},{9,10... | collective-permute-start | bytes 12296 | tf_op jit(solution)/shard_map/ppermute | solution.py:997
  51.9 3.7 %collective-permute-start.7 = (f32[8,128]{1,0:T(8,128)S(1)}, f32[8,128]{1,0:T(8,128)S(1)}, u32[]{:S(2)}, u32[]{:S(2)}) collective-permute-start(f32[8,128]{1,0:T(8,128)S(1)} %shard_map.154.refs_0_.refs_4_), channel_id=1, source_target_pairs={{2,0},{3,1},{0,2},{1,3},{6,4},{7,5},{4,6},{5,7},{10,8},{11,9},{8,1... | collective-permute-start | bytes 12296 | tf_op jit(solution)/shard_map/ppermute | solution.py:997
  52.0 3.6 %collective-permute-start.6 = (f32[8,128]{1,0:T(8,128)S(1)}, f32[8,128]{1,0:T(8,128)S(1)}, u32[]{:S(2)}, u32[]{:S(2)}) collective-permute-start(f32[8,128]{1,0:T(8,128)S(1)} %shard_map.154.refs_0_.refs_4_), channel_id=1, source_target_pairs={{1,0},{2,1},{3,2},{0,3},{5,4},{6,5},{7,6},{4,7},{9,8},{10,9},{11,1... | collective-permute-start | bytes 12296 | tf_op jit(solution)/shard_map/ppermute | solution.py:997
  56.0 5.5 %collective-permute-start.11 = (f32[8,128]{1,0:T(8,128)S(1)}, f32[8,128]{1,0:T(8,128)S(1)}, u32[]{:S(2)}, u32[]{:S(2)}) collective-permute-start(f32[8,128]{1,0:T(8,128)S(1)} %get-tuple-element.75.refs_0_), channel_id=1, source_target_pairs={{12,0},{13,1},{14,2},{15,3},{0,4},{1,5},{2,6},{3,7},{4,8},{5,9},{6... | collective-permute-start | bytes 12296 | tf_op jit(solution)/shard_map/ppermute | solution.py:997
  56.0 5.4 %collective-permute-start.10 = (f32[8,128]{1,0:T(8,128)S(1)}, f32[8,128]{1,0:T(8,128)S(1)}, u32[]{:S(2)}, u32[]{:S(2)}) collective-permute-start(f32[8,128]{1,0:T(8,128)S(1)} %get-tuple-element.75.refs_0_), channel_id=1, source_target_pairs={{8,0},{9,1},{10,2},{11,3},{12,4},{13,5},{14,6},{15,7},{0,8},{1,9},... | collective-permute-start | bytes 12296 | tf_op jit(solution)/shard_map/ppermute | solution.py:997
  58.4 3.6 %collective-permute-start.9 = (f32[8,128]{1,0:T(8,128)S(1)}, f32[8,128]{1,0:T(8,128)S(1)}, u32[]{:S(2)}, u32[]{:S(2)}) collective-permute-start(f32[8,128]{1,0:T(8,128)S(1)} %get-tuple-element.75.refs_0_), channel_id=1, source_target_pairs={{4,0},{5,1},{6,2},{7,3},{8,4},{9,5},{10,6},{11,7},{12,8},{13,9},{1... | collective-permute-start | bytes 12296 | tf_op jit(solution)/shard_map/ppermute | solution.py:997

commit v4 on v3

--- a/solution.py
+++ b/solution.py
@@ -32,6 +32,8 @@
 LAST = (NCOEF - (GROUPS - 1) * PER_GROUP) * C
 GROUP_ROWS = (PACKED,) * (GROUPS - 1) + (LAST,)
 GRANT = 18
+STEP = 32
+SHORT = 16
 
 F32 = jnp.float32
 BF16 = jnp.bfloat16
@@ -78,20 +80,26 @@
     return high, middle, rest - middle
 
 
+def side_bases():
+    even = lax.rem(lax.axis_index("gx"), 2) == 0
+    return jnp.where(even, OWN, 0), jnp.where(even, 0, OWN)
+
+
+def rim_hits(atom, lane, group):
+    low_base, high_base = side_bases()
+    low = (lane - low_base - GHOST * group == atom) & (atom < GHOST)
+    high = lane - high_base - GHOST * group == atom - (OWN - GHOST)
+    return one_hot(low | (high & (atom >= OWN - GHOST)))
+
+
 def rim_select(group):
-    atom = iota((OWN, 2 * OWN), 0)
-    lane = iota((OWN, 2 * OWN), 1)
-    low = (lane < OWN) & (lane - GHOST * group == atom) & (atom < GHOST)
-    high = (lane >= OWN) & (lane - OWN - GHOST * group == atom - (OWN - GHOST))
-    return one_hot(low | (high & (atom >= OWN - GHOST)))
+    shape = (OWN, 2 * OWN)
+    return rim_hits(iota(shape, 0), iota(shape, 1), group)
 
 
 def rim_place(group):
-    lane = iota((2 * OWN, OWN), 0)
-    atom = iota((2 * OWN, OWN), 1)
-    low = (lane < OWN) & (lane - GHOST * group == atom) & (atom < GHOST)
-    high = (lane >= OWN) & (lane - OWN - GHOST * group == atom - (OWN - GHOST))
-    return one_hot(low | (high & (atom >= OWN - GHOST)))
+    shape = (2 * OWN, OWN)
+    return rim_hits(iota(shape, 1), iota(shape, 0), group)
 
 
 def pack_rims(read_rows, low_ref, high_ref, extra=None):
@@ -182,7 +190,7 @@
         high = gap < -(OWN // 2)
         own_at.append(jnp.where(low | high, -1, place))
         low_at.append(jnp.where(low, place - (OWN - GHOST), -1))
-        high_at.append(jnp.where(high, place + OWN, -1))
+        high_at.append(jnp.where(high, place, -1))
     merge = functools.partial(jnp.concatenate, axis=1)
     return merge(own_at), merge(low_at), merge(high_at)
 
@@ -192,8 +200,9 @@
 
 
 def ghost_one_hot(low_at, high_at, group):
-    at = jnp.maximum(low_at, high_at)
-    at = jnp.where(at >= 0, at + GHOST * group, -1)
+    low_base, high_base = side_bases()
+    at = jnp.where(high_at >= 0, high_at + (high_base + GHOST * group), -1)
+    at = jnp.where(low_at >= 0, low_at + (low_base + GHOST * group), at)
     return one_hot(iota((2 * OWN, EDGES), 0) == at)
 
 
@@ -280,8 +289,8 @@
         out_ref[pl.ds(start, rows), :] = found
 
 
-def twice(values):
-    return jnp.concatenate([values, values], axis=0)
+def tall(values, rows):
+    return jnp.concatenate([values] * (rows // 8), axis=0)
 
 
 def slot_lanes(slot):
@@ -289,45 +298,45 @@
 
 
 def to_frame(picked_ref, wide_ref, out_ref):
-    @pl.loop(0, C // 16)
+    @pl.loop(0, C // STEP)
     def _(step):
-        start = pl.multiple_of(step * 16, 16)
+        start = pl.multiple_of(step * STEP, STEP)
         for slot in range(TILES):
             lanes = slot_lanes(slot)
             for degree, row_count, offset in LAYOUT:
                 size = 2 * degree + 1
                 parts = [
-                    picked_ref[pl.ds((degree * degree + k) * C + start, 16), lanes]
+                    picked_ref[pl.ds((degree * degree + k) * C + start, STEP), lanes]
                     for k in range(size)
                 ]
                 for row in range(row_count):
                     total = None
                     for k in range(size):
-                        term = twice(wide_ref[offset + row * size + k, :, lanes]) * parts[k]
+                        term = tall(wide_ref[offset + row * size + k, :, lanes], STEP) * parts[k]
                         total = term if total is None else total + term
                     at = edge_row(degree, row) * C
-                    out_ref[pl.ds(at + start, 16), lanes] = total.astype(BF16)
+                    out_ref[pl.ds(at + start, STEP), lanes] = total.astype(BF16)
 
 
 def from_frame(frame_rows_ref, wide_ref, out_ref):
-    @pl.loop(0, C // 16)
+    @pl.loop(0, C // STEP)
     def _(step):
-        start = pl.multiple_of(step * 16, 16)
+        start = pl.multiple_of(step * STEP, STEP)
         for slot in range(TILES):
             lanes = slot_lanes(slot)
             for degree, row_count, offset in LAYOUT:
                 size = 2 * degree + 1
                 parts = [
-                    frame_rows_ref[pl.ds(edge_row(degree, row) * C + start, 16), lanes]
+                    frame_rows_ref[pl.ds(edge_row(degree, row) * C + start, STEP), lanes]
                     for row in range(row_count)
                 ]
                 for k in range(size):
                     total = None
                     for row in range(row_count):
-                        term = twice(wide_ref[offset + row * size + k, :, lanes]) * parts[row]
+                        term = tall(wide_ref[offset + row * size + k, :, lanes], STEP) * parts[row]
                         total = term if total is None else total + term
                     at = (degree * degree + k) * C
-                    out_ref[pl.ds(at + start, 16), lanes] = total.astype(BF16)
+                    out_ref[pl.ds(at + start, STEP), lanes] = total.astype(BF16)
 
 
 def build_weights(weight_ref, layer, zero_ref, pair_ref):
@@ -353,14 +362,19 @@
         pair_ref[order - 1, C:, C:] = real
 
 
-def convolve(rows_ref, zero_ref, pair_ref, out_ref):
+def convolve(rows_ref, zero_ref, pair_ref, out_ref, keep_ref=None):
+    def put(rows, found):
+        out_ref[rows, :] = found
+        if keep_ref is not None:
+            keep_ref[rows, :] = found.astype(BF16)
+
     for degree in range(LMAX + 1):
         rows = pl.ds(degree * C, C)
-        out_ref[rows, :] = dot(zero_ref[...], rows_ref[rows, :]).astype(out_ref.dtype)
+        put(rows, dot(zero_ref[...], rows_ref[rows, :]))
     for order in range(1, MMAX + 1):
         for degree in range(order, LMAX + 1):
             rows = pl.ds((ORDER_START[order] + 2 * (degree - order)) * C, 2 * C)
-            out_ref[rows, :] = dot(pair_ref[order - 1], rows_ref[rows, :]).astype(out_ref.dtype)
+            put(rows, dot(pair_ref[order - 1], rows_ref[rows, :]))
 
 
 def radial(distance):
@@ -369,14 +383,24 @@
     return jnp.exp(-(offset * offset)), offset
 
 
-def edge_gate(radial_ref, basis):
-    return lax.dot_general(
-        radial_ref[...],
-        basis,
-        (((0,), (0,)), ((), ())),
-        precision=lax.Precision.HIGHEST,
-        preferred_element_type=F32,
-    )
+FORMER_PARTS = (0, 0, 1, 0, 2, 1)
+LATTER_PARTS = (0, 1, 0, 2, 0, 1)
+
+
+def stack_parts(values, order):
+    parts = split_three(values)
+    rest = C - len(order) * NRBF
+    return jnp.concatenate(
+        [parts[at] for at in order] + [jnp.zeros((rest, values.shape[1]), F32)], axis=0
+    )
+
+
+def gate_weights(radial):
+    return jnp.transpose(stack_parts(radial * KNB ** (-0.5), FORMER_PARTS)).astype(BF16)
+
+
+def edge_gate(gate_weight_ref, basis):
+    return dot(gate_weight_ref[...], stack_parts(basis, LATTER_PARTS).astype(BF16))
 
 
 def distance_slope(radial_ref, gate_slope, distance):
@@ -384,52 +408,56 @@
     basis_slope = jnp.dot(
         radial_ref[...], gate_slope, precision=lax.Precision.HIGHEST, preferred_element_type=F32
     )
-    terms = basis_slope * basis * offset * (-2.0 / RADIAL_SPREAD)
+    terms = basis_slope * basis * offset * (-2.0 * KNB ** (-0.5) / RADIAL_SPREAD)
     return jnp.sum(terms, axis=0, keepdims=True)
 
 
-def message_rows(degree, row_count, offset, start, turned_ref, gate_ref, wide_ref):
+def message_rows(
+    degree, row_count, offset, start, size_rows, turned_ref, gate_ref, wide_ref
+):
     size = 2 * degree + 1
     sums = [None] * size
     for slot in range(TILES):
         lanes = slot_lanes(slot)
-        gate = gate_ref[pl.ds(start, 16), lanes]
+        gate = gate_ref[pl.ds(start, size_rows), lanes]
         for row in range(row_count):
-            gated = turned_ref[pl.ds(edge_row(degree, row) * C + start, 16), lanes] * gate
+            gated = turned_ref[pl.ds(edge_row(degree, row) * C + start, size_rows), lanes] * gate
             for k in range(size):
-                term = twice(wide_ref[offset + row * size + k, :, lanes]) * gated
+                term = tall(wide_ref[offset + row * size + k, :, lanes], size_rows) * gated
                 sums[k] = term if sums[k] is None else sums[k] + term
     return [fold_slots(total) for total in sums]
 
 
-def slope_rows(degree, row_count, offset, row, lanes, slopes, wide_ref):
+def slope_rows(degree, offset, row, lanes, slopes, wide_ref):
     size = 2 * degree + 1
+    size_rows = slopes[0].shape[0]
     total = None
     for k in range(size):
-        term = twice(wide_ref[offset + row * size + k, :, lanes]) * slopes[k]
+        term = tall(wide_ref[offset + row * size + k, :, lanes], size_rows) * slopes[k]
         total = term if total is None else total + term
     return total
 
 
-def layer_forward(picked_ref, wide_ref, rows_ref, zero_ref, pair_ref, turned_ref):
+def layer_forward(
+    picked_ref, wide_ref, rows_ref, zero_ref, pair_ref, turned_ref, keep_ref=None
+):
     to_frame(picked_ref, wide_ref, rows_ref)
-    convolve(rows_ref, zero_ref, pair_ref, turned_ref)
-
-
-def add_messages(base_ref, half, turned_ref, gate_ref, wide_ref, hidden_ref, keep_ref):
-    @pl.loop(0, C // 16)
+    convolve(rows_ref, zero_ref, pair_ref, turned_ref, keep_ref)
+
+
+def add_messages(base_ref, half, turned_ref, gate_ref, wide_ref, hidden_ref):
+    @pl.loop(0, C // STEP, unroll=2)
     def _(step):
-        start = pl.multiple_of(step * 16, 16)
-        held = inside((16, OWN), half)
+        start = pl.multiple_of(step * STEP, STEP)
+        held = inside((STEP, OWN), half)
         for degree, row_count, offset in LAYOUT:
-            sums = message_rows(degree, row_count, offset, start, turned_ref, gate_ref, wide_ref)
+            sums = message_rows(
+                degree, row_count, offset, start, STEP, turned_ref, gate_ref, wide_ref
+            )
             for k, total in enumerate(sums):
-                rows = pl.ds((degree * degree + k) * C + start, 16)
-                added = jnp.where(held, total * KNB ** (-0.5), 0.0)
-                hidden_ref[rows, :] = (base_ref[rows, :].astype(F32) + added).astype(BF16)
-        for row in range(EDGE_ROWS):
-            rows = pl.ds(row * C + start, 16)
-            keep_ref[rows, :] = turned_ref[rows, :].astype(BF16)
+                rows = pl.ds((degree * degree + k) * C + start, STEP)
+                base = base_ref[rows, :].astype(F32)
+                hidden_ref[rows, :] = jnp.where(held, base + total, base).astype(BF16)
 
 
 def edge_geometry(source, shift, target, edge_ref):
@@ -448,11 +476,12 @@
 
 def first_inner_kernel(
     feat_hbm, frames_hbm, nb_hbm, counts_hbm, pos_hbm, box_hbm, weight_hbm, radial_hbm,
-    readout_hbm,
+    readout_hbm, control_hbm,
     hidden_ref, keep_ref, edge_ref, own_ref, inner_wide_ref, rim_wide_ref, inner_hot_ref,
     rim_hot_ref, ghost_hot_ref, index_ref, target_ref, parts_out_ref, zero_ref, pair_ref,
-    radial_ref, readout_wide_ref,
+    radial_ref, gate_weight_ref, readout_wide_ref, consts_ref,
     feat_ref, frames_ref, nb_ref, counts_ref, pos_ref, box_ref, weight_ref, readout_ref,
+    control_ref,
     parts_ref, picked_ref, rows_ref, turned_ref, gate_ref, sems,
 ):
     fetch(
@@ -460,6 +489,7 @@
             (nb_hbm, nb_ref), (counts_hbm, counts_ref), (pos_hbm, pos_ref),
             (box_hbm, box_ref), (frames_hbm, frames_ref), (radial_hbm, radial_ref),
             (feat_hbm, feat_ref), (weight_hbm, weight_ref), (readout_hbm, readout_ref),
+            (control_hbm, control_ref),
         ],
         sems,
     )
@@ -475,14 +505,23 @@
     positions = parts_ref[0:8, :]
     target = jnp.concatenate([both_lanes(positions, INNER)] * TILES, axis=1)
     distance = edge_geometry(join_parts(dot(parts, inner_hot_ref[...])), None, target, edge_ref)
-    gate_ref[...] = edge_gate(radial_ref.at[0], radial(distance)[0])
+    for layer in range(2):
+        gate_weight_ref[layer] = gate_weights(radial_ref[layer])
+    gate_ref[...] = edge_gate(gate_weight_ref.at[0], radial(distance)[0])
     build_weights(weight_ref, 0, zero_ref.at[0], pair_ref.at[0])
     normalise_own(feat_ref, own_ref)
     gather(own_ref, inner_hot_ref, picked_ref)
     layer_forward(
-        picked_ref, inner_wide_ref, rows_ref, zero_ref.at[0], pair_ref.at[0], turned_ref
-    )
-    add_messages(feat_ref, INNER, turned_ref, gate_ref, inner_wide_ref, hidden_ref, keep_ref)
+        picked_ref, inner_wide_ref, rows_ref, zero_ref.at[0], pair_ref.at[0], turned_ref,
+        keep_ref,
+    )
+    add_messages(feat_ref, INNER, turned_ref, gate_ref, inner_wide_ref, hidden_ref)
+    row = iota((8, OWN), 0)
+    consts = jnp.zeros((8, OWN), F32)
+    for at in range(3):
+        consts = jnp.where(row == at, box_ref[at], consts)
+        consts = jnp.where(row == 3 + at, control_ref[at], consts)
+    consts_ref[...] = consts
     half_frames(frames_ref, counts, RIM, rim_wide_ref)
     own_at, low_at, high_at = edge_sources(nb_ref, RIM)
     index_ref[0:1, EDGES:] = own_at
@@ -501,12 +540,12 @@
     build_back_weights(weight_ref, 1, zero_ref.at[2], pair_ref.at[2])
     for degree in range(LMAX + 1):
         row = jnp.broadcast_to(readout_ref[degree : degree + 1, :], (C, C))
-        readout_wide_ref[degree] = jnp.transpose(row) * (1.0 / (2 * degree + 1))
+        readout_wide_ref[degree] = jnp.transpose(row) * (2.0 / (2 * degree + 1))
 
 
 def first_rim_kernel(
     base_ref, low_ref, high_ref, own_ref, wide_ref, own_hot_ref, ghost_hot_ref, target_ref,
-    parts_ref, zero_ref, pair_ref, radial_ref,
+    parts_ref, zero_ref, pair_ref, gate_weight_ref,
     hidden_ref, keep_ref, edge_ref, send_low_ref, send_high_ref,
     ghost_ref, picked_ref, rows_ref, turned_ref, gate_ref,
 ):
@@ -516,11 +555,13 @@
     found = dot(parts_ref[...], own_hot_ref[...]) + dot(ghosts, ghost_hot_ref[GROUPS - 1])
     target = jnp.where(iota((8, EDGES), 0) == 3, 0.0, target_ref[...])
     distance = edge_geometry(join_parts(found), target_ref[3:4, :], target, edge_ref)
-    gate_ref[...] = edge_gate(radial_ref.at[0], radial(distance)[0])
+    gate_ref[...] = edge_gate(gate_weight_ref.at[0], radial(distance)[0])
     normalise_ghosts(low_ref, high_ref, ghost_ref)
     gather(own_ref, own_hot_ref, picked_ref, ghost_ref, ghost_hot_ref)
-    layer_forward(picked_ref, wide_ref, rows_ref, zero_ref.at[0], pair_ref.at[0], turned_ref)
-    add_messages(base_ref, RIM, turned_ref, gate_ref, wide_ref, hidden_ref, keep_ref)
+    layer_forward(
+        picked_ref, wide_ref, rows_ref, zero_ref.at[0], pair_ref.at[0], turned_ref, keep_ref
+    )
+    add_messages(base_ref, RIM, turned_ref, gate_ref, wide_ref, hidden_ref)
     pack_rims(lambda start, size: hidden_ref[pl.ds(start, size), :], send_low_ref, send_high_ref)
 
 
@@ -528,29 +569,31 @@
     hidden_ref, half, turned_ref, gate_ref, wide_ref, readout_wide_ref, upper_ref,
     turned_slope_ref, gate_slope_ref,
 ):
-    @pl.loop(0, C // 16)
+    @pl.loop(0, C // SHORT)
     def _(step):
-        start = pl.multiple_of(step * 16, 16)
-        channels = pl.ds(start, 16)
+        start = pl.multiple_of(step * SHORT, SHORT)
+        channels = pl.ds(start, SHORT)
         gate_slopes = [None] * TILES
         for degree, row_count, offset in LAYOUT:
-            sums = message_rows(degree, row_count, offset, start, turned_ref, gate_ref, wide_ref)
+            sums = message_rows(
+                degree, row_count, offset, start, SHORT, turned_ref, gate_ref, wide_ref
+            )
             weight = readout_wide_ref[degree, channels, :]
             slopes = []
             for k, total in enumerate(sums):
-                rows = pl.ds((degree * degree + k) * C + start, 16)
+                rows = pl.ds((degree * degree + k) * C + start, SHORT)
                 below = both_lanes(hidden_ref[rows, :].astype(F32), half)
-                slope = (below + total * KNB ** (-0.5)) * weight
-                upper_ref[rows, :] = slope * 2.0
-                slopes.append(slope * (2.0 * KNB ** (-0.5)))
+                slope = (below + total) * weight
+                upper_ref[rows, :] = slope
+                slopes.append(slope)
             for slot in range(TILES):
                 lanes = slot_lanes(slot)
                 gate = gate_ref[channels, lanes]
                 for row in range(row_count):
                     slope = slope_rows(
-                        degree, row_count, offset, row, lanes, slopes, wide_ref
+                        degree, offset, row, lanes, slopes, wide_ref
                     )
-                    rows = pl.ds(edge_row(degree, row) * C + start, 16)
+                    rows = pl.ds(edge_row(degree, row) * C + start, SHORT)
                     term = turned_ref[rows, lanes] * slope
                     before = gate_slopes[slot]
                     gate_slopes[slot] = term if before is None else before + term
@@ -565,13 +608,13 @@
 
 
 def second_inner_kernel(
-    hidden_ref, wide_ref, own_hot_ref, edge_ref, zero_ref, pair_ref, radial_ref,
+    hidden_ref, wide_ref, own_hot_ref, edge_ref, zero_ref, pair_ref, radial_ref, gate_weight_ref,
     readout_wide_ref,
     own_ref, scale_ref, upper_ref, turned_slope_ref, slope_ref,
     picked_ref, rows_ref, turned_ref, gate_ref, gate_slope_ref,
 ):
     distance = edge_ref[3:4, :]
-    gate_ref[...] = edge_gate(radial_ref.at[1], radial(distance)[0])
+    gate_ref[...] = edge_gate(gate_weight_ref.at[1], radial(distance)[0])
     scale_ref[...] = jnp.broadcast_to(normalise_own(hidden_ref, own_ref), (8, OWN))
     gather(own_ref, own_hot_ref, picked_ref)
     layer_forward(picked_ref, wide_ref, rows_ref, zero_ref.at[1], pair_ref.at[1], turned_ref)
@@ -592,13 +635,13 @@
 
 def second_rim_kernel(
     hidden_ref, low_ref, high_ref, own_ref, wide_ref, own_hot_ref, ghost_hot_ref, edge_ref,
-    zero_ref, pair_ref, radial_ref, readout_wide_ref,
+    zero_ref, pair_ref, radial_ref, gate_weight_ref, readout_wide_ref,
     upper_ref, slope_ref, own_slope_ref, send_low_ref, send_high_ref,
     ghost_ref, picked_ref, rows_ref, turned_ref, gate_ref, gate_slope_ref, turned_slope_ref,
     edge_slope_ref, ghost_slope_ref,
 ):
     distance = edge_ref[3:4, :]
-    gate_ref[...] = edge_gate(radial_ref.at[1], radial(distance)[0])
+    gate_ref[...] = edge_gate(gate_weight_ref.at[1], radial(distance)[0])
     ghost_scale = normalise_ghosts(low_ref, high_ref, ghost_ref)
     gather(own_ref, own_hot_ref, picked_ref, ghost_ref, ghost_hot_ref)
     layer_forward(picked_ref, wide_ref, rows_ref, zero_ref.at[1], pair_ref.at[1], turned_ref)
@@ -632,14 +675,14 @@
 
 
 def gate_slopes_back(hidden_slope_ref, half, wide_ref, keep_ref, gate_slope_ref):
-    @pl.loop(0, C // 16)
+    @pl.loop(0, C // STEP, unroll=2)
     def _(step):
-        start = pl.multiple_of(step * 16, 16)
+        start = pl.multiple_of(step * STEP, STEP)
         gate_slopes = [None] * TILES
         for degree, row_count, offset in LAYOUT:
             slopes = [
                 both_lanes(
-                    hidden_slope_ref[pl.ds((degree * degree + k) * C + start, 16), :], half
+                    hidden_slope_ref[pl.ds((degree * degree + k) * C + start, STEP), :], half
                 )
                 for k in range(2 * degree + 1)
             ]
@@ -647,14 +690,14 @@
                 lanes = slot_lanes(slot)
                 for row in range(row_count):
                     slope = slope_rows(
-                        degree, row_count, offset, row, lanes, slopes, wide_ref
+                        degree, offset, row, lanes, slopes, wide_ref
                     )
-                    rows = pl.ds(edge_row(degree, row) * C + start, 16)
+                    rows = pl.ds(edge_row(degree, row) * C + start, STEP)
                     term = keep_ref[rows, lanes].astype(F32) * slope
                     before = gate_slopes[slot]
                     gate_slopes[slot] = term if before is None else before + term
         for slot in range(TILES):
-            gate_slope_ref[pl.ds(start, 16), slot_lanes(slot)] = gate_slopes[slot]
+            gate_slope_ref[pl.ds(start, STEP), slot_lanes(slot)] = gate_slopes[slot]
 
 
 def edge_pulls(radial_ref, gate_slope_ref, edge_ref, second_slope_ref, half):
@@ -698,7 +741,7 @@
         rows = pl.ds(coef * C, C)
         upper = jnp.where(held, inner_upper_ref[rows, :], rim_upper_ref[rows, :])
         total = upper + slope_ref[rows, :] * scale - hidden_ref[rows, :].astype(F32) * along
-        slope_ref[rows, :] = total * KNB ** (-0.5)
+        slope_ref[rows, :] = total
     gate_slopes_back(slope_ref, INNER, wide_ref, keep_ref, gate_slope_ref)
     parts, on_target, virial = edge_pulls(
         radial_ref.at[0], gate_slope_ref, edge_ref, second_slope_ref, INNER
@@ -716,16 +759,14 @@
     for group, rows in enumerate(GROUP_ROWS):
         block = pl.ds(group * PACKED, rows)
         back = jnp.concatenate([low_ref[pl.ds(0, rows), :], high_ref[pl.ds(0, rows), :]], axis=1)
-        added = dot(back, rim_place(group)) * KNB ** (-0.5)
-        hidden_slope_ref[block, :] = slope_ref[block, :] + added
+        hidden_slope_ref[block, :] = slope_ref[block, :] + dot(back, rim_place(group))
     gate_slopes_back(hidden_slope_ref, RIM, wide_ref, keep_ref, gate_slope_ref)
     parts, on_target, virial = edge_pulls(
         radial_ref.at[0], gate_slope_ref, edge_ref, second_slope_ref, RIM
     )
     landed = join_parts(dot(parts, spread(own_hot_ref[...]))) - on_target + part_ref[...]
     low_at, high_at = index_ref[1:2, EDGES:], index_ref[2:3, EDGES:]
-    rim_at = jnp.where(low_at >= 0, low_at + (OWN - GHOST), high_at - OWN)
-    rim_at = jnp.where((low_at >= 0) | (high_at >= 0), rim_at, -1)
+    rim_at = jnp.where(low_at >= 0, low_at + (OWN - GHOST), high_at)
     outward = -join_parts(dot(parts, spread(own_one_hot(rim_at))))
     virial = virial + part_ref[7:8, :]
     masses = masses_ref[...]
@@ -765,7 +806,7 @@
     ordered = []
     for run in range(ways):
         chosen = tiles[0]
-        step = lax.rem(run - digit + ways, ways)
+        step = digit ^ run if ways in (2, 4) else lax.rem(run - digit + ways, ways)
         for far in range(1, ways):
             chosen = jnp.where(step == far, tiles[far], chosen)
         ordered.append(chosen)
@@ -789,9 +830,9 @@
 
 def finish_kernel(width, ways, first_round, *refs):
     (
-        masses_ref, noise_ref, positions_ref, box_ref, control_ref,
+        masses_ref, noise_ref, positions_ref, consts_ref,
         fractional_ref, velocities_ref, new_box_ref,
-    ) = refs[-8:]
+    ) = refs[-7:]
     tiles = [ref[...] for ref in refs[:ways]]
     start = tiles[0] if first_round else refs[ways][...]
     caught = jnp.zeros((8, OWN), F32) if first_round else refs[ways + 1][...]
@@ -802,28 +843,22 @@
     caught = jnp.where((lane < GHOST) & (place == 0), merged, caught)
     strain = merged[7:8] + join_tiles(merged, merged)
     kicked = (start + start[3:4] * pltpu.roll(caught, 4, 0))[0:3]
-    row = iota((3, OWN), 0)
-    box = jnp.where(row == 0, box_ref[0], jnp.where(row == 1, box_ref[1], box_ref[2]))
-    volume = box_ref[0] * box_ref[1] * box_ref[2]
+    box = consts_ref[0:3, :]
+    temperature, coupling, wanted = (consts_ref[at : at + 1, :] for at in (3, 4, 5))
+    volume = consts_ref[0:1, :] * consts_ref[1:2, :] * consts_ref[2:3, :]
     pressure = strain / (3.0 * volume)
-    rescale = jnp.exp(control_ref[1] * (pressure - control_ref[2]) / 3.0)
-    kick = jnp.sqrt((1.0 - FRICTION * FRICTION) * control_ref[0] / masses_ref[...])
+    rescale = jnp.exp(coupling * (pressure - wanted) / 3.0)
+    kick = jnp.sqrt((1.0 - FRICTION * FRICTION) * temperature / masses_ref[...])
     thermal = FRICTION * kicked + kick * noise_ref[...]
     fractional_ref[...] = (positions_ref[...] + STEP_TIME * thermal) / box
     velocities_ref[...] = thermal / rescale
-    scale = rescale[0, 0]
+    scaled = box * rescale
     for side in range(3):
-        new_box_ref[side] = box_ref[side] * scale
-
-
-SMALL = ("box", "control")
+        new_box_ref[side] = scaled[side, 0]
 
 
 def call(kernel, outs, scratch, args, grant=GRANT, hbm=False, cost=1):
-    def space(name):
-        if hbm:
-            return pltpu.HBM
-        return pltpu.SMEM if name in SMALL else pltpu.VMEM
+    space = pltpu.HBM if hbm else pltpu.VMEM
 
     def buffer(entry):
         return entry if len(entry) == 3 else entry + (pltpu.VMEM,)
@@ -838,7 +873,7 @@
     return pl.pallas_call(
         kernel,
         out_shape=[jax.ShapeDtypeStruct(shape, kind) for shape, kind in outs],
-        in_specs=[pl.BlockSpec(memory_space=space(name)) for name in args],
+        in_specs=[pl.BlockSpec(memory_space=space) for _ in args],
         out_specs=[
             pl.BlockSpec(memory_space=pltpu.SMEM if len(shape) == 1 else pltpu.VMEM)
             for shape, kind in outs
@@ -868,13 +903,14 @@
 ):
     assert positions.shape[1] == OWN
     count = lax.axis_size("gx")
-    forward = [(i, (i + 1) % count) for i in range(count)]
-    backward = [(target, source) for source, target in forward]
-
-    def exchange(to_low, to_high):
-        from_low = lax.ppermute(to_high, "gx", forward)
-        from_high = lax.ppermute(to_low, "gx", backward)
-        return from_low, from_high
+    assert count % 2 == 0
+    within = [(i, i ^ 1) for i in range(count)]
+    across = [(i, (i + 2 * (i % 2) - 1) % count) for i in range(count)]
+
+    def exchange(to_first, to_second):
+        from_second = lax.ppermute(to_second, "gx", across)
+        from_first = lax.ppermute(to_first, "gx", within)
+        return from_first, from_second
 
     packed = ((PACKED, OWN), BF16)
     own_rows = ((ROWS, OWN), BF16)
@@ -902,24 +938,25 @@
     from_low, from_high = exchange(to_low, to_high)
     (
         hidden, keep_inner, edge_inner, own, wide_inner, wide_rim, hot_inner, hot_rim,
-        hot_ghost, index, target, own_parts, zero, pair, radial_rows, readout_wide,
+        hot_ghost, index, target, own_parts, zero, pair, radial_rows, gate_weight,
+        readout_wide, consts,
     ) = call(
         first_inner_kernel,
         [
             own_rows, kept, edge, own_rows, wide, wide, hot, hot,
             ((GROUPS, 2 * OWN, EDGES), BF16), ((8, 2 * EDGES), jnp.int32), edge,
             ((32, OWN), BF16), ((3, C, C), BF16), ((3, MMAX, 2 * C, 2 * C), BF16),
-            (radial_weight.shape, F32), ((LMAX + 1, C, C), F32),
+            (radial_weight.shape, F32), ((2, C, C), BF16), ((LMAX + 1, C, C), F32), small,
         ],
         [
             own_rows, (frames.shape, BF16), ((KNB, OWN), jnp.int32), ((1, OWN), jnp.int32),
             place, ((3,), F32, pltpu.SMEM), (conv_weight.shape, BF16), (readout.shape, F32),
-            parts, picked, kept, turned, gate, 9,
+            ((3,), F32, pltpu.SMEM), parts, picked, kept, turned, gate, 10,
         ],
         dict(
             feat=node_feat, frames=frames, neighbours=neighbours, counts=counts[None, :],
             positions=positions, box=box_lengths, weight=conv_weight, radial=radial_weight,
-            readout=readout,
+            readout=readout, control=control,
         ),
         hbm=True,
         cost=5,
@@ -931,7 +968,7 @@
         dict(
             base=hidden, low=from_low, high=from_high, own=own, wide=wide_rim, hot=hot_rim,
             ghost_hot=hot_ghost, target=target, parts=own_parts, zero=zero, pair=pair,
-            radial=radial_rows,
+            gate_weight=gate_weight,
         ),
     )
     from_low, from_high = exchange(to_low, to_high)
@@ -941,7 +978,7 @@
         [picked, kept, turned, gate, gate],
         dict(
             hidden=hidden, wide=wide_inner, hot=hot_inner, edge=edge_inner, zero=zero,
-            pair=pair, radial=radial_rows, readout=readout_wide,
+            pair=pair, radial=radial_rows, gate_weight=gate_weight, readout=readout_wide,
         ),
         cost=5,
     )
@@ -955,7 +992,7 @@
         dict(
             hidden=hidden, low=from_low, high=from_high, own=own, wide=wide_rim, hot=hot_rim,
             ghost_hot=hot_ghost, edge=edge_rim, zero=zero, pair=pair, radial=radial_rows,
-            readout=readout_wide,
+            gate_weight=gate_weight, readout=readout_wide,
         ),
     )
     from_low, from_high = exchange(to_low, to_high)
@@ -992,7 +1029,8 @@
             pairs = []
             for target in range(count):
                 digit = target // width % ways
-                source = target + ((digit + far) % ways - digit) * width
+                other = digit ^ far if ways in (2, 4) else (digit + far) % ways
+                source = target + (other - digit) * width
                 pairs.append((source, target))
             tiles["tile%d" % far] = lax.ppermute(tile, "gx", pairs)
         if caught is not None:
@@ -1012,7 +1050,7 @@
         [],
         dict(
             tiles, masses=mass_row, noise=thermal_noise, positions=positions,
-            box=box_lengths, control=control,
+            consts=consts,
         ),
         grant=1,
     )

time: 64 us -> 61.3 us (0.958)
  starting transfers between devices: 20.2 us -> 17.5 us
  Pallas kernels: 36.6 us -> 34.5 us
  waiting for transfers between devices: 4.07 us -> 6.17 us
    ppermute x6, starting transfers between devices: 14.5 us -> 11.1 us  [the longest x3 10.4 us: exchange(): from_second = lax.ppermute(to_second, 'gx', across)]
    pallas_call x9, Pallas kernels: 36.6 us -> 34.5 us  [call(): pl.pallas_call(kernel, out_shape=[jax.ShapeDtypeStruct(shape, kind) for s...]
    ppermute x6, waiting for transfers between devices: 0.02 us -> 1.57 us  [the longest x3 1.56 us: exchange(): from_second = lax.ppermute(to_second, 'gx', across)]
    ppermute x6, starting transfers between devices: 5.69 us -> 6.39 us  [shards(): tiles['tile%d' % far] = lax.ppermute(tile, 'gx', pairs)]
  transfers between devices with their start and end apart: 12 -> 12, of which waited for: 4 -> 6; matrix products, arithmetic and copies ran while one was open for 0% -> 0% of each run, Pallas kernels for 26% -> 26%
where the time goes in v4:
time: 61.3 us; the launch traced here: 61.1 us
  Pallas kernels  34.5 us (56%)
  starting transfers between devices  17.5 us (29%)
  waiting for transfers between devices  6.17 us (10%)
  local copies, waits for them, and re-layouts  1.87 us (3%)
  between operations  1.03 us (2%)
    pallas_call x9, Pallas kernels, call(): pl.pallas_call(kernel, out_shape=[jax.ShapeDtypeStruct(shape, kind) for s...  34.5 us
    ppermute x3, starting transfers between devices, exchange(): from_second = lax.ppermute(to_second, 'gx', across)  10.4 us
    ppermute x6, starting transfers between devices, shards(): tiles['tile%d' % far] = lax.ppermute(tile, 'gx', pairs)  6.39 us
    ppermute x6, waiting for transfers between devices, shards(): tiles['tile%d' % far] = lax.ppermute(tile, 'gx', pairs)  4.6 us
    unnamed x30, local copies, waits for them, and re-layouts  1.87 us
    ppermute x3, waiting for transfers between devices, exchange(): from_second = lax.ppermute(to_second, 'gx', across)  1.56 us
  transfers between devices with their start and end apart: 12, of which 6 were waited for; matrix products, arithmetic and copies ran while one was open for 0% of the time, Pallas kernels for 26%

profile of v4, /device:TPU:0, one launch (start us, length us, event | category | flops | bytes accessed | tf_op | source)
XLA Modules:
  0.0 61.1 jit_solution(13867204446344535626)
XLA Ops:
  0.6 1.1 %copy-done.2 = bf16[3200,128]{1,0:T(8,128)(2,1)S(1)} copy-done((bf16[3200,128]{1,0:T(8,128)(2,1)S(1)}, bf16[3200,128]{1,0:T(8,128)(2,1)}, u32[]{:S(2)}) %copy-start.2) | copy-done | bytes 819224
  1.8 0.7 %copy-done.9 = f32[3,128]{1,0:T(4,128)S(1)} copy-done((f32[3,128]{1,0:T(4,128)S(1)}, f32[3,128]{1,0:T(4,128)}, u32[]{:S(2)}) %copy-start.9) | copy-done | bytes 1560
  2.5 0.7 %shard_map.149 = (bf16[896,128]{1,0:T(8,128)(2,1)S(1)}, bf16[896,128]{1,0:T(8,128)(2,1)S(1)}) custom-call(bf16[3200,128]{1,0:T(8,128)(2,1)S(1)} %copy-done.2, f32[3,128]{1,0:T(4,128)S(1)} %copy-done.9), custom_call_target="tpu_custom_call" | custom-call | flops 1073741824 | bytes 1048576 | tf_op jit(solution)/shard_map/pallas_call | solution.py:873
  3.3 0.5 collective-permute-start
  3.8 5.7 %collective-permute-start.1 = (bf16[896,128]{1,0:T(8,128)(2,1)S(1)}, bf16[896,128]{1,0:T(8,128)(2,1)S(1)}, u32[]{:S(2)}, u32[]{:S(2)}) collective-permute-start(bf16[896,128]{1,0:T(8,128)(2,1)S(1)} %get-tuple-element.44), channel_id=1, source_target_pairs={{0,15},{1,2},{2,1},{3,4},{4,3},{5,6},{6,5},{7,8},{8,7},{9,10},{10,... | collective-permute-start | bytes 688136 | tf_op jit(solution)/shard_map/ppermute | solution.py:911
  9.5 5.6 %shard_map.148 = (bf16[3200,128]{1,0:T(8,128)(2,1)S(1)}, bf16[2432,256]{1,0:T(8,128)(2,1)S(1)}, f32[8,256]{1,0:T(8,128)S(1)}, bf16[3200,128]{1,0:T(8,128)(2,1)S(...) custom-call(bf16[3200,128]{1,0:T(8,128)(2,1)S(1)} %copy-done.3, ...), custom_call_target="tpu_custom_call" | custom-call | flops 5368709120 | bytes 1048576 | tf_op jit(solution)/shard_map/pallas_call | solution.py:873
  15.2 0.0 collective-permute-done.1.high_ref
  15.2 5.0 %shard_map.150 = (bf16[3200,128]{1,0:T(8,128)(2,1)S(1)}, bf16[2432,256]{1,0:T(8,128)(2,1)S(1)}, f32[8,256]{1,0:T(8,128)S(1)}, bf16[896,128]{1,0:T(8,128)(2,1)S(1)}, bf16[896,128]{1,0:T(8,128)(2,1)S(1)}) custom-call(bf16[3200,128]{1,0:T(8,128)(2,1)S(1)} %get-tuple-element.42.base_ref, bf16[896,128]{1,0:T(8,128)(2,1)S(1)} %collective-permute-done.low_ref, ...), custom_call_target="tpu_custom_call" | custom-call | flops 1073741824 | bytes 1048576 | tf_op jit(solution)/shard_map/pallas_call | solution.py:873
  20.2 0.1 collective-permute-start.2
  20.2 2.5 %collective-permute-start.3 = (bf16[896,128]{1,0:T(8,128)(2,1)S(1)}, bf16[896,128]{1,0:T(8,128)(2,1)S(1)}, u32[]{:S(2)}, u32[]{:S(2)}) collective-permute-start(bf16[896,128]{1,0:T(8,128)(2,1)S(1)} %get-tuple-element.63), channel_id=1, source_target_pairs={{0,15},{1,2},{2,1},{3,4},{4,3},{5,6},{6,5},{7,8},{8,7},{9,10},{10,... | collective-permute-start | bytes 688136 | tf_op jit(solution)/shard_map/ppermute | solution.py:911
  22.7 5.6 %shard_map.151 = (bf16[3200,128]{1,0:T(8,128)(2,1)S(1)}, f32[8,128]{1,0:T(8,128)S(1)}, f32[3200,128]{1,0:T(8,128)S(1)}, bf16[2432,256]{1,0:T(8,128)(2,1)S(1)}, f32[8,256]{1,0:T(8,128)S(1)}) custom-call(bf16[3200,128]{1,0:T(8,128)(2,1)S(1)} %get-tuple-element.54.hidden_ref, f32[115,8,256]{2,1,0:T(8,128)S(1)} %get-tuple-element.55.wide_ref, ...), custom_call_target="tpu_custom_call" | custom-call | flops 5368709120 | bytes 1048576 | tf_op jit(solution)/shard_map/pallas_call | solution.py:873
  28.3 0.0 collective-permute-done.2.low_ref
  28.3 0.2 collective-permute-done.3.high_ref
  28.5 8.8 %shard_map.152 = (f32[3200,128]{1,0:T(8,128)S(1)}, f32[8,256]{1,0:T(8,128)S(1)}, f32[3200,128]{1,0:T(8,128)S(1)}, bf16[896,128]{1,0:T(8,128)(2,1)S(1)}, bf16[896,128]{1,0:T(8,128)(2,1)S(1)}) custom-call(bf16[3200,128]{1,0:T(8,128)(2,1)S(1)} %get-tuple-element.54.hidden_ref, bf16[896,128]{1,0:T(8,128)(2,1)S(1)} %collective-permute-done.2.low_ref, ...), custom_call_target="tpu_custom_call" | custom-call | flops 1073741824 | bytes 1048576 | tf_op jit(solution)/shard_map/pallas_call | solution.py:873
  37.4 0.1 collective-permute-start.4
  37.5 2.3 %collective-permute-start.5 = (bf16[896,128]{1,0:T(8,128)(2,1)S(1)}, bf16[896,128]{1,0:T(8,128)(2,1)S(1)}, u32[]{:S(2)}, u32[]{:S(2)}) collective-permute-start(bf16[896,128]{1,0:T(8,128)(2,1)S(1)} %get-tuple-element.73), channel_id=1, source_target_pairs={{0,15},{1,2},{2,1},{3,4},{4,3},{5,6},{6,5},{7,8},{8,7},{9,10},{10,... | collective-permute-start | bytes 688136 | tf_op jit(solution)/shard_map/ppermute | solution.py:911
  39.8 4.6 %shard_map.153 = (f32[3200,128]{1,0:T(8,128)S(1)}, f32[8,128]{1,0:T(8,128)S(1)}) custom-call(bf16[3200,128]{1,0:T(8,128)(2,1)S(1)} %get-tuple-element.54.hidden_ref, f32[8,128]{1,0:T(8,128)S(1)} %get-tuple-element.60.scale_ref, f32[3200,128]{1,0:T(8,128)S(1)} %get-tuple-element.61.inner_upper_ref, f32[3200,128]{1,0:T(8,128)S(1)} %get-tuple-element.66.rim_upper_ref, ...), custom_call_target="tpu_custom_call" | custom-call | flops 5368709120 | bytes 1048576 | tf_op jit(solution)/shard_map/pallas_call | solution.py:873
  44.4 1.3 %collective-permute-done.5.high_ref = bf16[896,128]{1,0:T(8,128)(2,1)S(1)} collective-permute-done((bf16[896,128]{1,0:T(8,128)(2,1)S(1)}, bf16[896,128]{1,0:T(8,128)(2,1)S(1)}, u32[]{:S(2)}, u32[]{:S(2)}) %collective-permute-start.5) | collective-permute-done | bytes 229408 | tf_op jit(solution)/shard_map/ppermute | solution.py:911
  45.8 2.6 %shard_map.154.refs_0_.refs_4_ = f32[8,128]{1,0:T(8,128)S(1)} custom-call(f32[3200,128]{1,0:T(8,128)S(1)} %get-tuple-element.71.slope_ref, bf16[896,128]{1,0:T(8,128)(2,1)S(1)} %collective-permute-done.4.low_ref, bf16[896,128]{1,0:T(8,128)(2,1)S(1)} %collective-permute-done.5.high_ref, f32[115,8,256]{2,1,0:T(8,128)S(1)} %get-tuple-element.46.wide_ref, ...), custom_call_target="tpu_custom_call" | custom-call | flops 1073741824 | bytes 1048576 | tf_op jit(solution)/shard_map/pallas_call | solution.py:873
  48.4 0.0 copy-start.11
  48.4 0.1 collective-permute-start.8
  48.5 1.7 %collective-permute-start.7 = (f32[8,128]{1,0:T(8,128)S(1)}, f32[8,128]{1,0:T(8,128)S(1)}, u32[]{:S(2)}, u32[]{:S(2)}) collective-permute-start(f32[8,128]{1,0:T(8,128)S(1)} %shard_map.154.refs_0_.refs_4_), channel_id=1, source_target_pairs={{2,0},{3,1},{0,2},{1,3},{6,4},{7,5},{4,6},{5,7},{10,8},{11,9},{8,1... | collective-permute-start | bytes 12296 | tf_op jit(solution)/shard_map/ppermute | solution.py:1035
  50.2 0.2 collective-permute-start.6
  50.3 1.2 %collective-permute-done.8.refs_3_ = f32[8,128]{1,0:T(8,128)S(1)} collective-permute-done((f32[8,128]{1,0:T(8,128)S(1)}, f32[8,128]{1,0:T(8,128)S(1)}, u32[]{:S(2)}, u32[]{:S(2)}) %collective-permute-start.8) | collective-permute-done | bytes 4128 | tf_op jit(solution)/shard_map/ppermute | solution.py:1035
  51.5 0.7 %collective-permute-done.7.refs_2_ = f32[8,128]{1,0:T(8,128)S(1)} collective-permute-done((f32[8,128]{1,0:T(8,128)S(1)}, f32[8,128]{1,0:T(8,128)S(1)}, u32[]{:S(2)}, u32[]{:S(2)}) %collective-permute-start.7) | collective-permute-done | bytes 4128 | tf_op jit(solution)/shard_map/ppermute | solution.py:1035
  52.1 0.0 collective-permute-done.6.refs_1_
  52.1 0.4 shard_map.155
  52.5 2.7 %collective-permute-start.11 = (f32[8,128]{1,0:T(8,128)S(1)}, f32[8,128]{1,0:T(8,128)S(1)}, u32[]{:S(2)}, u32[]{:S(2)}) collective-permute-start(f32[8,128]{1,0:T(8,128)S(1)} %get-tuple-element.78.refs_0_), channel_id=1, source_target_pairs={{12,0},{13,1},{14,2},{15,3},{8,4},{9,5},{10,6},{11,7},{4,8},{5,9},... | collective-permute-start | bytes 12296 | tf_op jit(solution)/shard_map/ppermute | solution.py:1035
  55.3 1.7 %collective-permute-start.9 = (f32[8,128]{1,0:T(8,128)S(1)}, f32[8,128]{1,0:T(8,128)S(1)}, u32[]{:S(2)}, u32[]{:S(2)}) collective-permute-start(f32[8,128]{1,0:T(8,128)S(1)} %get-tuple-element.78.refs_0_), channel_id=1, source_target_pairs={{4,0},{5,1},{6,2},{7,3},{0,4},{1,5},{2,6},{3,7},{12,8},{13,9},{14,... | collective-permute-start | bytes 12296 | tf_op jit(solution)/shard_map/ppermute | solution.py:1035
  57.0 1.0 %collective-permute-done.11.refs_3_ = f32[8,128]{1,0:T(8,128)S(1)} collective-permute-done((f32[8,128]{1,0:T(8,128)S(1)}, f32[8,128]{1,0:T(8,128)S(1)}, u32[]{:S(2)}, u32[]{:S(2)}) %collective-permute-start.11) | collective-permute-done | bytes 4128 | tf_op jit(solution)/shard_map/ppermute | solution.py:1035
  58.0 1.8 %collective-permute-done.10.refs_2_ = f32[8,128]{1,0:T(8,128)S(1)} collective-permute-done((f32[8,128]{1,0:T(8,128)S(1)}, f32[8,128]{1,0:T(8,128)S(1)}, u32[]{:S(2)}, u32[]{:S(2)}) %collective-permute-start.10) | collective-permute-done | bytes 4128 | tf_op jit(solution)/shard_map/ppermute | solution.py:1035
  59.8 1.1 %shard_map.156 = (f32[3,128]{1,0:T(4,128)}, f32[3,128]{1,0:T(4,128)}, f32[3]{0:T(128)}) custom-call(f32[8,128]{1,0:T(8,128)S(1)} %get-tuple-element.78.refs_0_, f32[8,128]{1,0:T(8,128)S(1)} %collective-permute-done.9.refs_1_, f32[8,128]{1,0:T(8,128)S(1)} %collective-permute-done.10.refs_2_, f32[8,128]{1,0:T(8,128)S(1)} %collective-permute-done.11.refs_3_, ...), custom_call_target="tpu_custom_call" | custom-call | flops 1073741824 | bytes 1048576 | tf_op jit(solution)/shard_map/pallas_call | solution.py:873
  (31 shorter events, 0.1 us)
Async XLA Ops:
  0.6 1.1 %copy-start.2 = (bf16[3200,128]{1,0:T(8,128)(2,1)S(1)}, bf16[3200,128]{1,0:T(8,128)(2,1)}, u32[]{:S(2)}) copy-start(bf16[3200,128]{1,0:T(8,128)(2,1)} %feat_hbm.3) | copy-start | bytes 2457604
  1.8 0.7 %copy-start.9 = (f32[3,128]{1,0:T(4,128)S(1)}, f32[3,128]{1,0:T(4,128)}, u32[]{:S(2)}) copy-start(f32[3,128]{1,0:T(4,128)} %refs_8_.1) | copy-start | bytes 4612
  2.5 7.0 %copy-start.3 = (bf16[3200,128]{1,0:T(8,128)(2,1)S(1)}, bf16[3200,128]{1,0:T(8,128)(2,1)}, u32[]{:S(2)}) copy-start(bf16[3200,128]{1,0:T(8,128)(2,1)} %feat_hbm.3) | copy-start | bytes 2457604
  2.5 7.0 %copy-start.4 = (bf16[2,5,128,128]{3,2,1,0:T(8,128)(2,1)S(1)}, bf16[2,5,128,128]{3,2,1,0:T(8,128)(2,1)}, u32[]{:S(2)}) copy-start(bf16[2,5,128,128]{3,2,1,0:T(8,128)(2,1)} %weight_hbm.1) | copy-start | bytes 983044
  2.5 7.0 %copy-start.5 = (bf16[115,512]{1,0:T(8,128)(2,1)S(1)}, bf16[115,512]{1,0:T(8,128)(2,1)}, u32[]{:S(2)}) copy-start(bf16[115,512]{1,0:T(8,128)(2,1)} %frames_hbm.1) | copy-start | bytes 353284
  2.5 7.0 %copy-start.6 = (f32[2,16,128]{2,1,0:T(8,128)S(1)}, f32[2,16,128]{2,1,0:T(8,128)}, u32[]{:S(2)}) copy-start(f32[2,16,128]{2,1,0:T(8,128)} %radial_hbm.1) | copy-start | bytes 49156
  2.5 7.0 %copy-start.7 = (f32[5,128]{1,0:T(8,128)S(1)}, f32[5,128]{1,0:T(8,128)}, u32[]{:S(2)}) copy-start(f32[5,128]{1,0:T(8,128)} %readout_hbm.1) | copy-start | bytes 7684
  2.5 7.0 %copy-start.8 = (s32[4,128]{1,0:T(4,128)S(1)}, s32[4,128]{1,0:T(4,128)}, u32[]{:S(2)}) copy-start(s32[4,128]{1,0:T(4,128)} %nb_hbm.1) | copy-start | bytes 6148
  2.5 7.0 %copy-start.10 = (f32[3,128]{1,0:T(4,128)S(1)}, f32[3,128]{1,0:T(4,128)}, u32[]{:S(2)}) copy-start(f32[3,128]{1,0:T(4,128)} %refs_8_.1) | copy-start | bytes 4612
  2.5 7.0 %copy-start.12 = (s32[128]{0:T(128)S(1)}, s32[128]{0:T(128)}, u32[]{:S(2)}) copy-start(s32[128]{0:T(128)} %param.16) | copy-start | bytes 1540
  2.5 7.0 %copy-start.13 = (f32[3]{0:T(128)S(1)}, f32[3]{0:T(128)}, u32[]{:S(2)}) copy-start(f32[3]{0:T(128)} %box_hbm.1) | copy-start | bytes 40
  2.5 7.0 %copy-start.14 = (f32[3]{0:T(128)S(1)}, f32[3]{0:T(128)}, u32[]{:S(2)}) copy-start(f32[3]{0:T(128)} %control_hbm.1) | copy-start | bytes 40
  3.3 11.9 %collective-permute-start = (bf16[896,128]{1,0:T(8,128)(2,1)S(1)}, bf16[896,128]{1,0:T(8,128)(2,1)S(1)}, u32[]{:S(2)}, u32[]{:S(2)}) collective-permute-start(bf16[896,128]{1,0:T(8,128)(2,1)S(1)} %get-tuple-element.43), channel_id=1, source_target_pairs={{0,1},{1,0},{2,3},{3,2},{4,5},{5,4},{6,7},{7,6},{8,9},{9,8},{10,11... | collective-permute-start | bytes 688136 | tf_op jit(solution)/shard_map/ppermute | solution.py:912
  3.8 11.4 %collective-permute-start.1 = (bf16[896,128]{1,0:T(8,128)(2,1)S(1)}, bf16[896,128]{1,0:T(8,128)(2,1)S(1)}, u32[]{:S(2)}, u32[]{:S(2)}) collective-permute-start(bf16[896,128]{1,0:T(8,128)(2,1)S(1)} %get-tuple-element.44), channel_id=1, source_target_pairs={{0,15},{1,2},{2,1},{3,4},{4,3},{5,6},{6,5},{7,8},{8,7},{9,10},{10,... | collective-permute-start | bytes 688136 | tf_op jit(solution)/shard_map/ppermute | solution.py:911
  20.2 8.2 %collective-permute-start.2 = (bf16[896,128]{1,0:T(8,128)(2,1)S(1)}, bf16[896,128]{1,0:T(8,128)(2,1)S(1)}, u32[]{:S(2)}, u32[]{:S(2)}) collective-permute-start(bf16[896,128]{1,0:T(8,128)(2,1)S(1)} %get-tuple-element.62), channel_id=1, source_target_pairs={{0,1},{1,0},{2,3},{3,2},{4,5},{5,4},{6,7},{7,6},{8,9},{9,8},{10,11... | collective-permute-start | bytes 688136 | tf_op jit(solution)/shard_map/ppermute | solution.py:912
  20.2 8.3 %collective-permute-start.3 = (bf16[896,128]{1,0:T(8,128)(2,1)S(1)}, bf16[896,128]{1,0:T(8,128)(2,1)S(1)}, u32[]{:S(2)}, u32[]{:S(2)}) collective-permute-start(bf16[896,128]{1,0:T(8,128)(2,1)S(1)} %get-tuple-element.63), channel_id=1, source_target_pairs={{0,15},{1,2},{2,1},{3,4},{4,3},{5,6},{6,5},{7,8},{8,7},{9,10},{10,... | collective-permute-start | bytes 688136 | tf_op jit(solution)/shard_map/ppermute | solution.py:911
  37.4 7.1 %collective-permute-start.4 = (bf16[896,128]{1,0:T(8,128)(2,1)S(1)}, bf16[896,128]{1,0:T(8,128)(2,1)S(1)}, u32[]{:S(2)}, u32[]{:S(2)}) collective-permute-start(bf16[896,128]{1,0:T(8,128)(2,1)S(1)} %get-tuple-element.72), channel_id=1, source_target_pairs={{0,1},{1,0},{2,3},{3,2},{4,5},{5,4},{6,7},{7,6},{8,9},{9,8},{10,11... | collective-permute-start | bytes 688136 | tf_op jit(solution)/shard_map/ppermute | solution.py:912
  37.5 8.3 %collective-permute-start.5 = (bf16[896,128]{1,0:T(8,128)(2,1)S(1)}, bf16[896,128]{1,0:T(8,128)(2,1)S(1)}, u32[]{:S(2)}, u32[]{:S(2)}) collective-permute-start(bf16[896,128]{1,0:T(8,128)(2,1)S(1)} %get-tuple-element.73), channel_id=1, source_target_pairs={{0,15},{1,2},{2,1},{3,4},{4,3},{5,6},{6,5},{7,8},{8,7},{9,10},{10,... | collective-permute-start | bytes 688136 | tf_op jit(solution)/shard_map/ppermute | solution.py:911
  39.8 6.0 %copy-start = (f32[3,128]{1,0:T(4,128)S(1)}, f32[3,128]{1,0:T(4,128)}, u32[]{:S(2)}) copy-start(f32[3,128]{1,0:T(4,128)} %velocities_ref.1) | copy-start | bytes 4612
  39.8 6.0 %copy-start.1 = (f32[128]{0:T(128)S(1)}, f32[128]{0:T(128)}, u32[]{:S(2)}) copy-start(f32[128]{0:T(128)} %param.19) | copy-start | bytes 1540
  48.4 11.4 %copy-start.11 = (f32[3,128]{1,0:T(4,128)S(1)}, f32[3,128]{1,0:T(4,128)}, u32[]{:S(2)}) copy-start(f32[3,128]{1,0:T(4,128)} %refs_7_.1) | copy-start | bytes 4612
  48.4 3.1 %collective-permute-start.8 = (f32[8,128]{1,0:T(8,128)S(1)}, f32[8,128]{1,0:T(8,128)S(1)}, u32[]{:S(2)}, u32[]{:S(2)}) collective-permute-start(f32[8,128]{1,0:T(8,128)S(1)} %shard_map.154.refs_0_.refs_4_), channel_id=1, source_target_pairs={{3,0},{2,1},{1,2},{0,3},{7,4},{6,5},{5,6},{4,7},{11,8},{10,9},{9,1... | collective-permute-start | bytes 12296 | tf_op jit(solution)/shard_map/ppermute | solution.py:1035
  48.5 3.7 %collective-permute-start.7 = (f32[8,128]{1,0:T(8,128)S(1)}, f32[8,128]{1,0:T(8,128)S(1)}, u32[]{:S(2)}, u32[]{:S(2)}) collective-permute-start(f32[8,128]{1,0:T(8,128)S(1)} %shard_map.154.refs_0_.refs_4_), channel_id=1, source_target_pairs={{2,0},{3,1},{0,2},{1,3},{6,4},{7,5},{4,6},{5,7},{10,8},{11,9},{8,1... | collective-permute-start | bytes 12296 | tf_op jit(solution)/shard_map/ppermute | solution.py:1035
  50.2 2.0 %collective-permute-start.6 = (f32[8,128]{1,0:T(8,128)S(1)}, f32[8,128]{1,0:T(8,128)S(1)}, u32[]{:S(2)}, u32[]{:S(2)}) collective-permute-start(f32[8,128]{1,0:T(8,128)S(1)} %shard_map.154.refs_0_.refs_4_), channel_id=1, source_target_pairs={{1,0},{0,1},{3,2},{2,3},{5,4},{4,5},{7,6},{6,7},{9,8},{8,9},{11,10... | collective-permute-start | bytes 12296 | tf_op jit(solution)/shard_map/ppermute | solution.py:1035
  52.5 5.5 %collective-permute-start.11 = (f32[8,128]{1,0:T(8,128)S(1)}, f32[8,128]{1,0:T(8,128)S(1)}, u32[]{:S(2)}, u32[]{:S(2)}) collective-permute-start(f32[8,128]{1,0:T(8,128)S(1)} %get-tuple-element.78.refs_0_), channel_id=1, source_target_pairs={{12,0},{13,1},{14,2},{15,3},{8,4},{9,5},{10,6},{11,7},{4,8},{5,9},... | collective-permute-start | bytes 12296 | tf_op jit(solution)/shard_map/ppermute | solution.py:1035
  55.3 4.5 %collective-permute-start.10 = (f32[8,128]{1,0:T(8,128)S(1)}, f32[8,128]{1,0:T(8,128)S(1)}, u32[]{:S(2)}, u32[]{:S(2)}) collective-permute-start(f32[8,128]{1,0:T(8,128)S(1)} %get-tuple-element.78.refs_0_), channel_id=1, source_target_pairs={{8,0},{9,1},{10,2},{11,3},{12,4},{13,5},{14,6},{15,7},{0,8},{1,9},... | collective-permute-start | bytes 12296 | tf_op jit(solution)/shard_map/ppermute | solution.py:1035
  55.3 4.5 %collective-permute-start.9 = (f32[8,128]{1,0:T(8,128)S(1)}, f32[8,128]{1,0:T(8,128)S(1)}, u32[]{:S(2)}, u32[]{:S(2)}) collective-permute-start(f32[8,128]{1,0:T(8,128)S(1)} %get-tuple-element.78.refs_0_), channel_id=1, source_target_pairs={{4,0},{5,1},{6,2},{7,3},{0,4},{1,5},{2,6},{3,7},{12,8},{13,9},{14,... | collective-permute-start | bytes 12296 | tf_op jit(solution)/shard_map/ppermute | solution.py:1035
